TPU v7x, 32 devices: a whole 2x2x4 slice. The times are simulated.
32 devices in a mesh: section: 2 (over core), ctx: 4 (over z), fsdp: 4 (over y, x).
Axes of the slice: x: 2, y: 2, z: 4, core: 2. Of those that a mesh axis runs over, the one named last changes fastest.
Arguments:
- inputs: bfloat16 [2, 4, 1024, 768], P(None, 'fsdp', 'ctx'), may hold values from -6 to 6
- cotangent: bfloat16 [2, 4, 1024, 768], P(None, 'fsdp', 'ctx'), may hold values from -6 to 6
- block_order: int32 [4], replicated, may hold values from 0 to 3, as said below
- norm_gain: float32 [2, 2, 768], P('section', None, 'fsdp'), may hold values from 0.5 to 1.5
- norm_bias: float32 [2, 2, 768], P('section', None, 'fsdp'), may hold values from -2 to 2
- qkv_weight: bfloat16 [2, 768, 2304], P('section', 'fsdp'), may hold values from -0.21875 to 0.21875
- biases: float32 [2, 6912], P('section', 'fsdp'), may hold values from -2 to 2
- out_weight: bfloat16 [2, 768, 768], P('section', 'fsdp'), may hold values from -0.875 to 0.875
- up_weight: bfloat16 [2, 768, 3072], P('section', 'fsdp'), may hold values from -0.21875 to 0.21875
- down_weight: bfloat16 [2, 3072, 768], P('section', 'fsdp'), may hold values from -0.109375 to 0.109375
Outputs:
- layer_out: bfloat16 [2, 2, 4, 1024, 768], P('section', None, 'fsdp', 'ctx')
- input_grads: bfloat16 [2, 2, 4, 1024, 768], P('section', None, 'fsdp', 'ctx')
- gain_grads: float32 [2, 2, 768], P('section', None, ('ctx', 'fsdp'))
- shift_grads: float32 [2, 2, 768], P('section', None, ('ctx', 'fsdp'))
- qkv_grads: float32 [2, 768, 2304], P('section', ('ctx', 'fsdp'))
- bias_grads: float32 [2, 6912], P('section', ('ctx', 'fsdp'))
- out_grads: float32 [2, 768, 768], P('section', ('ctx', 'fsdp'))
- up_grads: float32 [2, 768, 3072], P('section', ('ctx', 'fsdp'))
- down_grads: float32 [2, 3072, 768], P('section', ('ctx', 'fsdp'))
Inputs may be any that keep to these rules, and one draw needn't show every extreme that they name: block_order is a permutation of 0 to 3.
All inputs are finite; a program needn't handle non-finite values.
Results may differ from a plain program's by a relative error of at most 0.028.
Values may be sent and summed in bfloat16 or wider, within the bound.
No kernel may reach another device: no remote copies, remote signals or barrier semaphores. Data moves between devices by JAX's collectives and lax.ppermute only.
A program may use at most 256 MiB of HBM per device.

v0:
```python
import jax
import jax.numpy as jnp
from jax import lax
from jax.sharding import PartitionSpec as P

D = 768
HEADS = 12
HEAD_DIM = 64
ROT = 16
FF = 3072


def passed_along(block, axis, distance):
    devices = range(lax.axis_size(axis))
    route = [(i - distance, i) for i in devices if i - distance in devices]
    return lax.ppermute(block, axis, route)


def norm_apply(tok_rows, gain_vec, shift_vec):
    row_mean = jnp.mean(tok_rows, -1, keepdims=True)
    centred = tok_rows - row_mean
    spread = jnp.mean(centred * centred, -1, keepdims=True)
    return centred * lax.rsqrt(spread + 1e-05) * gain_vec + shift_vec


def angle_tables(places):
    half_dims = ROT // 2
    frequency = 10000.0 ** (-(jnp.arange(half_dims, dtype=jnp.float32) * 2.0) / ROT)
    phases = places.astype(jnp.float32)[:, None] * frequency[None, :]
    phases = jnp.concatenate([phases, phases], -1)
    return (jnp.cos(phases)[:, None, :], jnp.sin(phases)[:, None, :])


def rotary(head_rows, cosine, sine):
    half_dims = ROT // 2
    rot_part = head_rows[..., :ROT]
    swapped = jnp.concatenate([-rot_part[..., half_dims:], rot_part[..., :half_dims]], -1)
    return jnp.concatenate([rot_part * cosine + swapped * sine, head_rows[..., ROT:]], -1)


def token_places(block_order, block_rows):
    rank_count = block_order.shape[0]
    row_ids = jnp.arange(rank_count * 2 * block_rows, dtype=jnp.int32)
    owner_ids = row_ids // (2 * block_rows)
    within = row_ids % (2 * block_rows)
    first_block = block_order[owner_ids]
    block_ids = jnp.where(within < block_rows, first_block, 2 * rank_count - 1 - first_block)
    return block_ids * block_rows + within % block_rows


def gelu_exact(up_rows):
    return jax.nn.gelu(up_rows, approximate=False)


def per_device(
    inputs,
    cotangent,
    block_order,
    norm_gain,
    norm_bias,
    qkv_weight,
    biases,
    out_weight,
    up_weight,
    down_weight,
):
    micro_count = inputs.shape[0]
    rows_dev = inputs.shape[2]
    seq_len = block_order.shape[0] * rows_dev
    section_idx = lax.axis_index("section")
    ctx_idx = lax.axis_index("ctx")
    places = token_places(block_order, rows_dev // 2)
    own_places = lax.dynamic_slice_in_dim(places, ctx_idx * rows_dev, rows_dev)
    cosine, sine = angle_tables(own_places)
    allowed = (own_places[:, None] >= places[None, :])[None]
    shards = (
        norm_gain[0],
        norm_bias[0],
        qkv_weight[0],
        biases[0],
        out_weight[0],
        up_weight[0],
        down_weight[0],
    )
    held_weights = (
        lax.all_gather(shards[0].astype(jnp.bfloat16), "fsdp", axis=1, tiled=True).astype(
            jnp.float32
        ),
        lax.all_gather(shards[1].astype(jnp.bfloat16), "fsdp", axis=1, tiled=True).astype(
            jnp.float32
        ),
        lax.all_gather(shards[2], "fsdp", axis=0, tiled=True),
        lax.all_gather(shards[3].astype(jnp.bfloat16), "fsdp", axis=0, tiled=True).astype(
            jnp.float32
        ),
        lax.all_gather(shards[4], "fsdp", axis=0, tiled=True),
        lax.all_gather(shards[5], "fsdp", axis=0, tiled=True),
        lax.all_gather(shards[6], "fsdp", axis=0, tiled=True),
    )

    def fetch_weights():
        return held_weights

    passed = jnp.zeros((rows_dev, D), jnp.bfloat16)
    outs_step = []
    kept_step = []
    for moment in range(micro_count + 1):
        params = fetch_weights()
        fresh_rows = inputs[min(moment, micro_count - 1), 0]
        tok_rows = jnp.where(section_idx == 0, fresh_rows, passed).astype(jnp.float32)
        (
            layer_gain_pair,
            layer_shift_pair,
            layer_qkv_mat,
            layer_bias_vec,
            layer_out_mat,
            layer_up_mat,
            layer_down_mat,
        ) = params
        layer_attn_in = norm_apply(tok_rows, layer_gain_pair[0], layer_shift_pair[0]).astype(
            jnp.bfloat16
        )
        layer_mlp_in = norm_apply(tok_rows, layer_gain_pair[1], layer_shift_pair[1]).astype(
            jnp.bfloat16
        )
        qkv_rows = (
            jnp.dot(layer_attn_in, layer_qkv_mat, preferred_element_type=jnp.float32)
            + layer_bias_vec[: 3 * D]
        )
        qkv_rows = qkv_rows.reshape(rows_dev, 3, HEADS, HEAD_DIM)
        layer_query_rows = rotary(qkv_rows[:, 0], cosine, sine).astype(jnp.bfloat16)
        key_rows = rotary(qkv_rows[:, 1], cosine, sine).astype(jnp.bfloat16).reshape(rows_dev, D)
        value_rows = qkv_rows[:, 2].astype(jnp.bfloat16).reshape(rows_dev, D)
        key_all = lax.all_gather(key_rows, "ctx", axis=0, tiled=True)
        value_all = lax.all_gather(value_rows, "ctx", axis=0, tiled=True)
        layer_key_heads = key_all.reshape(seq_len, HEADS, HEAD_DIM)
        layer_value_heads = value_all.reshape(seq_len, HEADS, HEAD_DIM)
        layer_scores = (
            jnp.einsum(
                "qhd,khd->hqk",
                layer_query_rows,
                layer_key_heads,
                preferred_element_type=jnp.float32,
            )
            * 0.125
        )
        layer_scores = jnp.where(allowed, layer_scores, -1e30)
        layer_row_max = jnp.max(layer_scores, -1, keepdims=True)
        exp_scores = jnp.exp(layer_scores - layer_row_max)
        layer_row_sum = jnp.sum(exp_scores, -1, keepdims=True)
        prob_rows = (exp_scores / layer_row_sum).astype(jnp.bfloat16)
        layer_mixed_rows = jnp.einsum(
            "hqk,khd->qhd", prob_rows, layer_value_heads, preferred_element_type=jnp.float32
        )
        layer_mixed_rows = layer_mixed_rows.reshape(rows_dev, D).astype(jnp.bfloat16)
        attn_rows = (
            jnp.dot(layer_mixed_rows, layer_out_mat, preferred_element_type=jnp.float32)
            + layer_bias_vec[3 * D : 4 * D]
        )
        layer_up_rows = (
            jnp.dot(layer_mlp_in, layer_up_mat, preferred_element_type=jnp.float32)
            + layer_bias_vec[4 * D : 4 * D + FF]
        )
        layer_gelu_rows = gelu_exact(layer_up_rows).astype(jnp.bfloat16)
        mlp_rows = (
            jnp.dot(layer_gelu_rows, layer_down_mat, preferred_element_type=jnp.float32)
            + layer_bias_vec[4 * D + FF :]
        )
        out_rows = tok_rows + (attn_rows + mlp_rows)
        layer_kept_vals = (
            tok_rows,
            layer_attn_in,
            layer_mlp_in,
            layer_query_rows,
            layer_key_heads,
            layer_value_heads,
            layer_row_max,
            layer_row_sum,
            layer_mixed_rows,
            layer_up_rows,
            layer_gelu_rows,
        )
        out_rows, kept_vals = (out_rows, layer_kept_vals)
        sent_rows = out_rows.astype(jnp.bfloat16)
        if moment < micro_count:
            passed = passed_along(sent_rows, "section", 1)
        outs_step.append(sent_rows)
        kept_step.append(kept_vals)
    returned = jnp.zeros((rows_dev, D), jnp.bfloat16)
    grads_step = []
    totals = None
    for moment in range(micro_count + 1):
        params = fetch_weights()
        late_vals = kept_step[min(moment + 1, micro_count)]
        early_vals = kept_step[max(moment - 1, 0)]
        kept_vals = jax.tree.map(
            lambda late_one, early_one: jnp.where(section_idx == 1, late_one, early_one),
            late_vals,
            early_vals,
        )
        valid_flag = jnp.where(section_idx == 1, moment < micro_count, moment >= 1).astype(
            jnp.float32
        )
        top_grad = cotangent[min(moment, micro_count - 1), 0]
        grad_rows = jnp.where(section_idx == 1, top_grad, returned).astype(jnp.float32) * valid_flag
        gain_pair, shift_pair, qkv_mat, bias_vec, out_mat, up_mat, down_mat = params
        (
            layer_tok_rows,
            attn_in,
            mlp_in,
            query_rows,
            key_heads,
            value_heads,
            row_max,
            row_sum,
            mixed_rows,
            up_rows,
            gelu_rows,
        ) = kept_vals
        grad_low = grad_rows.astype(jnp.bfloat16)
        down_term = jnp.einsum("rf,rd->fd", gelu_rows, grad_low, preferred_element_type=jnp.float32)
        out_term = jnp.einsum("rc,rd->cd", mixed_rows, grad_low, preferred_element_type=jnp.float32)
        gelu_grad = jnp.einsum("rd,fd->rf", grad_low, down_mat, preferred_element_type=jnp.float32)
        gelu_pull = jax.vjp(gelu_exact, up_rows)[1]
        up_grad = gelu_pull(gelu_grad)[0].astype(jnp.bfloat16)
        up_term = jnp.einsum("rd,rf->df", mlp_in, up_grad, preferred_element_type=jnp.float32)
        mlp_back = jnp.einsum("rf,df->rd", up_grad, up_mat, preferred_element_type=jnp.float32)
        mixed_grad = jnp.einsum("rd,cd->rc", grad_low, out_mat, preferred_element_type=jnp.float32)
        mixed_grad = mixed_grad.astype(jnp.bfloat16).reshape(rows_dev, HEADS, HEAD_DIM)
        scores = (
            jnp.einsum("qhd,khd->hqk", query_rows, key_heads, preferred_element_type=jnp.float32)
            * 0.125
        )
        scores = jnp.where(allowed, scores, -1e30)
        prob_full = jnp.exp(scores - row_max) / row_sum
        prob_grad = jnp.einsum(
            "qhd,khd->hqk", mixed_grad, value_heads, preferred_element_type=jnp.float32
        )
        centre = jnp.sum(prob_full * prob_grad, -1, keepdims=True)
        score_grad = (prob_full * (prob_grad - centre)).astype(jnp.bfloat16)
        query_grad = (
            jnp.einsum("hqk,khd->qhd", score_grad, key_heads, preferred_element_type=jnp.float32)
            * 0.125
        )
        key_grad = (
            jnp.einsum("hqk,qhd->khd", score_grad, query_rows, preferred_element_type=jnp.float32)
            * 0.125
        )
        value_grad = jnp.einsum(
            "hqk,qhd->khd",
            prob_full.astype(jnp.bfloat16),
            mixed_grad,
            preferred_element_type=jnp.float32,
        )
        key_grad, value_grad = (
            lax.psum_scatter(
                key_grad.reshape(seq_len, D).astype(jnp.bfloat16),
                "ctx",
                scatter_dimension=0,
                tiled=True,
            ).astype(jnp.float32),
            lax.psum_scatter(
                value_grad.reshape(seq_len, D).astype(jnp.bfloat16),
                "ctx",
                scatter_dimension=0,
                tiled=True,
            ).astype(jnp.float32),
        )
        query_back = rotary(query_grad, cosine, -sine).reshape(rows_dev, D)
        key_back = rotary(key_grad.reshape(rows_dev, HEADS, HEAD_DIM), cosine, -sine).reshape(
            rows_dev, D
        )
        qkv_grad = jnp.concatenate([query_back, key_back, value_grad], -1).astype(jnp.bfloat16)
        qkv_term = jnp.einsum("rd,rc->dc", attn_in, qkv_grad, preferred_element_type=jnp.float32)
        attn_back = jnp.einsum("rc,dc->rd", qkv_grad, qkv_mat, preferred_element_type=jnp.float32)
        attn_pull = jax.vjp(norm_apply, layer_tok_rows, gain_pair[0], shift_pair[0])[1]
        mlp_pull = jax.vjp(norm_apply, layer_tok_rows, gain_pair[1], shift_pair[1])[1]
        attn_x, attn_gain, attn_shift = attn_pull(attn_back)
        mlp_x, mlp_gain, mlp_shift = mlp_pull(mlp_back)
        grad_total = jnp.sum(grad_low.astype(jnp.float32), 0)
        bias_term = jnp.concatenate(
            [
                jnp.sum(qkv_grad.astype(jnp.float32), 0),
                grad_total,
                jnp.sum(up_grad.astype(jnp.float32), 0),
                grad_total,
            ]
        )
        terms = (
            jnp.stack([attn_gain, mlp_gain]),
            jnp.stack([attn_shift, mlp_shift]),
            qkv_term,
            bias_term,
            out_term,
            up_term,
            down_term,
        )
        back_rows, terms = (grad_rows + attn_x + mlp_x, terms)
        sent_rows = back_rows.astype(jnp.bfloat16)
        if moment < micro_count:
            returned = passed_along(sent_rows, "section", -1)
        grads_step.append(sent_rows)
        shares = (
            lax.psum_scatter(terms[0], ("ctx", "fsdp"), scatter_dimension=1, tiled=True),
            lax.psum_scatter(terms[1], ("ctx", "fsdp"), scatter_dimension=1, tiled=True),
            lax.psum_scatter(terms[2], ("ctx", "fsdp"), scatter_dimension=0, tiled=True),
            lax.psum_scatter(terms[3], ("ctx", "fsdp"), scatter_dimension=0, tiled=True),
            lax.psum_scatter(terms[4], ("ctx", "fsdp"), scatter_dimension=0, tiled=True),
            lax.psum_scatter(terms[5], ("ctx", "fsdp"), scatter_dimension=0, tiled=True),
            lax.psum_scatter(terms[6], ("ctx", "fsdp"), scatter_dimension=0, tiled=True),
        )
        if moment == 0:
            totals = shares
        else:
            totals = jax.tree.map(jnp.add, totals, shares)
    layer_out = jnp.stack(
        [
            jnp.where(section_idx == 0, outs_step[mb_index], outs_step[mb_index + 1])
            for mb_index in range(micro_count)
        ]
    )
    input_grads = jnp.stack(
        [
            jnp.where(section_idx == 1, grads_step[mb_index], grads_step[mb_index + 1])
            for mb_index in range(micro_count)
        ]
    )
    return (
        layer_out[None, :, None],
        input_grads[None, :, None],
        totals[0][None],
        totals[1][None],
        totals[2][None],
        totals[3][None],
        totals[4][None],
        totals[5][None],
        totals[6][None],
    )


def solution(mesh):
    in_specs = (
        P(None, "fsdp", "ctx", None),
        P(None, "fsdp", "ctx", None),
        P(),
        P("section", None, "fsdp"),
        P("section", None, "fsdp"),
        P("section", "fsdp", None),
        P("section", "fsdp"),
        P("section", "fsdp", None),
        P("section", "fsdp", None),
        P("section", "fsdp", None),
    )
    out_specs = (
        P("section", None, "fsdp", "ctx", None),
        P("section", None, "fsdp", "ctx", None),
        P("section", None, ("ctx", "fsdp")),
        P("section", None, ("ctx", "fsdp")),
        P("section", ("ctx", "fsdp"), None),
        P("section", ("ctx", "fsdp")),
        P("section", ("ctx", "fsdp"), None),
        P("section", ("ctx", "fsdp"), None),
        P("section", ("ctx", "fsdp"), None),
    )
    return jax.shard_map(
        per_device, mesh=mesh, in_specs=in_specs, out_specs=out_specs, check_vma=False
    )
```

profile of v0, /device:TPU:0, one launch (start us, length us, event | category | flops | bytes accessed | tf_op | source)
XLA Modules:
  0.0 1698.1 jit_solution(2459522952384695152)
XLA Ops:
  11.1 17.7 %all-reduce = bf16[6912]{0:T(1024)(128)(2,1)S(1)} all-reduce(bf16[6912]{0:T(1024)(128)(2,1)S(1)} %dynamic-update-slice), channel_id=5, replica_groups=mesh['section'=2,'ctx'=4,'fsdp'=4] {'fsdp'}, use_global_device_ids=true, to_apply=%add | all-reduce | flops 6912 | bytes 27648
  29.0 9.9 all-gather.1
  39.5 12.2 all-gather
  80.0 43.1 %all-gather.34.cloned.1.call-done = bf16[1,768,3072]{2,1,0:T(8,128)(2,1)} async-done(((bf16[1,192,3072]{2,1,0:T(8,128)(2,1)}), bf16[1,768,3072]{2,1,0:T(8,128)(2,1)}) %all-gather.34.cloned.1.call-update) | async-done | bytes 4718608 | tf_op jit(solution)/shard_map/all_gather | solution.py:97
  123.1 10.8 fusion.59
  133.9 48.1 %all-gather.36.cloned.1.call-done = bf16[1,3072,768]{2,1,0:T(8,128)(2,1)} async-done(((bf16[1,768,768]{2,1,0:T(8,128)(2,1)}), bf16[1,3072,768]{2,1,0:T(8,128)(2,1)}) %all-gather.36.cloned.1.call-update) | async-done | bytes 4718608 | tf_op jit(solution)/shard_map/all_gather | solution.py:98
  186.7 35.1 %all-gather.20.cloned.1.call-done = bf16[1024,768]{0,1:T(8,128)(2,1)} async-done(((bf16[256,768]{0,1:T(8,128)(2,1)}), bf16[1024,768]{0,1:T(8,128)(2,1)}) %all-gather.20.cloned.1.call-update) | async-done | bytes 1572880 | tf_op jit(solution)/shard_map/all_gather | solution.py:134
  233.7 26.0 %all-gather.18.cloned.1.call-done = bf16[1024,768]{0,1:T(8,128)(2,1)} async-done(((bf16[256,768]{0,1:T(8,128)(2,1)}), bf16[1024,768]{0,1:T(8,128)(2,1)}) %all-gather.18.cloned.1.call-update) | async-done | bytes 1572880 | tf_op jit(solution)/shard_map/all_gather | solution.py:135
  259.7 7.0 fusion.170
  266.8 20.6 %all-gather.32.cloned.1.call-done = bf16[1,768,768]{2,1,0:T(8,128)(2,1)} async-done(((bf16[1,192,768]{2,1,0:T(8,128)(2,1)}), bf16[1,768,768]{2,1,0:T(8,128)(2,1)}) %all-gather.32.cloned.1.call-update) | async-done | bytes 1179664 | tf_op jit(solution)/shard_map/all_gather | solution.py:96
  289.3 11.9 collective-permute-start
  317.3 11.2 fusion.62
  329.6 21.0 %all-gather.24.cloned.1.call-done = bf16[1024,768]{0,1:T(8,128)(2,1)} async-done(((bf16[256,768]{0,1:T(8,128)(2,1)}), bf16[1024,768]{0,1:T(8,128)(2,1)}) %all-gather.24.cloned.1.call-update) | async-done | bytes 1572880 | tf_op jit(solution)/shard_map/all_gather | solution.py:134
  359.7 29.0 %all-gather.22.cloned.1.call-done = bf16[1024,768]{0,1:T(8,128)(2,1)} async-done(((bf16[256,768]{0,1:T(8,128)(2,1)}), bf16[1024,768]{0,1:T(8,128)(2,1)}) %all-gather.22.cloned.1.call-update) | async-done | bytes 1572880 | tf_op jit(solution)/shard_map/all_gather | solution.py:135
  388.8 8.1 fusion.141
  396.9 8.2 multiply_reduce_fusion.2
  405.1 9.9 multiply_convert_fusion.2
  418.2 11.3 convert_reduce_fusion.2
  429.5 5.3 fusion.31
  434.9 5.3 fusion.159
  442.6 7.8 broadcast_select_fusion.9
  453.0 4.9 fusion.149
  463.8 24.5 %reduce-scatter.19.cloned.1.call-done = bf16[256,768]{0,1:T(8,128)(2,1)} async-done(((bf16[1024,768]{0,1:T(8,128)(2,1)}), bf16[256,768]{0,1:T(8,128)(2,1)}) %reduce-scatter.19.cloned.1.call-update) | async-done | bytes 393232 | tf_op jit(solution)/shard_map/reduce_scatter | solution.py:262
  488.3 5.1 multiply_reduce_fusion.16
  519.2 20.7 %all-gather.28.cloned.1.call-done = bf16[1024,768]{0,1:T(8,128)(2,1)} async-done(((bf16[256,768]{0,1:T(8,128)(2,1)}), bf16[1024,768]{0,1:T(8,128)(2,1)}) %all-gather.28.cloned.1.call-update) | async-done | bytes 1572880 | tf_op jit(solution)/shard_map/all_gather | solution.py:134
  549.0 28.9 %all-gather.26.cloned.1.call-done = bf16[1024,768]{0,1:T(8,128)(2,1)} async-done(((bf16[256,768]{0,1:T(8,128)(2,1)}), bf16[1024,768]{0,1:T(8,128)(2,1)}) %all-gather.26.cloned.1.call-update) | async-done | bytes 1572880 | tf_op jit(solution)/shard_map/all_gather | solution.py:135
  578.0 8.1 fusion.139
  586.1 8.3 multiply_reduce_fusion.1
  594.3 9.7 multiply_convert_fusion.1
  611.6 5.7 fusion.45
  621.4 18.7 %convert_reduce_fusion.1 = (f32[3072]{0:T(1024)}, bf16[256,3072]{1,0:T(8,128)(2,1)S(1)}, bf16[256,3072]{1,0:T(8,128)(2,1)}) fusion(f32[256,3072]{1,0:T(8,128)} %fusion.45, f32[256,3072]{1,0:T(8,128)} %get-tuple-element.171, pred[]{:T(512)S(6)} %eq.8, bf16[256,768]{1,0:T(8,128)(2,1)S(1)} %get-tuple-element.103, ...), kind=kOutput, calls=%fused_computation.106 | convolution fusion | flops 1318056960 | bytes 14561281 | tf_op jit(solution)/shard_map/rd,fd->rf/dot_general | solution.py:223
  646.1 5.1 fusion.150
  657.1 20.1 %reduce-scatter.23.cloned.1.call-done = bf16[256,768]{0,1:T(8,128)(2,1)} async-done(((bf16[1024,768]{0,1:T(8,128)(2,1)}), bf16[256,768]{0,1:T(8,128)(2,1)}) %reduce-scatter.23.cloned.1.call-update) | async-done | bytes 393232 | tf_op jit(solution)/shard_map/reduce_scatter | solution.py:262
  694.4 8.1 fusion.137
  702.5 8.3 multiply_reduce_fusion
  710.8 9.7 multiply_convert_fusion
  723.6 7.6 fusion.168
  739.6 4.9 fusion.151
  748.0 11.1 convert_reduce_fusion
  769.2 26.1 %reduce-scatter.27.cloned.1.call-done = bf16[256,768]{0,1:T(8,128)(2,1)} async-done(((bf16[1024,768]{0,1:T(8,128)(2,1)}), bf16[256,768]{0,1:T(8,128)(2,1)}) %reduce-scatter.27.cloned.1.call-update) | async-done | bytes 393232 | tf_op jit(solution)/shard_map/reduce_scatter | solution.py:262
  821.6 5.5 add_add_fusion.1
  831.8 6.9 add_add_fusion
  849.6 74.9 %all-reduce.1 = f32[6912]{0:T(1024)S(1)} all-reduce(f32[6912]{0:T(1024)S(1)} %fusion.280), channel_id=32, replica_groups=mesh['section'=2,'ctx'=4,'fsdp'=4] {'ctx','fsdp'}, use_global_device_ids=true, to_apply=%region_63.64.clone | all-reduce | flops 6912 | bytes 55296
  930.8 118.0 %reduce-scatter.39.cloned.1.call-done = f32[48,2]{1,0:T(8,128)} async-done(((f32[768,2]{1,0:T(8,128)}), f32[48,2]{1,0:T(8,128)}) %reduce-scatter.39.cloned.1.call-update) | async-done | bytes 400
  1050.2 130.8 %reduce-scatter.31.cloned.1.call-done = f32[48,768]{1,0:T(8,128)} async-done(((f32[768,768]{1,0:T(8,128)}), f32[48,768]{1,0:T(8,128)}) %reduce-scatter.31.cloned.1.call-update) | async-done | bytes 147472 | tf_op jit(solution)/shard_map/reduce_scatter | solution.py:308
  1181.0 156.0 %reduce-scatter.29.cloned.1.call-done = f32[48,2304]{1,0:T(8,128)} async-done(((f32[768,2304]{1,0:T(8,128)}), f32[48,2304]{1,0:T(8,128)}) %reduce-scatter.29.cloned.1.call-update) | async-done | bytes 442384 | tf_op jit(solution)/shard_map/reduce_scatter | solution.py:306
  1337.0 177.5 %reduce-scatter.33.cloned.1.call-done = f32[48,3072]{1,0:T(8,128)} async-done(((f32[768,3072]{1,0:T(8,128)}), f32[48,3072]{1,0:T(8,128)}) %reduce-scatter.33.cloned.1.call-update) | async-done | bytes 589840 | tf_op jit(solution)/shard_map/reduce_scatter | solution.py:309
  1514.5 176.4 %reduce-scatter.35.cloned.1.call-done = f32[192,768]{1,0:T(8,128)} async-done(((f32[3072,768]{1,0:T(8,128)}), f32[192,768]{1,0:T(8,128)}) %reduce-scatter.35.cloned.1.call-update) | async-done | bytes 589840 | tf_op jit(solution)/shard_map/reduce_scatter | solution.py:310
  (657 shorter events, 238.3 us)
Async XLA Ops:
  7.2 49.6 %copy-start.14 = (bf16[2,1,256,768]{3,2,1,0:T(8,128)(2,1)S(1)}, bf16[2,1,256,768]{3,2,1,0:T(8,128)(2,1)}, u32[]{:S(2)}) copy-start(bf16[2,1,256,768]{3,2,1,0:T(8,128)(2,1)} %param.10) | copy-start | bytes 2359300
  7.2 59.2 %all-gather.30.cloned.1.call-start = ((), (), s32[]{:S(2)}) async-start(), calls=%async_computation.24 | async-start | bytes 4423680 | tf_op jit(solution)/shard_map/all_gather | solution.py:92
  8.0 115.1 %all-gather.34.cloned.1.call-start = ((), (), s32[]{:S(2)}) async-start(), calls=%async_computation.26 | async-start | bytes 5898240 | tf_op jit(solution)/shard_map/all_gather | solution.py:97
  8.7 173.3 %all-gather.36.cloned.1.call-start = ((), (), s32[]{:S(2)}) async-start(), calls=%async_computation.27 | async-start | bytes 5898240 | tf_op jit(solution)/shard_map/all_gather | solution.py:98
  9.5 212.3 %all-gather.20.cloned.1.call-start = ((), (), s32[]{:S(2)}) async-start(), calls=%async_computation.13 | async-start | bytes 1966080 | tf_op jit(solution)/shard_map/all_gather | solution.py:134
  56.8 599.0 %copy-start.104 = (f32[256,16]{0,1:T(8,128)}, f32[256,16]{0,1:T(8,128)S(1)}, u32[]{:S(2)}) copy-start(f32[256,16]{0,1:T(8,128)S(1)} %get-tuple-element.162) | copy-start | bytes 49156
  57.0 66.1 %copy-start.132 = (f32[256]{0:T(256)}, f32[256]{0:T(256)S(1)}, u32[]{:S(2)}) copy-start(f32[256]{0:T(256)S(1)} %broadcast_multiply_fusion.6) | copy-start | bytes 3076
  61.8 255.5 %copy-start.107 = (f32[768]{0:T(1024)}, f32[768]{0:T(1024)S(1)}, u32[]{:S(2)}) copy-start(f32[768]{0:T(1024)S(1)} %get-tuple-element.95) | copy-start | bytes 9220
  61.8 431.6 %copy-start.110 = (f32[768]{0:T(1024)}, f32[768]{0:T(1024)S(1)}, u32[]{:S(2)}) copy-start(f32[768]{0:T(1024)S(1)} %get-tuple-element.94) | copy-start | bytes 9220
  66.4 56.7 %copy-start.134 = (f32[256]{0:T(256)}, f32[256]{0:T(256)S(1)}, u32[]{:S(2)}) copy-start(f32[256]{0:T(256)S(1)} %add_rsqrt_fusion.2) | copy-start | bytes 3076
  76.8 182.9 %all-gather.18.cloned.1.call-start = ((), (), s32[]{:S(2)}) async-start(), calls=%async_computation.12 | async-start | bytes 1966080 | tf_op jit(solution)/shard_map/all_gather | solution.py:135
  79.1 208.4 %all-gather.32.cloned.1.call-start = ((), (), s32[]{:S(2)}) async-start(), calls=%async_computation.25 | async-start | bytes 1474560 | tf_op jit(solution)/shard_map/all_gather | solution.py:96
  79.6 271.0 %all-gather.24.cloned.1.call-start = ((), (), s32[]{:S(2)}) async-start(), calls=%async_computation.15 | async-start | bytes 1966080 | tf_op jit(solution)/shard_map/all_gather | solution.py:134
  79.7 54.3 %copy-start.175 = (f32[1,3072]{1,0:T(1,128)}, f32[1,3072]{1,0:T(1,128)S(1)}, u32[]{:S(2)}) copy-start(f32[1,3072]{1,0:T(1,128)S(1)} %slice.369) | copy-start | bytes 36868
  79.7 102.3 %copy-start.193 = (f32[768]{0:T(1024)}, f32[768]{0:T(1024)S(1)}, u32[]{:S(2)}) copy-start(f32[768]{0:T(1024)S(1)} %get-tuple-element.97) | copy-start | bytes 9220
  79.7 370.7 %copy-start.151 = (f32[768]{0:T(1024)}, f32[768]{0:T(1024)S(1)}, u32[]{:S(2)}) copy-start(f32[768]{0:T(1024)S(1)} %get-tuple-element.96) | copy-start | bytes 9220
  80.0 141.8 %copy-start.42 = (bf16[256,12,48]{0,2,1:T(8,128)(2,1)}, bf16[256,12,48]{0,2,1:T(8,128)(2,1)S(1)}, u32[]{:S(2)}) copy-start(bf16[256,12,48]{0,2,1:T(8,128)(2,1)S(1)} %slice.611) | copy-start | bytes 884740
  133.9 52.7 %copy-start.23 = (bf16[256,3072]{1,0:T(8,128)(2,1)}, bf16[256,3072]{1,0:T(8,128)(2,1)S(1)}, u32[]{:S(2)}) copy-start(bf16[256,3072]{1,0:T(8,128)(2,1)S(1)} %get-tuple-element.170) | copy-start | bytes 4718596
  289.3 11.9 collective-permute-start
  301.3 205.1 %copy-start.12 = (bf16[256,768]{1,0:T(8,128)(2,1)}, bf16[256,768]{1,0:T(8,128)(2,1)S(1)}, u32[]{:S(2)}) copy-start(bf16[256,768]{1,0:T(8,128)(2,1)S(1)} %get-tuple-element.115) | copy-start | bytes 1179652
  312.0 103.0 %copy-start.81 = (bf16[256,12,16]{0,2,1:T(8,128)(2,1)}, bf16[256,12,16]{0,2,1:T(8,128)(2,1)S(1)}, u32[]{:S(2)}) copy-start(bf16[256,12,16]{0,2,1:T(8,128)(2,1)S(1)} %get-tuple-element.152) | copy-start | bytes 294916
  312.8 76.0 %all-gather.22.cloned.1.call-start = ((), (), s32[]{:S(2)}) async-start(), calls=%async_computation.14 | async-start | bytes 1966080 | tf_op jit(solution)/shard_map/all_gather | solution.py:135
  317.3 142.3 %reduce-scatter.17.cloned.1.call-start = ((), (), s32[]{:S(2)}) async-start(), calls=%async_computation.18 | async-start | bytes 1966080 | tf_op jit(solution)/shard_map/reduce_scatter | solution.py:256
  329.6 85.4 %copy-start.40 = (bf16[256,12,48]{0,2,1:T(8,128)(2,1)}, bf16[256,12,48]{0,2,1:T(8,128)(2,1)S(1)}, u32[]{:S(2)}) copy-start(bf16[256,12,48]{0,2,1:T(8,128)(2,1)S(1)} %slice.609) | copy-start | bytes 884740
  329.6 158.7 %copy-start.180 = (f32[256]{0:T(256)}, f32[256]{0:T(256)S(1)}, u32[]{:S(2)}) copy-start(f32[256]{0:T(256)S(1)} %broadcast_multiply_fusion.3) | copy-start | bytes 3076
  418.2 70.1 %reduce-scatter.19.cloned.1.call-start = ((), (), s32[]{:S(2)}) async-start(), calls=%async_computation.19 | async-start | bytes 1966080 | tf_op jit(solution)/shard_map/reduce_scatter | solution.py:262
  442.6 97.3 %all-gather.28.cloned.1.call-start = ((), (), s32[]{:S(2)}) async-start(), calls=%async_computation.17 | async-start | bytes 1966080 | tf_op jit(solution)/shard_map/all_gather | solution.py:134
  451.2 8.1 collective-permute-start.1
  459.6 152.0 %copy-start.145 = (f32[256]{0:T(256)}, f32[256]{0:T(256)S(1)}, u32[]{:S(2)}) copy-start(f32[256]{0:T(256)S(1)} %broadcast_multiply_fusion.4) | copy-start | bytes 3076
  493.4 118.2 %copy-start.148 = (f32[256]{0:T(256)}, f32[256]{0:T(256)S(1)}, u32[]{:S(2)}) copy-start(f32[256]{0:T(256)S(1)} %add_rsqrt_fusion) | copy-start | bytes 3076
  503.1 74.8 %all-gather.26.cloned.1.call-start = ((), (), s32[]{:S(2)}) async-start(), calls=%async_computation.16 | async-start | bytes 1966080 | tf_op jit(solution)/shard_map/all_gather | solution.py:135
  509.4 4.7 collective-permute-start.2
  513.9 139.0 %reduce-scatter.21.cloned.1.call-start = ((), (), s32[]{:S(2)}) async-start(), calls=%async_computation.20 | async-start | bytes 1966080 | tf_op jit(solution)/shard_map/reduce_scatter | solution.py:256
  516.0 216.4 %copy-start.30 = (bf16[256,768]{1,0:T(8,128)(2,1)}, bf16[256,768]{1,0:T(8,128)(2,1)S(1)}, u32[]{:S(2)}) copy-start(bf16[256,768]{1,0:T(8,128)(2,1)S(1)} %get-tuple-element.103) | copy-start | bytes 1179652
  607.1 70.1 %reduce-scatter.23.cloned.1.call-start = ((), (), s32[]{:S(2)}) async-start(), calls=%async_computation.21 | async-start | bytes 1966080 | tf_op jit(solution)/shard_map/reduce_scatter | solution.py:262
  621.2 143.8 %reduce-scatter.25.cloned.1.call-start = ((), (), s32[]{:S(2)}) async-start(), calls=%async_computation.22 | async-start | bytes 1966080 | tf_op jit(solution)/shard_map/reduce_scatter | solution.py:256
  683.7 6.6 collective-permute-start.3
  723.6 71.7 %reduce-scatter.27.cloned.1.call-start = ((), (), s32[]{:S(2)}) async-start(), calls=%async_computation.23 | async-start | bytes 1966080 | tf_op jit(solution)/shard_map/reduce_scatter | solution.py:262
  747.7 181.7 %reduce-scatter.37.cloned.1.call-start = ((), (), s32[]{:S(2)}) async-start(), calls=%async_computation.32 | async-start | bytes 417792
  802.1 246.7 %reduce-scatter.39.cloned.1.call-start = ((), (), s32[]{:S(2)}) async-start(), calls=%async_computation.33 | async-start | bytes 417792
  803.3 377.6 %reduce-scatter.31.cloned.1.call-start = ((), (), s32[]{:S(2)}) async-start(), calls=%async_computation.29 | async-start | bytes 2506752 | tf_op jit(solution)/shard_map/reduce_scatter | solution.py:308
  807.8 529.1 %reduce-scatter.29.cloned.1.call-start = ((), (), s32[]{:S(2)}) async-start(), calls=%async_computation.28 | async-start | bytes 7520256 | tf_op jit(solution)/shard_map/reduce_scatter | solution.py:306
  816.8 697.7 %reduce-scatter.33.cloned.1.call-start = ((), (), s32[]{:S(2)}) async-start(), calls=%async_computation.30 | async-start | bytes 10027008 | tf_op jit(solution)/shard_map/reduce_scatter | solution.py:309
  827.2 863.7 %reduce-scatter.35.cloned.1.call-start = ((), (), s32[]{:S(2)}) async-start(), calls=%async_computation.31 | async-start | bytes 10027008 | tf_op jit(solution)/shard_map/reduce_scatter | solution.py:310
  847.1 79.4 %copy-start.95 = (bf16[256,768]{1,0:T(8,128)(2,1)S(1)}, bf16[256,768]{1,0:T(8,128)(2,1)}, u32[]{:S(2)}) copy-start(bf16[256,768]{1,0:T(8,128)(2,1)} %copy-done.94) | copy-start | bytes 1179652
  847.1 79.3 %copy-start.184 = (f32[256]{0:T(256)S(1)}, f32[256]{0:T(256)}, u32[]{:S(2)}) copy-start(f32[256]{0:T(256)} %copy-done.183) | copy-start | bytes 3076
  847.1 79.3 %copy-start.186 = (f32[256]{0:T(256)S(1)}, f32[256]{0:T(256)}, u32[]{:S(2)}) copy-start(f32[256]{0:T(256)} %copy-done.185) | copy-start | bytes 3076
  848.7 79.8 %copy-start.91 = (bf16[1,256,768]{2,1,0:T(8,128)(2,1)S(1)}, bf16[1,256,768]{2,1,0:T(8,128)(2,1)}, u32[]{:S(2)}) copy-start(bf16[1,256,768]{2,1,0:T(8,128)(2,1)} %get-tuple-element.104) | copy-start | bytes 1179652
  (186 other events, 1492.3 us)
Sparse Core Ops, SparseCore 0:
  9.9 54.3 all-gather.29
  66.1 56.9 all-gather.33
  124.9 57.0 all-gather.35
  184.0 37.6 all-gather.19
  223.8 35.9 all-gather.17
  261.4 25.9 all-gather.31
  312.9 37.6 all-gather.23
  352.8 35.9 all-gather.21
  418.3 33.5 reduce-scatter.16
  454.0 34.2 reduce-scatter.18
  503.2 36.6 all-gather.27
  541.9 35.9 all-gather.25
  607.2 33.4 reduce-scatter.20
  642.9 34.2 reduce-scatter.22
  723.7 35.0 reduce-scatter.24
  760.9 34.2 reduce-scatter.26
  802.3 120.5 reduce-scatter.36
  928.1 120.7 reduce-scatter.38
  1054.3 126.6 reduce-scatter.30
  1187.6 149.3 reduce-scatter.28
  1344.2 170.2 reduce-scatter.32
  1520.7 170.1 reduce-scatter.34
where the time goes:
time: 1710 us; the launch traced here: 1700 us
  waiting for transfers between devices  1100 us (64%)
  matrix products  280 us (16%)
  blocking collectives  115 us (7%)
  other arithmetic  83.1 us (5%)
  local copies, waits for them, and re-layouts  78 us (5%)
  starting transfers between devices  19 us (1%)
  between operations  19 us (1%)
    reduce_scatter x1, waiting for transfers between devices, per_device(): lax.psum_scatter(terms[5], ('ctx', 'fsdp'), scatter_dimension=0, tiled=True)  177 us
    reduce_scatter x1, waiting for transfers between devices, per_device(): lax.psum_scatter(terms[6], ('ctx', 'fsdp'), scatter_dimension=0, tiled=True)  176 us
    reduce_scatter x1, waiting for transfers between devices, per_device(): lax.psum_scatter(terms[2], ('ctx', 'fsdp'), scatter_dimension=0, tiled=True)  156 us
    reduce_scatter x1, waiting for transfers between devices, per_device(): lax.psum_scatter(terms[4], ('ctx', 'fsdp'), scatter_dimension=0, tiled=True)  131 us
    unnamed x24, waiting for transfers between devices  121 us
    unnamed x2, blocking collectives  92.6 us
    all_gather x3, waiting for transfers between devices, per_device(): value_all = lax.all_gather(value_rows, 'ctx', axis=0, tiled=True)  83.9 us
    all_gather x3, waiting for transfers between devices, per_device(): key_all = lax.all_gather(key_rows, 'ctx', axis=0, tiled=True)  76.8 us
  transfers between devices with their start and end apart: 26, of which 17 were waited for; matrix products, arithmetic and copies ran while one was open for 17% of the time, Pallas kernels for 0%

commit v1 on v0

v1 whole, which is shorter than its diff:
```python
import jax
import jax.numpy as jnp
from jax import lax
from jax.sharding import PartitionSpec as P

D = 768
HEADS = 12
HEAD_DIM = 64
ROT = 16
FF = 3072
BF = jnp.bfloat16
F32 = jnp.float32


def pick(stack, index, axis=0):
    return lax.dynamic_index_in_dim(stack, index, axis, keepdims=False)


def swap_cores(block):
    return lax.ppermute(block, "section", [(0, 1), (1, 0)])


def along_ctx(block, step):
    count = lax.axis_size("ctx")
    return lax.ppermute(block, "ctx", [(i, i ^ step) for i in range(count)])


def along_square(block):
    count = lax.axis_size("fsdp")
    route = [(core * count + i, core * count + (i ^ (1 + core))) for core in (0, 1) for i in range(count)]
    return lax.ppermute(block, ("section", "fsdp"), route)


def across_halves(block, source_core, target_core):
    count = lax.axis_size("ctx")
    route = [
        (source_core * count + i, target_core * count + (i + count // 2) % count)
        for i in range(count)
    ]
    return lax.ppermute(block, ("section", "ctx"), route)


def half_columns(block, which):
    width = block.shape[-1] // 2
    return lax.dynamic_slice_in_dim(block, which * width, width, block.ndim - 1)


def gather_matrix(shard, core, place):
    rows, cols = shard.shape
    mine = along_square(shard)
    theirs = swap_cores(mine)
    halved = theirs.reshape(2, rows // 2, cols)
    diag_mine = along_square(pick(halved, core))
    diag_theirs = swap_cores(diag_mine)
    whole = jnp.zeros((8, rows // 2, cols), shard.dtype)

    def put(whole, piece, index):
        return lax.dynamic_update_slice_in_dim(
            whole, piece.reshape(-1, rows // 2, cols), index, 0
        )

    whole = put(whole, shard, 2 * place)
    whole = put(whole, mine, 2 * (place ^ (1 + core)))
    whole = put(whole, theirs, 2 * (place ^ (2 - core)))
    whole = put(whole, diag_mine, 2 * (place ^ 3) + core)
    whole = put(whole, diag_theirs, 2 * (place ^ 3) + 1 - core)
    return whole.reshape(4 * rows, cols)


def gather_vectors(packed, core, place):
    own = [packed, *[
        lax.ppermute(packed, "fsdp", [(i, i ^ k) for i in range(4)]) for k in (1, 2, 3)
    ]]
    mine = jnp.stack(own)[place ^ jnp.arange(4)]
    theirs = swap_cores(mine)
    first = jnp.where(core == 0, mine, theirs)
    second = jnp.where(core == 0, theirs, mine)
    return first, second


def sum_over_square(parts, core, place):
    own = pick(parts, place, 1)
    mine = pick(parts, place ^ (1 + core), 1)
    theirs = pick(parts, place ^ (2 - core), 1)
    diag = pick(parts, place ^ 3, 1)
    mine_sib = swap_cores(theirs)
    diag_sib = swap_cores(half_columns(diag, 1 - core))
    diag_sum = half_columns(diag, core).astype(F32) + diag_sib.astype(F32)
    extra = swap_cores(along_square(diag_sum.astype(BF)))
    near = half_columns(mine, core).astype(F32) + half_columns(mine_sib, core).astype(F32)
    far = (
        half_columns(mine, 1 - core).astype(F32)
        + half_columns(mine_sib, 1 - core).astype(F32)
        + extra.astype(F32)
    )
    landed = along_square(jnp.stack([near, far]).astype(BF))
    give = half_columns(own, 1 - core).astype(F32) + landed[1].astype(F32)
    got = swap_cores(give.astype(BF))
    return half_columns(own, core).astype(F32) + landed[0].astype(F32) + got.astype(F32)


def sum_over_ctx(total, ctx_idx):
    count = lax.axis_size("ctx")
    step = 1
    while step < count:
        bit = (ctx_idx // step) % 2
        pairs = total.reshape(total.shape[0] // 2, 2, *total.shape[1:])
        sent = pick(pairs, 1 - bit, 1).astype(BF)
        total = pick(pairs, bit, 1) + along_ctx(sent, step).astype(F32)
        step *= 2
    return total[0]


def angle_tables(places):
    half_dims = ROT // 2
    frequency = 10000.0 ** (-(jnp.arange(half_dims, dtype=F32) * 2.0) / ROT)
    phases = places.astype(F32)[:, None] * frequency[None, :]
    phases = jnp.concatenate([phases, phases], -1)
    return (jnp.cos(phases)[:, None, :], jnp.sin(phases)[:, None, :])


def rotary(head_rows, cosine, sine):
    half_dims = ROT // 2
    rot_part = head_rows[..., :ROT]
    swapped = jnp.concatenate([-rot_part[..., half_dims:], rot_part[..., :half_dims]], -1)
    return jnp.concatenate([rot_part * cosine + swapped * sine, head_rows[..., ROT:]], -1)


def rotate_rows(rows, cosine, sine):
    heads = rows.reshape(rows.shape[0], HEADS, HEAD_DIM)
    return rotary(heads, cosine, sine).reshape(rows.shape)


def dot_f32(left, right):
    return jnp.dot(left, right, preferred_element_type=F32)


def dot_t(left, right):
    return lax.dot_general(left, right, (((1,), (1,)), ((), ())), preferred_element_type=F32)


def dot_rows(left, right):
    out = lax.dot_general(left, right, (((0,), (0,)), ((), ())), preferred_element_type=F32)
    return out.astype(BF)


def heads_of(rows):
    return rows.reshape(rows.shape[0], HEADS, HEAD_DIM)


def attention(query, key, value, allowed):
    scores = (
        jnp.einsum("qhd,khd->hqk", heads_of(query), heads_of(key), preferred_element_type=F32)
        * 0.125
    )
    scores = jnp.where(allowed, scores, -1e30)
    row_max = jnp.max(scores, -1, keepdims=True)
    exp_scores = jnp.exp(scores - row_max)
    row_sum = jnp.sum(exp_scores, -1, keepdims=True)
    probs = (exp_scores / row_sum).astype(BF)
    mixed = jnp.einsum("hqk,khd->qhd", probs, heads_of(value), preferred_element_type=F32)
    return mixed.reshape(query.shape).astype(BF), row_max, row_sum


def attention_back(query, key, value, allowed, row_max, row_sum, mixed_grad):
    q, k, v, dm = heads_of(query), heads_of(key), heads_of(value), heads_of(mixed_grad)
    scores = jnp.einsum("qhd,khd->hqk", q, k, preferred_element_type=F32) * 0.125
    scores = jnp.where(allowed, scores, -1e30)
    probs = jnp.exp(scores - row_max) / row_sum
    prob_grad = jnp.einsum("qhd,khd->hqk", dm, v, preferred_element_type=F32)
    centre = jnp.sum(probs * prob_grad, -1, keepdims=True)
    score_grad = (probs * (prob_grad - centre)).astype(BF)
    query_grad = jnp.einsum("hqk,khd->qhd", score_grad, k, preferred_element_type=F32) * 0.125
    key_grad = jnp.einsum("hqk,qhd->khd", score_grad, q, preferred_element_type=F32) * 0.125
    value_grad = jnp.einsum("hqk,qhd->khd", probs.astype(BF), dm, preferred_element_type=F32)
    return (
        query_grad.reshape(query.shape),
        key_grad.reshape(key.shape),
        value_grad.reshape(value.shape),
    )


def gelu_exact(up_rows):
    return jax.nn.gelu(up_rows, approximate=False)


def per_device(
    inputs,
    cotangent,
    block_order,
    norm_gain,
    norm_bias,
    qkv_weight,
    biases,
    out_weight,
    up_weight,
    down_weight,
):
    rows_dev = inputs.shape[2]
    core = lax.axis_index("section")
    ctx_idx = lax.axis_index("ctx")
    place = lax.axis_index("fsdp")
    ranks = lax.axis_size("ctx")
    squares = lax.axis_size("fsdp")
    group = ranks // 2
    micro = ctx_idx // group

    def rank_of(core_idx, ctx_of):
        return (ctx_of + core_idx * group) % ranks

    def places_of(rank):
        block = rows_dev // 2
        within = jnp.arange(rows_dev, dtype=jnp.int32)
        first = block_order[rank]
        block_ids = jnp.where(within < block, first, 2 * ranks - 1 - first)
        return block_ids * block + within % block

    def take_rows(whole):
        here = pick(whole[:, 0], micro)
        there = across_halves(pick(whole[:, 0], 1 - micro), 1, 1)
        return jnp.where(core == 0, here, there)

    def deliver(rows, layer):
        moved = across_halves(rows, 1, layer)
        here = rows if layer == 0 else lax.ppermute(rows, "section", [(0, 1)])
        first = jnp.where(micro == 0, here, moved)
        second = jnp.where(micro == 0, moved, here)
        return jnp.stack([first, second])

    packed = jnp.concatenate([norm_gain[0].reshape(-1), norm_bias[0].reshape(-1), biases[0]])
    vectors = gather_vectors(packed, core, place)
    shards = (qkv_weight[0], out_weight[0], up_weight[0], down_weight[0])
    siblings = [swap_cores(shard) for shard in shards]
    weights = []
    for layer in (0, 1):
        mats = [
            gather_matrix(jnp.where(core == layer, shard, sibling), core, place)
            for shard, sibling in zip(shards, siblings)
        ]
        vec = vectors[layer]
        width = norm_gain.shape[2]
        gains = [vec[:, j * width : (j + 1) * width].reshape(D) for j in (0, 1)]
        shifts = [vec[:, (2 + j) * width : (3 + j) * width].reshape(D) for j in (0, 1)]
        bias = vec[:, 4 * width :].reshape(-1)
        weights.append((mats, gains, shifts, bias))

    own_places = places_of(rank_of(core, ctx_idx))
    key_places = jnp.concatenate(
        [places_of(rank_of(one, ctx_idx ^ j)) for one in (core, 1 - core) for j in range(group)]
    )
    cosine, sine = angle_tables(own_places)
    allowed = (own_places[:, None] >= key_places[None, :])[None]

    tok_low = take_rows(inputs)
    top_grad = take_rows(cotangent)
    kept = []
    layer_outs = []
    for layer in (0, 1):
        (qkv_mat, out_mat, up_mat, down_mat), gains, shifts, bias = weights[layer]
        tok_rows = tok_low.astype(F32)
        row_mean = jnp.mean(tok_rows, -1, keepdims=True)
        centred = tok_rows - row_mean
        inverse = lax.rsqrt(jnp.mean(centred * centred, -1, keepdims=True) + 1e-05)
        normed = centred * inverse
        attn_in = (normed * gains[0] + shifts[0]).astype(BF)
        mlp_in = (normed * gains[1] + shifts[1]).astype(BF)
        qkv_rows = dot_f32(attn_in, qkv_mat) + bias[: 3 * D]
        query = rotate_rows(qkv_rows[:, :D], cosine, sine).astype(BF)
        key_rows = rotate_rows(qkv_rows[:, D : 2 * D], cosine, sine).astype(BF)
        value_rows = qkv_rows[:, 2 * D :].astype(BF)
        pair = jnp.concatenate([key_rows, value_rows], -1)
        near = [pair, *[along_ctx(pair, j) for j in range(1, group)]]
        far = [swap_cores(one) for one in near]
        every = jnp.concatenate(near + far)
        key, value = every[:, :D], every[:, D:]
        up_rows = dot_f32(mlp_in, up_mat) + bias[4 * D : 4 * D + FF]
        gelu_rows = gelu_exact(up_rows).astype(BF)
        mlp_rows = dot_f32(gelu_rows, down_mat) + bias[4 * D + FF :]
        mixed, row_max, row_sum = attention(query, key, value, allowed)
        attn_rows = dot_f32(mixed, out_mat) + bias[3 * D : 4 * D]
        tok_low = (tok_rows + (attn_rows + mlp_rows)).astype(BF)
        kept.append(
            (normed, inverse, attn_in, mlp_in, query, key, value, row_max, row_sum, mixed, up_rows, gelu_rows)
        )
        layer_outs.append(deliver(tok_low, layer))

    grad_low = top_grad
    grad_outs = [None, None]
    reduced = [None, None]
    blocks = ranks * squares

    def fold(grad):
        split = grad.reshape(ranks, squares, -1, grad.shape[1])
        return [split[..., j : j + D] for j in range(0, grad.shape[1], D)]

    for layer in (1, 0):
        (qkv_mat, out_mat, up_mat, down_mat), gains, shifts, bias = weights[layer]
        (normed, inverse, attn_in, mlp_in, query, key, value, row_max, row_sum, mixed, up_rows, gelu_rows) = kept[layer]
        mixed_grad = dot_t(grad_low, out_mat).astype(BF)
        query_grad, key_grad, value_grad = attention_back(
            query, key, value, allowed, row_max, row_sum, mixed_grad
        )
        pair_grad = jnp.concatenate([key_grad, value_grad], -1)
        local = pair_grad[: group * rows_dev]
        remote = pair_grad[group * rows_dev :].astype(BF)
        local = local + swap_cores(remote).astype(F32)
        total = local[:rows_dev]
        for j in range(1, group):
            sent = local[j * rows_dev : (j + 1) * rows_dev].astype(BF)
            total = total + along_ctx(sent, j).astype(F32)

        down_term = dot_rows(gelu_rows, grad_low)
        gelu_grad = dot_t(grad_low, down_mat)
        up_grad = jax.vjp(gelu_exact, up_rows)[1](gelu_grad)[0].astype(BF)
        up_term = dot_rows(mlp_in, up_grad)
        mlp_back = dot_t(up_grad, up_mat)
        out_term = dot_rows(mixed, grad_low)

        wide = jnp.concatenate(fold(down_term) + fold(up_term) , 2)
        wide = sum_over_ctx(sum_over_square(wide, core, place), ctx_idx)

        qkv_grad = jnp.concatenate(
            [
                rotate_rows(query_grad, cosine, -sine),
                rotate_rows(total[:, :D], cosine, -sine),
                total[:, D:],
            ],
            -1,
        ).astype(BF)
        qkv_term = dot_rows(attn_in, qkv_grad)
        attn_back = dot_t(qkv_grad, qkv_mat)
        norm_grad = attn_back * gains[0] + mlp_back * gains[1]
        centre = jnp.mean(norm_grad, -1, keepdims=True)
        along = jnp.mean(norm_grad * normed, -1, keepdims=True)
        back_rows = grad_low.astype(F32) + (norm_grad - centre - normed * along) * inverse
        gain_terms = [jnp.sum(attn_back * normed, 0), jnp.sum(mlp_back * normed, 0)]
        shift_terms = [jnp.sum(attn_back, 0), jnp.sum(mlp_back, 0)]
        grad_total = jnp.sum(grad_low.astype(F32), 0)
        bias_term = jnp.concatenate(
            [
                jnp.sum(qkv_grad.astype(F32), 0),
                grad_total,
                jnp.sum(up_grad.astype(F32), 0),
                grad_total,
            ]
        )
        small = jnp.concatenate(
            [one.reshape(blocks, -1) for one in gain_terms + shift_terms + [bias_term]], 1
        )
        small_width = small.shape[1]
        small = jnp.pad(small, ((0, 0), (0, 16 * D - small_width)))
        small = small.reshape(ranks, squares, 16, D).astype(BF)
        thin = jnp.concatenate(fold(qkv_term) + fold(out_term) + [small], 2)
        thin = sum_over_ctx(sum_over_square(thin, core, place), ctx_idx)
        grad_low = back_rows.astype(BF)
        grad_outs[layer] = deliver(grad_low, layer)
        reduced[layer] = (wide, thin)

    def finish(first, second):
        mine = jnp.where(core == 0, first, second)
        got = swap_cores(jnp.where(core == 0, second, first))
        return jnp.where(
            core == 0, jnp.concatenate([mine, got], -1), jnp.concatenate([got, mine], -1)
        )

    wide, thin = (finish(a, b) for a, b in zip(reduced[0], reduced[1]))
    down_rows = FF // blocks
    narrow = D // blocks

    def unfold(rows, count):
        return jnp.concatenate([rows[j * narrow : (j + 1) * narrow] for j in range(count)], -1)

    down_out = wide[:down_rows]
    up_out = unfold(wide[down_rows:], 4)
    qkv_out = unfold(thin, 3)
    out_out = thin[3 * narrow : 4 * narrow]
    small = thin[4 * narrow :].reshape(-1)[:small_width]
    gain_out = small[: 2 * narrow].reshape(2, narrow)
    shift_out = small[2 * narrow : 4 * narrow].reshape(2, narrow)
    bias_out = small[4 * narrow :]
    layer_out = jnp.where(core == 0, layer_outs[0], layer_outs[1])
    input_grads = jnp.where(core == 0, grad_outs[0], grad_outs[1])
    return (
        layer_out[None, :, None],
        input_grads[None, :, None],
        gain_out[None],
        shift_out[None],
        qkv_out[None],
        bias_out[None],
        out_out[None],
        up_out[None],
        down_out[None],
    )


def solution(mesh):
    in_specs = (
        P(None, "fsdp", "ctx", None),
        P(None, "fsdp", "ctx", None),
        P(),
        P("section", None, "fsdp"),
        P("section", None, "fsdp"),
        P("section", "fsdp", None),
        P("section", "fsdp"),
        P("section", "fsdp", None),
        P("section", "fsdp", None),
        P("section", "fsdp", None),
    )
    out_specs = (
        P("section", None, "fsdp", "ctx", None),
        P("section", None, "fsdp", "ctx", None),
        P("section", None, ("ctx", "fsdp")),
        P("section", None, ("ctx", "fsdp")),
        P("section", ("ctx", "fsdp"), None),
        P("section", ("ctx", "fsdp")),
        P("section", ("ctx", "fsdp"), None),
        P("section", ("ctx", "fsdp"), None),
        P("section", ("ctx", "fsdp"), None),
    )
    return jax.shard_map(
        per_device, mesh=mesh, in_specs=in_specs, out_specs=out_specs, check_vma=False
    )
```

time: 1710 us -> 668 us (0.39)
  waiting for transfers between devices: 1100 us -> 199 us
  matrix products: 280 us -> 135 us
  blocking collectives: 115 us -> 0 us
  starting transfers between devices: 19 us -> 78.8 us
  local copies, waits for them, and re-layouts: 78 us -> 136 us
  other arithmetic: 83.1 us -> 101 us
    reduce_scatter x10 -> x0, waiting for transfers between devices: 711 us -> none  [the longest x1 177 us: per_device(): lax.psum_scatter(terms[5], ('ctx', 'fsdp'), scatter_dimension=0, tiled=True)]
    all_gather x10 -> x0, waiting for transfers between devices: 273 us -> none  [the longest x3 83.9 us: per_device(): value_all = lax.all_gather(value_rows, 'ctx', axis=0, tiled=True)]
    ppermute x4 -> x92, waiting for transfers between devices: 0.01 us -> 199 us  [the longest x24 127 us: along_square(): return lax.ppermute(block, ('section', 'fsdp'), route)]
    dot_general x57 -> x34, matrix products: 280 us -> 114 us  [the longest x8 26.8 us: dot_f32(): return jnp.dot(left, right, preferred_element_type=F32)]
    unnamed x24 -> x0, waiting for transfers between devices: 121 us -> none
    unnamed x2 -> x0, blocking collectives: 92.6 us -> none
    ppermute x4 -> x92, starting transfers between devices: 16.8 us -> 78.8 us  [the longest x45 27.6 us: swap_cores(): return lax.ppermute(block, 'section', [(0, 1), (1, 0)])]
    dynamic_update_slice x0 -> x40, local copies, waits for them, and re-layouts: none -> 25.7 us  [put(): lax.dynamic_update_slice_in_dim(whole, piece.reshape(-1, rows // 2, cols)...]
  transfers between devices with their start and end apart: 26 -> 92, of which waited for: 17 -> 25; matrix products, arithmetic and copies ran while one was open for 17% -> 53% of each run, Pallas kernels for 0% -> 0%
where the time goes in v1:
time: 668 us; the launch traced here: 657 us
  waiting for transfers between devices  199 us (30%)
  local copies, waits for them, and re-layouts  136 us (20%)
  matrix products  135 us (20%)
  other arithmetic  101 us (15%)
  starting transfers between devices  78.8 us (12%)
  between operations  6.7 us (1%)
    ppermute x24, waiting for transfers between devices, along_square(): return lax.ppermute(block, ('section', 'fsdp'), route)  127 us
    ppermute x12, waiting for transfers between devices, along_ctx(): return lax.ppermute(block, 'ctx', [(i, i ^ step) for i in range(count)])  70.2 us
    unnamed x318, local copies, waits for them, and re-layouts  28.8 us
    ppermute x45, starting transfers between devices, swap_cores(): return lax.ppermute(block, 'section', [(0, 1), (1, 0)])  27.6 us
    dot_general x8, matrix products, dot_f32(): return jnp.dot(left, right, preferred_element_type=F32)  26.8 us
    dynamic_update_slice x40, local copies, waits for them, and re-layouts, put(): lax.dynamic_update_slice_in_dim(whole, piece.reshape(-1, rows // 2, cols)...  25.7 us
    dot_general x8, matrix products, dot_t(): lax.dot_general(left, right, (((1,), (1,)), ((), ())), preferred_element_...  25 us
    ppermute x24, starting transfers between devices, along_square(): return lax.ppermute(block, ('section', 'fsdp'), route)  24.1 us
  transfers between devices with their start and end apart: 92, of which 25 were waited for; matrix products, arithmetic and copies ran while one was open for 53% of the time, Pallas kernels for 0%

profile of v1, /device:TPU:0, one launch (start us, length us, event | category | flops | bytes accessed | tf_op | source)
XLA Modules:
  0.0 656.5 jit_solution(5837183650025266350)
XLA Ops:
  3.0 4.0 collective-permute-start.3
  20.9 3.9 collective-permute-start.5
  43.1 3.0 collective-permute-done.36
  52.0 10.2 %collective-permute-done.16 = bf16[96,768]{1,0:T(8,128)(2,1)S(1)} collective-permute-done((bf16[96,768]{1,0:T(8,128)(2,1)S(1)}, bf16[96,768]{1,0:T(8,128)(2,1)S(1)}, u32[]{:S(2)}, u32[]{:S(2)}) %collective-permute-start.16) | collective-permute-done | bytes 147488 | tf_op jit(solution)/shard_map/ppermute | solution.py:31
  79.8 9.9 %collective-permute-done.19 = bf16[192,3072]{1,0:T(8,128)(2,1)} collective-permute-done((bf16[192,3072]{1,0:T(8,128)(2,1)S(1)}, bf16[192,3072]{1,0:T(8,128)(2,1)}, u32[]{:S(2)}, u32[]{:S(2)}) %collective-permute-start.19) | collective-permute-done | bytes 1179680 | tf_op jit(solution)/shard_map/ppermute | solution.py:31
  91.1 11.2 %collective-permute-done.40 = bf16[192,3072]{1,0:T(8,128)(2,1)} collective-permute-done((bf16[192,3072]{1,0:T(8,128)(2,1)S(1)}, bf16[192,3072]{1,0:T(8,128)(2,1)}, u32[]{:S(2)}, u32[]{:S(2)}) %collective-permute-start.40) | collective-permute-done | bytes 1179680 | tf_op jit(solution)/shard_map/ppermute | solution.py:31
  103.8 11.2 %collective-permute-done.24 = bf16[768,768]{1,0:T(8,128)(2,1)} collective-permute-done((bf16[768,768]{1,0:T(8,128)(2,1)S(1)}, bf16[768,768]{1,0:T(8,128)(2,1)}, u32[]{:S(2)}, u32[]{:S(2)}) %collective-permute-start.24) | collective-permute-done | bytes 1179680 | tf_op jit(solution)/shard_map/ppermute | solution.py:31
  116.5 11.2 %collective-permute-done.44 = bf16[768,768]{1,0:T(8,128)(2,1)} collective-permute-done((bf16[768,768]{1,0:T(8,128)(2,1)S(1)}, bf16[768,768]{1,0:T(8,128)(2,1)}, u32[]{:S(2)}, u32[]{:S(2)}) %collective-permute-start.44) | collective-permute-done | bytes 1179680 | tf_op jit(solution)/shard_map/ppermute | solution.py:31
  131.5 6.7 %collective-permute-done.8 = bf16[96,2304]{1,0:T(8,128)(2,1)S(1)} collective-permute-done((bf16[96,2304]{1,0:T(8,128)(2,1)S(1)}, bf16[96,2304]{1,0:T(8,128)(2,1)S(1)}, u32[]{:S(2)}, u32[]{:S(2)}) %collective-permute-start.8) | collective-permute-done | bytes 442400 | tf_op jit(solution)/shard_map/ppermute | solution.py:31
  139.7 6.8 %collective-permute-done.31 = bf16[96,2304]{1,0:T(8,128)(2,1)S(1)} collective-permute-done((bf16[96,2304]{1,0:T(8,128)(2,1)S(1)}, bf16[96,2304]{1,0:T(8,128)(2,1)S(1)}, u32[]{:S(2)}, u32[]{:S(2)}) %collective-permute-start.31) | collective-permute-done | bytes 442400 | tf_op jit(solution)/shard_map/ppermute | solution.py:31
  192.4 7.2 %collective-permute-done.42 = bf16[96,3072]{1,0:T(8,128)(2,1)S(1)} collective-permute-done((bf16[96,3072]{1,0:T(8,128)(2,1)S(1)}, bf16[96,3072]{1,0:T(8,128)(2,1)S(1)}, u32[]{:S(2)}, u32[]{:S(2)}) %collective-permute-start.42) | collective-permute-done | bytes 589856 | tf_op jit(solution)/shard_map/ppermute | solution.py:31
  201.1 11.4 %multiply_convert_fusion.3 = (bf16[256,3072]{1,0:T(8,128)(2,1)S(1)}, f32[256,3072]{1,0:T(8,128)}, f32[256,3072]{1,0:T(8,128)}) fusion(f32[3072]{0:T(1024)S(1)} %slice-done.17, bf16[768,3072]{1,0:T(8,128)(2,1)S(1)} %bitcast.509, bf16[256,768]{1,0:T(8,128)(2,1)S(1)} %get-tuple-element.35, f32[768]{0:T(1024)S(1)} %copy-done.85, f32[768]{0:T(1024)S(1)} %copy-done.82, ...), kind=kOutput, calls=%fused_computation.68 | convolution fusion | flops 1261043712 | bytes 12996608 | tf_op jit(solution)/shard_map/dot_general | solution.py:135
  217.3 3.0 pad_maximum_fusion.2
  227.5 11.0 %fusion.203 = (f32[12,256]{1,0:T(8,128)}, f32[12,256,1024]{2,1,0:T(8,128)}) fusion(pred[256,1024]{1,0:T(8,128)(4,1)} %broadcast_compare_fusion, bf16[1024,12,64]{0,2,1:T(8,128)(2,1)} %bitcast.495, bf16[256,12,48]{0,2,1:T(8,128)(2,1)S(1)} %copy-done.63, bf16[256,12,16]{0,2,1:T(8,128)(2,1)S(1)} %copy-done.73), kind=kOutput, calls=%fused_computation.486 | convolution fusion | flops 416023552 | bytes 14823424 | tf_op jit(solution)/shard_map/sub | solution.py:158
  238.5 7.1 %fusion.70 = bf16[12,64,256]{2,1,0:T(8,128)(2,1)S(1)} fusion(bf16[1024,12,64]{0,2,1:T(8,128)(2,1)} %bitcast.561, f32[12,256,1024]{2,1,0:T(8,128)} %get-tuple-element.141, f32[12,256]{1,0:T(8,128)} %get-tuple-element.140), kind=kOutput, calls=%fused_computation.161 | convolution fusion | flops 409141248 | bytes 14561280 | tf_op jit(solution)/shard_map/hqk,khd->qhd/dot_general | solution.py:161
  260.7 4.1 convolution_add_fusion.2
  264.9 11.0 %fusion.185 = (bf16[3072]{0:T(1024)(128)(2,1)}, bf16[256,3072]{1,0:T(8,128)(2,1)S(1)}, f32[256,3072]{1,0:T(8,128)S(1)}) fusion(f32[256,3072]{1,0:T(8,128)S(1)} %convolution_add_fusion.2, bf16[256,768]{1,0:T(8,128)(2,1)S(1)} %get-tuple-element.25, bf16[3072,768]{1,0:T(8,128)(2,1)S(1)} %bitcast.506), kind=kOutput, calls=%fused_computation.471 | convolution fusion | flops 1265366016 | bytes 12982272 | tf_op jit(solution)/shard_map/dot_general | solution.py:139
  280.7 3.6 copy-done.1
  294.5 3.8 collective-permute-start.35
  298.3 3.3 dynamic-slice_bitcast_fusion
  301.6 4.6 convolution_add_fusion.6
  306.2 3.5 fusion.38
  310.3 4.1 pad_maximum_fusion.3
  317.9 10.8 %fusion.204 = (f32[12,256]{1,0:T(8,128)}, f32[12,256,1024]{2,1,0:T(8,128)}) fusion(pred[256,1024]{1,0:T(8,128)(4,1)} %broadcast_compare_fusion, bf16[1024,12,64]{0,2,1:T(8,128)(2,1)S(1)} %bitcast.498, bf16[256,12,48]{0,2,1:T(8,128)(2,1)} %slice.713, bf16[256,12,16]{0,2,1:T(8,128)(2,1)} %get-tuple-element.124), kind=kOutput, calls=%fused_computation.487 | convolution fusion | flops 416023552 | bytes 14823424 | tf_op jit(solution)/shard_map/sub | solution.py:158
  328.7 6.2 fusion.23
  337.4 5.7 multiply_reduce_fusion.1
  343.1 5.8 multiply_convert_fusion.1
  352.7 5.1 fusion.73
  357.8 3.6 fusion.52
  370.7 4.1 fusion.80
  376.9 8.0 %collective-permute-done.52 = bf16[256,1536]{0,1:T(8,128)(2,1)S(1)} collective-permute-done((bf16[256,1536]{0,1:T(8,128)(2,1)S(1)}, bf16[256,1536]{0,1:T(8,128)(2,1)S(1)}, u32[]{:S(2)}, u32[]{:S(2)}) %collective-permute-start.52) | collective-permute-done | bytes 786464 | tf_op jit(solution)/shard_map/ppermute | solution.py:25
  391.7 3.1 fusion.189
  396.3 10.2 %multiply_reduce_fusion = (f32[12,256]{1,0:T(8,128)S(1)}, f32[12,256,1024]{2,1,0:T(8,128)}) fusion(f32[12,256,1024]{2,1,0:T(8,128)} %get-tuple-element.141, f32[12,256]{1,0:T(8,128)S(1)} %copy-done.98, bf16[256,12,64]{0,2,1:T(8,128)(2,1)S(1)} %bitcast.598, bf16[1024,12,64]{0,2,1:T(8,128)(2,1)S(1)} %bitcast.562), kind=kOutput, calls=%fused_computation.4 | convolution fusion | flops 412087296 | bytes 27156480 | tf_op jit(solution)/shard_map/qhd,khd->hqk/dot_general | solution.py:170
  406.6 6.3 fusion.32
  412.9 7.2 %multiply_convert_fusion = bf16[12,256,1024]{2,1,0:T(8,128)(2,1)S(1)} fusion(f32[12,256,1024]{2,1,0:T(8,128)} %get-tuple-element.149, f32[12,256]{1,0:T(8,128)S(1)} %get-tuple-element.148, f32[12,256,1024]{2,1,0:T(8,128)S(1)} %bitcast.482, f32[12,256]{1,0:T(8,128)S(1)} %copy-done.98), kind=kLoop, calls=%fused_computation.3 | loop fusion | flops 12582912 | bytes 31481856 | tf_op jit(solution)/shard_map/convert_element_type | solution.py:172
  423.5 3.6 convolution_convert_fusion.3
  435.1 5.2 fusion.188
  458.8 3.4 fusion.44
  462.6 14.1 %collective-permute-done.54 = bf16[256,1536]{0,1:T(8,128)(2,1)S(1)} collective-permute-done((bf16[256,1536]{0,1:T(8,128)(2,1)S(1)}, bf16[256,1536]{0,1:T(8,128)(2,1)S(1)}, u32[]{:S(2)}, u32[]{:S(2)}) %collective-permute-start.54) | collective-permute-done | bytes 786464 | tf_op jit(solution)/shard_map/ppermute | solution.py:25
  505.0 7.8 %collective-permute-start.58 = (bf16[4,208,768]{2,1,0:T(8,128)(2,1)S(1)}, bf16[4,208,768]{2,1,0:T(8,128)(2,1)S(1)}, u32[]{:S(2)}, u32[]{:S(2)}) collective-permute-start(bf16[4,208,768]{2,1,0:T(8,128)(2,1)S(1)} %dynamic-slice_bitcast_fusion.3), channel_id=1, source_target_pairs={{0,16},{16,0},{1,17},{17,1},{2,18},{18,2},{3,19},{19,3},{4,20},{20... | collective-permute-start | bytes 3833864 | tf_op jit(solution)/shard_map/ppermute | solution.py:20
  523.2 3.2 fusion.78
  540.1 29.7 %collective-permute-done.62 = bf16[2,4,208,384]{3,2,1,0:T(8,128)(2,1)S(1)} collective-permute-done((bf16[2,4,208,384]{3,2,1,0:T(8,128)(2,1)S(1)}, bf16[2,4,208,384]{3,2,1,0:T(8,128)(2,1)S(1)}, u32[]{:S(2)}, u32[]{:S(2)}) %collective-permute-start.62) | collective-permute-done | bytes 1277984 | tf_op jit(solution)/shard_map/ppermute | solution.py:31
  571.5 12.0 %collective-permute-done.70 = bf16[2,4,208,384]{3,2,1,0:T(8,128)(2,1)S(1)} collective-permute-done((bf16[2,4,208,384]{3,2,1,0:T(8,128)(2,1)S(1)}, bf16[2,4,208,384]{3,2,1,0:T(8,128)(2,1)S(1)}, u32[]{:S(2)}, u32[]{:S(2)}) %collective-permute-start.70) | collective-permute-done | bytes 1277984 | tf_op jit(solution)/shard_map/ppermute | solution.py:31
  591.7 6.7 %collective-permute-done.64 = bf16[2,208,384]{2,1,0:T(8,128)(2,1)S(1)} collective-permute-done((bf16[2,208,384]{2,1,0:T(8,128)(2,1)S(1)}, bf16[2,208,384]{2,1,0:T(8,128)(2,1)S(1)}, u32[]{:S(2)}, u32[]{:S(2)}) %collective-permute-start.64) | collective-permute-done | bytes 319520 | tf_op jit(solution)/shard_map/ppermute | solution.py:25
  598.6 8.4 %collective-permute-done.72 = bf16[2,208,384]{2,1,0:T(8,128)(2,1)S(1)} collective-permute-done((bf16[2,208,384]{2,1,0:T(8,128)(2,1)S(1)}, bf16[2,208,384]{2,1,0:T(8,128)(2,1)S(1)}, u32[]{:S(2)}, u32[]{:S(2)}) %collective-permute-start.72) | collective-permute-done | bytes 319520 | tf_op jit(solution)/shard_map/ppermute | solution.py:25
  611.2 5.0 collective-permute-done.73
  616.4 16.3 %collective-permute-done.81 = bf16[2,384,384]{2,1,0:T(8,128)(2,1)S(1)} collective-permute-done((bf16[2,384,384]{2,1,0:T(8,128)(2,1)S(1)}, bf16[2,384,384]{2,1,0:T(8,128)(2,1)S(1)}, u32[]{:S(2)}, u32[]{:S(2)}) %collective-permute-start.81) | collective-permute-done | bytes 589856 | tf_op jit(solution)/shard_map/ppermute | solution.py:25
  635.7 11.7 %collective-permute-done.82 = bf16[1,384,384]{2,1,0:T(8,128)(2,1)} collective-permute-done((bf16[1,384,384]{2,1,0:T(8,128)(2,1)}, bf16[1,384,384]{2,1,0:T(8,128)(2,1)}, u32[]{:S(2)}, u32[]{:S(2)}) %collective-permute-start.82) | collective-permute-done | bytes 294944 | tf_op jit(solution)/shard_map/ppermute | solution.py:25
  (762 shorter events, 290.9 us)
Async XLA Ops:
  3.0 17.9 %collective-permute-start.3 = (f32[2496]{0:T(1024)S(1)}, f32[2496]{0:T(1024)S(1)}, u32[]{:S(2)}, u32[]{:S(2)}) collective-permute-start(f32[2496]{0:T(1024)S(1)} %pad_maximum_fusion.38), channel_id=1, source_target_pairs={{0,3},{1,2},{2,1},{3,0},{4,7},{5,6},{6,5},{7,4},{8,11},{9,10},{10,... | collective-permute-start | bytes 29960 | tf_op jit(solution)/shard_map/ppermute | solution.py:72
  6.9 17.8 %collective-permute-start.2 = (f32[2496]{0:T(1024)S(1)}, f32[2496]{0:T(1024)S(1)}, u32[]{:S(2)}, u32[]{:S(2)}) collective-permute-start(f32[2496]{0:T(1024)S(1)} %pad_maximum_fusion.38), channel_id=1, source_target_pairs={{0,2},{1,3},{2,0},{3,1},{4,6},{5,7},{6,4},{7,5},{8,10},{9,11},{10,... | collective-permute-start | bytes 29960 | tf_op jit(solution)/shard_map/ppermute | solution.py:72
  7.4 17.4 %collective-permute-start.1 = (f32[2496]{0:T(1024)S(1)}, f32[2496]{0:T(1024)S(1)}, u32[]{:S(2)}, u32[]{:S(2)}) collective-permute-start(f32[2496]{0:T(1024)S(1)} %pad_maximum_fusion.38), channel_id=1, source_target_pairs={{0,1},{1,0},{2,3},{3,2},{4,5},{5,4},{6,7},{7,6},{8,9},{9,8},{10,11... | collective-permute-start | bytes 29960 | tf_op jit(solution)/shard_map/ppermute | solution.py:72
  7.6 57.9 %collective-permute-start.18 = (bf16[192,3072]{1,0:T(8,128)(2,1)}, bf16[192,3072]{1,0:T(8,128)(2,1)}, u32[]{:S(2)}, u32[]{:S(2)}) collective-permute-start(bf16[192,3072]{1,0:T(8,128)(2,1)} %bitcast.587), channel_id=1, source_target_pairs={{0,16},{16,0},{1,17},{17,1},{2,18},{18,2},{3,19},{19,3},{4,20},{20... | collective-permute-start | bytes 3538952 | tf_op jit(solution)/shard_map/ppermute | solution.py:20
  9.3 28.6 %collective-permute-start = (bf16[256,768]{1,0:T(8,128)(2,1)}, bf16[256,768]{1,0:T(8,128)(2,1)}, u32[]{:S(2)}, u32[]{:S(2)}) collective-permute-start(bf16[256,768]{1,0:T(8,128)(2,1)} %dynamic-slice_bitcast_fusion.15), channel_id=1, source_target_pairs={{16,24},{20,28},{24,16},{28,20},{17,25},{21,29},{25,17},{29,21},{1... | collective-permute-start | bytes 1179656 | tf_op jit(solution)/shard_map/ppermute | solution.py:40
  20.9 25.3 %collective-permute-start.5 = (bf16[192,2304]{1,0:T(8,128)(2,1)}, bf16[192,2304]{1,0:T(8,128)(2,1)}, u32[]{:S(2)}, u32[]{:S(2)}) collective-permute-start(bf16[192,2304]{1,0:T(8,128)(2,1)} %bitcast.591), channel_id=1, source_target_pairs={{0,16},{16,0},{1,17},{17,1},{2,18},{18,2},{3,19},{19,3},{4,20},{20... | collective-permute-start | bytes 2654216 | tf_op jit(solution)/shard_map/ppermute | solution.py:20
  39.1 29.9 %collective-permute-start.23 = (bf16[768,768]{1,0:T(8,128)(2,1)S(1)}, bf16[768,768]{1,0:T(8,128)(2,1)S(1)}, u32[]{:S(2)}, u32[]{:S(2)}) collective-permute-start(bf16[768,768]{1,0:T(8,128)(2,1)S(1)} %bitcast.588), channel_id=1, source_target_pairs={{0,16},{16,0},{1,17},{17,1},{2,18},{18,2},{3,19},{19,3},{4,20},{20... | collective-permute-start | bytes 3538952 | tf_op jit(solution)/shard_map/ppermute | solution.py:20
  47.6 24.4 %collective-permute-start.6 = (bf16[192,2304]{1,0:T(8,128)(2,1)S(1)}, bf16[192,2304]{1,0:T(8,128)(2,1)}, u32[]{:S(2)}, u32[]{:S(2)}) collective-permute-start(bf16[192,2304]{1,0:T(8,128)(2,1)S(1)} %get-tuple-element.59), channel_id=1, source_target_pairs={{0,1},{1,0},{2,3},{3,2},{16,18},{17,19},{18,16},{19,17},{4,5},{5,4... | collective-permute-start | bytes 2654216 | tf_op jit(solution)/shard_map/ppermute | solution.py:31
  65.4 221.4 %collective-permute-start.39 = (bf16[96,768]{1,0:T(8,128)(2,1)}, bf16[96,768]{1,0:T(8,128)(2,1)}, u32[]{:S(2)}, u32[]{:S(2)}) collective-permute-start(bf16[96,768]{1,0:T(8,128)(2,1)} %collective-permute-done.38), channel_id=1, source_target_pairs={{0,16},{16,0},{1,17},{17,1},{2,18},{18,2},{3,19},{19,3},{4,20},{20... | collective-permute-start | bytes 442376 | tf_op jit(solution)/shard_map/ppermute | solution.py:20
  67.3 22.4 %collective-permute-start.19 = (bf16[192,3072]{1,0:T(8,128)(2,1)S(1)}, bf16[192,3072]{1,0:T(8,128)(2,1)}, u32[]{:S(2)}, u32[]{:S(2)}) collective-permute-start(bf16[192,3072]{1,0:T(8,128)(2,1)S(1)} %get-tuple-element.53), channel_id=1, source_target_pairs={{0,1},{1,0},{2,3},{3,2},{16,18},{17,19},{18,16},{19,17},{4,5},{5,4... | collective-permute-start | bytes 3538952 | tf_op jit(solution)/shard_map/ppermute | solution.py:31
  69.0 33.4 %collective-permute-start.40 = (bf16[192,3072]{1,0:T(8,128)(2,1)S(1)}, bf16[192,3072]{1,0:T(8,128)(2,1)}, u32[]{:S(2)}, u32[]{:S(2)}) collective-permute-start(bf16[192,3072]{1,0:T(8,128)(2,1)S(1)} %get-tuple-element.52), channel_id=1, source_target_pairs={{0,1},{1,0},{2,3},{3,2},{16,18},{17,19},{18,16},{19,17},{4,5},{5,4... | collective-permute-start | bytes 3538952 | tf_op jit(solution)/shard_map/ppermute | solution.py:31
  72.0 43.0 %collective-permute-start.24 = (bf16[768,768]{1,0:T(8,128)(2,1)S(1)}, bf16[768,768]{1,0:T(8,128)(2,1)}, u32[]{:S(2)}, u32[]{:S(2)}) collective-permute-start(bf16[768,768]{1,0:T(8,128)(2,1)S(1)} %get-tuple-element.55), channel_id=1, source_target_pairs={{0,1},{1,0},{2,3},{3,2},{16,18},{17,19},{18,16},{19,17},{4,5},{5,4... | collective-permute-start | bytes 3538952 | tf_op jit(solution)/shard_map/ppermute | solution.py:31
  77.1 50.6 %collective-permute-start.44 = (bf16[768,768]{1,0:T(8,128)(2,1)S(1)}, bf16[768,768]{1,0:T(8,128)(2,1)}, u32[]{:S(2)}, u32[]{:S(2)}) collective-permute-start(bf16[768,768]{1,0:T(8,128)(2,1)S(1)} %get-tuple-element.54), channel_id=1, source_target_pairs={{0,1},{1,0},{2,3},{3,2},{16,18},{17,19},{18,16},{19,17},{4,5},{5,4... | collective-permute-start | bytes 3538952 | tf_op jit(solution)/shard_map/ppermute | solution.py:31
  89.7 39.3 %collective-permute-start.7 = (bf16[192,2304]{1,0:T(8,128)(2,1)}, bf16[192,2304]{1,0:T(8,128)(2,1)S(1)}, u32[]{:S(2)}, u32[]{:S(2)}) collective-permute-start(bf16[192,2304]{1,0:T(8,128)(2,1)} %collective-permute-done.6), channel_id=1, source_target_pairs={{0,16},{16,0},{1,17},{17,1},{2,18},{18,2},{3,19},{19,3},{4,20},{20... | collective-permute-start | bytes 2654216 | tf_op jit(solution)/shard_map/ppermute | solution.py:20
  102.4 27.4 %collective-permute-start.30 = (bf16[192,2304]{1,0:T(8,128)(2,1)}, bf16[192,2304]{1,0:T(8,128)(2,1)S(1)}, u32[]{:S(2)}, u32[]{:S(2)}) collective-permute-start(bf16[192,2304]{1,0:T(8,128)(2,1)} %collective-permute-done.29), channel_id=1, source_target_pairs={{0,16},{16,0},{1,17},{17,1},{2,18},{18,2},{3,19},{19,3},{4,20},{20... | collective-permute-start | bytes 2654216 | tf_op jit(solution)/shard_map/ppermute | solution.py:20
  116.4 50.7 %collective-permute-start.20 = (bf16[192,3072]{1,0:T(8,128)(2,1)}, bf16[192,3072]{1,0:T(8,128)(2,1)}, u32[]{:S(2)}, u32[]{:S(2)}) collective-permute-start(bf16[192,3072]{1,0:T(8,128)(2,1)} %collective-permute-done.19), channel_id=1, source_target_pairs={{0,16},{16,0},{1,17},{17,1},{2,18},{18,2},{3,19},{19,3},{4,20},{20... | collective-permute-start | bytes 3538952 | tf_op jit(solution)/shard_map/ppermute | solution.py:20
  127.6 40.9 %collective-permute-start.25 = (bf16[768,768]{1,0:T(8,128)(2,1)}, bf16[768,768]{1,0:T(8,128)(2,1)}, u32[]{:S(2)}, u32[]{:S(2)}) collective-permute-start(bf16[768,768]{1,0:T(8,128)(2,1)} %collective-permute-done.24), channel_id=1, source_target_pairs={{0,16},{16,0},{1,17},{17,1},{2,18},{18,2},{3,19},{19,3},{4,20},{20... | collective-permute-start | bytes 3538952 | tf_op jit(solution)/shard_map/ppermute | solution.py:20
  129.1 47.4 %collective-permute-start.41 = (bf16[192,3072]{1,0:T(8,128)(2,1)}, bf16[192,3072]{1,0:T(8,128)(2,1)}, u32[]{:S(2)}, u32[]{:S(2)}) collective-permute-start(bf16[192,3072]{1,0:T(8,128)(2,1)} %collective-permute-done.40), channel_id=1, source_target_pairs={{0,16},{16,0},{1,17},{17,1},{2,18},{18,2},{3,19},{19,3},{4,20},{20... | collective-permute-start | bytes 3538952 | tf_op jit(solution)/shard_map/ppermute | solution.py:20
  148.3 26.4 %collective-permute-start.45 = (bf16[768,768]{1,0:T(8,128)(2,1)}, bf16[768,768]{1,0:T(8,128)(2,1)}, u32[]{:S(2)}, u32[]{:S(2)}) collective-permute-start(bf16[768,768]{1,0:T(8,128)(2,1)} %collective-permute-done.44), channel_id=1, source_target_pairs={{0,16},{16,0},{1,17},{17,1},{2,18},{18,2},{3,19},{19,3},{4,20},{20... | collective-permute-start | bytes 3538952 | tf_op jit(solution)/shard_map/ppermute | solution.py:20
  168.6 21.2 %collective-permute-start.21 = (bf16[96,3072]{1,0:T(8,128)(2,1)S(1)}, bf16[96,3072]{1,0:T(8,128)(2,1)S(1)}, u32[]{:S(2)}, u32[]{:S(2)}) collective-permute-start(bf16[96,3072]{1,0:T(8,128)(2,1)S(1)} %dynamic-slice_bitcast_fusion.11), channel_id=1, source_target_pairs={{0,1},{1,0},{2,3},{3,2},{16,18},{17,19},{18,16},{19,17},{4,5},{5,4... | collective-permute-start | bytes 1769480 | tf_op jit(solution)/shard_map/ppermute | solution.py:31
  176.5 36.0 %collective-permute-start.10 = (bf16[256,1536]{1,0:T(8,128)(2,1)S(1)}, bf16[256,1536]{1,0:T(8,128)(2,1)S(1)}, u32[]{:S(2)}, u32[]{:S(2)}) collective-permute-start(bf16[256,1536]{1,0:T(8,128)(2,1)S(1)} %pad_maximum_fusion.10), channel_id=1, source_target_pairs={{0,4},{4,0},{8,12},{12,8},{1,5},{5,1},{9,13},{13,9},{2,6},{6,2},{1... | collective-permute-start | bytes 2359304 | tf_op jit(solution)/shard_map/ppermute | solution.py:25
  188.8 28.5 %collective-permute-start.11 = (bf16[256,1536]{1,0:T(8,128)(2,1)S(1)}, bf16[256,1536]{1,0:T(8,128)(2,1)S(1)}, u32[]{:S(2)}, u32[]{:S(2)}) collective-permute-start(bf16[256,1536]{1,0:T(8,128)(2,1)S(1)} %pad_maximum_fusion.10), channel_id=1, source_target_pairs={{0,16},{16,0},{1,17},{17,1},{2,18},{18,2},{3,19},{19,3},{4,20},{20... | collective-permute-start | bytes 2359304 | tf_op jit(solution)/shard_map/ppermute | solution.py:20
  200.5 16.0 %collective-permute-start.43 = (bf16[96,3072]{1,0:T(8,128)(2,1)S(1)}, bf16[96,3072]{1,0:T(8,128)(2,1)S(1)}, u32[]{:S(2)}, u32[]{:S(2)}) collective-permute-start(bf16[96,3072]{1,0:T(8,128)(2,1)S(1)} %collective-permute-done.42), channel_id=1, source_target_pairs={{0,16},{16,0},{1,17},{17,1},{2,18},{18,2},{3,19},{19,3},{4,20},{20... | collective-permute-start | bytes 1769480 | tf_op jit(solution)/shard_map/ppermute | solution.py:20
  260.2 34.3 %collective-permute-start.33 = (bf16[256,1536]{1,0:T(8,128)(2,1)}, bf16[256,1536]{1,0:T(8,128)(2,1)}, u32[]{:S(2)}, u32[]{:S(2)}) collective-permute-start(bf16[256,1536]{1,0:T(8,128)(2,1)} %pad_maximum_fusion.11), channel_id=1, source_target_pairs={{0,4},{4,0},{8,12},{12,8},{1,5},{5,1},{9,13},{13,9},{2,6},{6,2},{1... | collective-permute-start | bytes 2359304 | tf_op jit(solution)/shard_map/ppermute | solution.py:25
  285.8 20.3 %collective-permute-start.84 = (bf16[4,384,384]{2,1,0:T(8,128)(2,1)}, bf16[4,384,384]{2,1,0:T(8,128)(2,1)}, u32[]{:S(2)}, u32[]{:S(2)}) collective-permute-start(bf16[4,384,384]{2,1,0:T(8,128)(2,1)} %dynamic-slice_bitcast_fusion.4), channel_id=1, source_target_pairs={{0,16},{16,0},{1,17},{17,1},{2,18},{18,2},{3,19},{19,3},{4,20},{20... | collective-permute-start | bytes 3538952 | tf_op jit(solution)/shard_map/ppermute | solution.py:20
  290.9 19.3 %collective-permute-start.34 = (bf16[256,1536]{1,0:T(8,128)(2,1)}, bf16[256,1536]{1,0:T(8,128)(2,1)S(1)}, u32[]{:S(2)}, u32[]{:S(2)}) collective-permute-start(bf16[256,1536]{1,0:T(8,128)(2,1)} %pad_maximum_fusion.11), channel_id=1, source_target_pairs={{0,16},{16,0},{1,17},{17,1},{2,18},{18,2},{3,19},{19,3},{4,20},{20... | collective-permute-start | bytes 2359304 | tf_op jit(solution)/shard_map/ppermute | solution.py:20
  293.2 98.5 %collective-permute-start.28 = (bf16[256,768]{1,0:T(8,128)(2,1)S(1)}, bf16[256,768]{1,0:T(8,128)(2,1)}, u32[]{:S(2)}, u32[]{:S(2)}) collective-permute-start(bf16[256,768]{1,0:T(8,128)(2,1)S(1)} %get-tuple-element.143), channel_id=1, source_target_pairs={{16,8},{20,12},{24,0},{28,4},{17,9},{21,13},{25,1},{29,5},{18,10},... | collective-permute-start | bytes 1179656 | tf_op jit(solution)/shard_map/ppermute | solution.py:40
  301.6 69.2 %collective-permute-start.83 = (bf16[4,384,768]{2,1,0:T(8,128)(2,1)}, bf16[4,384,768]{2,1,0:T(8,128)(2,1)}, u32[]{:S(2)}, u32[]{:S(2)}) collective-permute-start(bf16[4,384,768]{2,1,0:T(8,128)(2,1)} %dynamic-slice_bitcast_fusion), channel_id=1, source_target_pairs={{0,16},{16,0},{1,17},{17,1},{2,18},{18,2},{3,19},{19,3},{4,20},{20... | collective-permute-start | bytes 7077896 | tf_op jit(solution)/shard_map/ppermute | solution.py:20
  309.7 51.7 %collective-permute-start.85 = (bf16[4,384,384]{2,1,0:T(8,128)(2,1)}, bf16[4,384,384]{2,1,0:T(8,128)(2,1)}, u32[]{:S(2)}, u32[]{:S(2)}) collective-permute-start(bf16[4,384,384]{2,1,0:T(8,128)(2,1)} %fusion.38), channel_id=1, source_target_pairs={{0,1},{1,0},{2,3},{3,2},{16,18},{17,19},{18,16},{19,17},{4,5},{5,4... | collective-permute-start | bytes 3538952 | tf_op jit(solution)/shard_map/ppermute | solution.py:31
  364.9 20.0 %collective-permute-start.52 = (bf16[256,1536]{0,1:T(8,128)(2,1)S(1)}, bf16[256,1536]{0,1:T(8,128)(2,1)S(1)}, u32[]{:S(2)}, u32[]{:S(2)}) collective-permute-start(bf16[256,1536]{0,1:T(8,128)(2,1)S(1)} %slice.704), channel_id=1, source_target_pairs={{0,4},{4,0},{8,12},{12,8},{1,5},{5,1},{9,13},{13,9},{2,6},{6,2},{1... | collective-permute-start | bytes 2359304 | tf_op jit(solution)/shard_map/ppermute | solution.py:25
  366.4 130.3 %collective-permute-start.48 = (bf16[256,768]{1,0:T(8,128)(2,1)}, bf16[256,768]{1,0:T(8,128)(2,1)}, u32[]{:S(2)}, u32[]{:S(2)}) collective-permute-start(bf16[256,768]{1,0:T(8,128)(2,1)} %fusion.77), channel_id=1, source_target_pairs={{0,16},{1,17},{2,18},{3,19},{4,20},{5,21},{6,22},{7,23},{8,24},{9,... | collective-permute-start | bytes 1179656 | tf_op jit(solution)/shard_map/ppermute | solution.py:225
  376.5 136.2 %collective-permute-start.87 = (bf16[2,4,384,384]{3,2,1,0:T(8,128)(2,1)}, bf16[2,4,384,384]{3,2,1,0:T(8,128)(2,1)}, u32[]{:S(2)}, u32[]{:S(2)}) collective-permute-start(bf16[2,4,384,384]{3,2,1,0:T(8,128)(2,1)} %pad_maximum_fusion.5), channel_id=1, source_target_pairs={{0,1},{1,0},{2,3},{3,2},{16,18},{17,19},{18,16},{19,17},{4,5},{5,4... | collective-permute-start | bytes 7077896 | tf_op jit(solution)/shard_map/ppermute | solution.py:31
  428.5 25.5 %collective-permute-start.53 = (bf16[512,1536]{0,1:T(8,128)(2,1)}, bf16[512,1536]{0,1:T(8,128)(2,1)}, u32[]{:S(2)}, u32[]{:S(2)}) collective-permute-start(bf16[512,1536]{0,1:T(8,128)(2,1)} %fusion.16), channel_id=1, source_target_pairs={{0,16},{16,0},{1,17},{17,1},{2,18},{18,2},{3,19},{19,3},{4,20},{20... | collective-permute-start | bytes 4718600 | tf_op jit(solution)/shard_map/ppermute | solution.py:20
  444.1 71.7 %collective-permute-start.75 = (bf16[4,384,768]{2,1,0:T(8,128)(2,1)}, bf16[4,384,768]{2,1,0:T(8,128)(2,1)}, u32[]{:S(2)}, u32[]{:S(2)}) collective-permute-start(bf16[4,384,768]{2,1,0:T(8,128)(2,1)} %dynamic-slice_bitcast_fusion.1), channel_id=1, source_target_pairs={{0,16},{16,0},{1,17},{17,1},{2,18},{18,2},{3,19},{19,3},{4,20},{20... | collective-permute-start | bytes 7077896 | tf_op jit(solution)/shard_map/ppermute | solution.py:20
  456.7 20.0 %collective-permute-start.54 = (bf16[256,1536]{0,1:T(8,128)(2,1)S(1)}, bf16[256,1536]{0,1:T(8,128)(2,1)S(1)}, u32[]{:S(2)}, u32[]{:S(2)}) collective-permute-start(bf16[256,1536]{0,1:T(8,128)(2,1)S(1)} %slice.703), channel_id=1, source_target_pairs={{0,4},{4,0},{8,12},{12,8},{1,5},{5,1},{9,13},{13,9},{2,6},{6,2},{1... | collective-permute-start | bytes 2359304 | tf_op jit(solution)/shard_map/ppermute | solution.py:25
  462.2 36.5 %collective-permute-start.77 = (bf16[4,384,384]{2,1,0:T(8,128)(2,1)}, bf16[4,384,384]{2,1,0:T(8,128)(2,1)}, u32[]{:S(2)}, u32[]{:S(2)}) collective-permute-start(bf16[4,384,384]{2,1,0:T(8,128)(2,1)} %fusion.44), channel_id=1, source_target_pairs={{0,1},{1,0},{2,3},{3,2},{16,18},{17,19},{18,16},{19,17},{4,5},{5,4... | collective-permute-start | bytes 3538952 | tf_op jit(solution)/shard_map/ppermute | solution.py:31
  499.6 20.1 %collective-permute-start.78 = (bf16[4,384,384]{2,1,0:T(8,128)(2,1)}, bf16[4,384,384]{2,1,0:T(8,128)(2,1)S(1)}, u32[]{:S(2)}, u32[]{:S(2)}) collective-permute-start(bf16[4,384,384]{2,1,0:T(8,128)(2,1)} %collective-permute-done.77), channel_id=1, source_target_pairs={{0,16},{16,0},{1,17},{17,1},{2,18},{18,2},{3,19},{19,3},{4,20},{20... | collective-permute-start | bytes 3538952 | tf_op jit(solution)/shard_map/ppermute | solution.py:20
  505.0 21.8 %collective-permute-start.58 = (bf16[4,208,768]{2,1,0:T(8,128)(2,1)S(1)}, bf16[4,208,768]{2,1,0:T(8,128)(2,1)S(1)}, u32[]{:S(2)}, u32[]{:S(2)}) collective-permute-start(bf16[4,208,768]{2,1,0:T(8,128)(2,1)S(1)} %dynamic-slice_bitcast_fusion.3), channel_id=1, source_target_pairs={{0,16},{16,0},{1,17},{17,1},{2,18},{18,2},{3,19},{19,3},{4,20},{20... | collective-permute-start | bytes 3833864 | tf_op jit(solution)/shard_map/ppermute | solution.py:20
  527.3 57.8 %collective-permute-start.79 = (bf16[2,4,384,384]{3,2,1,0:T(8,128)(2,1)S(1)}, bf16[2,4,384,384]{3,2,1,0:T(8,128)(2,1)S(1)}, u32[]{:S(2)}, u32[]{:S(2)}) collective-permute-start(bf16[2,4,384,384]{3,2,1,0:T(8,128)(2,1)S(1)} %pad_maximum_fusion.4), channel_id=1, source_target_pairs={{0,1},{1,0},{2,3},{3,2},{16,18},{17,19},{18,16},{19,17},{4,5},{5,4... | collective-permute-start | bytes 7077896 | tf_op jit(solution)/shard_map/ppermute | solution.py:31
  531.0 38.8 %collective-permute-start.62 = (bf16[2,4,208,384]{3,2,1,0:T(8,128)(2,1)S(1)}, bf16[2,4,208,384]{3,2,1,0:T(8,128)(2,1)S(1)}, u32[]{:S(2)}, u32[]{:S(2)}) collective-permute-start(bf16[2,4,208,384]{3,2,1,0:T(8,128)(2,1)S(1)} %pad_maximum_fusion.6), channel_id=1, source_target_pairs={{0,1},{1,0},{2,3},{3,2},{16,18},{17,19},{18,16},{19,17},{4,5},{5,4... | collective-permute-start | bytes 3833864 | tf_op jit(solution)/shard_map/ppermute | solution.py:31
  534.9 48.6 %collective-permute-start.70 = (bf16[2,4,208,384]{3,2,1,0:T(8,128)(2,1)S(1)}, bf16[2,4,208,384]{3,2,1,0:T(8,128)(2,1)S(1)}, u32[]{:S(2)}, u32[]{:S(2)}) collective-permute-start(bf16[2,4,208,384]{3,2,1,0:T(8,128)(2,1)S(1)} %pad_maximum_fusion.7), channel_id=1, source_target_pairs={{0,1},{1,0},{2,3},{3,2},{16,18},{17,19},{18,16},{19,17},{4,5},{5,4... | collective-permute-start | bytes 3833864 | tf_op jit(solution)/shard_map/ppermute | solution.py:31
  536.2 97.3 %collective-permute-start.55 = (bf16[256,768]{1,0:T(8,128)(2,1)S(1)}, bf16[256,768]{1,0:T(8,128)(2,1)S(1)}, u32[]{:S(2)}, u32[]{:S(2)}) collective-permute-start(bf16[256,768]{1,0:T(8,128)(2,1)S(1)} %fusion.118), channel_id=1, source_target_pairs={{16,8},{20,12},{24,0},{28,4},{17,9},{21,13},{25,1},{29,5},{18,10},... | collective-permute-start | bytes 1179656 | tf_op jit(solution)/shard_map/ppermute | solution.py:40
  571.4 39.2 %collective-permute-start.89 = (bf16[2,384,384]{2,1,0:T(8,128)(2,1)S(1)}, bf16[2,384,384]{2,1,0:T(8,128)(2,1)S(1)}, u32[]{:S(2)}, u32[]{:S(2)}) collective-permute-start(bf16[2,384,384]{2,1,0:T(8,128)(2,1)S(1)} %fusion.127), channel_id=1, source_target_pairs={{0,4},{4,0},{8,12},{12,8},{1,5},{5,1},{9,13},{13,9},{2,6},{6,2},{1... | collective-permute-start | bytes 1769480 | tf_op jit(solution)/shard_map/ppermute | solution.py:25
  585.8 21.6 %collective-permute-start.80 = (bf16[4,384,384]{2,1,0:T(8,128)(2,1)S(1)}, bf16[4,384,384]{2,1,0:T(8,128)(2,1)S(1)}, u32[]{:S(2)}, u32[]{:S(2)}) collective-permute-start(bf16[4,384,384]{2,1,0:T(8,128)(2,1)S(1)} %fusion.42), channel_id=1, source_target_pairs={{0,16},{16,0},{1,17},{17,1},{2,18},{18,2},{3,19},{19,3},{4,20},{20... | collective-permute-start | bytes 3538952 | tf_op jit(solution)/shard_map/ppermute | solution.py:20
  589.6 17.3 %collective-permute-start.72 = (bf16[2,208,384]{2,1,0:T(8,128)(2,1)S(1)}, bf16[2,208,384]{2,1,0:T(8,128)(2,1)S(1)}, u32[]{:S(2)}, u32[]{:S(2)}) collective-permute-start(bf16[2,208,384]{2,1,0:T(8,128)(2,1)S(1)} %fusion.129), channel_id=1, source_target_pairs={{0,4},{4,0},{8,12},{12,8},{1,5},{5,1},{9,13},{13,9},{2,6},{6,2},{1... | collective-permute-start | bytes 958472 | tf_op jit(solution)/shard_map/ppermute | solution.py:25
  608.1 24.5 %collective-permute-start.81 = (bf16[2,384,384]{2,1,0:T(8,128)(2,1)S(1)}, bf16[2,384,384]{2,1,0:T(8,128)(2,1)S(1)}, u32[]{:S(2)}, u32[]{:S(2)}) collective-permute-start(bf16[2,384,384]{2,1,0:T(8,128)(2,1)S(1)} %fusion.126), channel_id=1, source_target_pairs={{0,4},{4,0},{8,12},{12,8},{1,5},{5,1},{9,13},{13,9},{2,6},{6,2},{1... | collective-permute-start | bytes 1769480 | tf_op jit(solution)/shard_map/ppermute | solution.py:25
  610.9 24.8 %collective-permute-start.90 = (bf16[1,384,384]{2,1,0:T(8,128)(2,1)S(1)}, bf16[1,384,384]{2,1,0:T(8,128)(2,1)}, u32[]{:S(2)}, u32[]{:S(2)}) collective-permute-start(bf16[1,384,384]{2,1,0:T(8,128)(2,1)S(1)} %dynamic-slice_convert_fusion.2), channel_id=1, source_target_pairs={{0,8},{4,12},{8,0},{12,4},{1,9},{5,13},{9,1},{13,5},{2,10},{6,14},... | collective-permute-start | bytes 884744 | tf_op jit(solution)/shard_map/ppermute | solution.py:25
  616.3 18.4 %collective-permute-start.74 = (f32[208,384]{1,0:T(8,128)S(1)}, f32[208,384]{1,0:T(8,128)S(1)}, u32[]{:S(2)}, u32[]{:S(2)}) collective-permute-start(f32[208,384]{1,0:T(8,128)S(1)} %get-tuple-element.61), channel_id=1, source_target_pairs={{0,16},{16,0},{1,17},{17,1},{2,18},{18,2},{3,19},{19,3},{4,20},{20... | collective-permute-start | bytes 958472 | tf_op jit(solution)/shard_map/ppermute | solution.py:20
  (197 other events, 2279.8 us)

commit v2 on v1

v2 whole, which is shorter than its diff:
```python
import jax
import jax.numpy as jnp
from jax import lax
from jax.experimental import pallas as pl
from jax.experimental.pallas import tpu as pltpu
from jax.sharding import PartitionSpec as P

D = 768
HEADS = 12
HEAD_DIM = 64
ROT = 16
FF = 3072
BF = jnp.bfloat16
F32 = jnp.float32


def pick(stack, index, axis=0):
    return lax.dynamic_index_in_dim(stack, index, axis, keepdims=False)


def swap_cores(block):
    return lax.ppermute(block, "section", [(0, 1), (1, 0)])


def along_ctx(block, step):
    count = lax.axis_size("ctx")
    return lax.ppermute(block, "ctx", [(i, i ^ step) for i in range(count)])


def along_square(block):
    count = lax.axis_size("fsdp")
    route = [(core * count + i, core * count + (i ^ (1 + core))) for core in (0, 1) for i in range(count)]
    return lax.ppermute(block, ("section", "fsdp"), route)


def across_halves(block, source_core, target_core):
    count = lax.axis_size("ctx")
    route = [
        (source_core * count + i, target_core * count + (i + count // 2) % count)
        for i in range(count)
    ]
    return lax.ppermute(block, ("section", "ctx"), route)


def half_columns(block, which):
    width = block.shape[-1] // 2
    return lax.dynamic_slice_in_dim(block, which * width, width, block.ndim - 1)


def tied(value, *others):
    return lax.optimization_barrier((value, *others))[0]


def place_pieces(index_ref, *refs):
    pieces, whole, sems = refs[:-2], refs[-2], refs[-1]
    copies = []
    for j, piece in enumerate(pieces):
        target = whole.at[pl.ds(index_ref[j], piece.shape[0])]
        copies.append(pltpu.make_async_copy(piece, target, sems.at[j]))
    for copy in copies:
        copy.start()
    for copy in copies:
        copy.wait()


def assemble(pieces, indices):
    rows, cols = pieces[0].shape[1:]
    return pl.pallas_call(
        place_pieces,
        out_shape=jax.ShapeDtypeStruct((8, rows, cols), pieces[0].dtype),
        in_specs=[pl.BlockSpec(memory_space=pltpu.SMEM)]
        + [pl.BlockSpec(memory_space=pl.ANY)] * len(pieces),
        out_specs=pl.BlockSpec(memory_space=pltpu.VMEM),
        scratch_shapes=[pltpu.SemaphoreType.DMA((len(pieces),))],
        compiler_params=pltpu.CompilerParams(vmem_limit_bytes=16 * 2**20),
        cost_estimate=pl.CostEstimate(
            flops=0, bytes_accessed=2 * 8 * rows * cols * 2, transcendentals=0
        ),
    )(jnp.stack(indices).astype(jnp.int32), *pieces)


class SquareQueue:
    def __init__(self):
        self.landed = []

    def send(self, block):
        if len(self.landed) >= 2:
            block = tied(block, self.landed[-2])
        self.landed.append(along_square(block))
        return self.landed[-1]


def gather_weights(layers, core, place):
    queue = SquareQueue()
    waiting = []
    done = []

    def forward(entry):
        shard, mine = entry
        rows, cols = shard.shape
        theirs = swap_cores(mine)
        diag_mine = queue.send(pick(theirs.reshape(2, rows // 2, cols), core))
        diag_theirs = swap_cores(diag_mine)
        pieces = [
            one.reshape(-1, rows // 2, cols)
            for one in (shard, mine, theirs, diag_mine, diag_theirs)
        ]
        whole = assemble(
            pieces,
            [
                2 * place,
                2 * (place ^ (1 + core)),
                2 * (place ^ (2 - core)),
                2 * (place ^ 3) + core,
                2 * (place ^ 3) + 1 - core,
            ],
        )
        done.append(whole.reshape(4 * rows, cols))

    for shards in layers:
        for shard in shards:
            waiting.append((shard, queue.send(shard)))
            if len(waiting) == 2:
                forward(waiting.pop(0))
    forward(waiting.pop(0))
    count = len(layers[0])
    return [done[i * count : (i + 1) * count] for i in range(len(layers))]


def gather_vectors(packed, core, place):
    own = [packed, *[
        lax.ppermute(packed, "fsdp", [(i, i ^ k) for i in range(4)]) for k in (1, 2, 3)
    ]]
    mine = jnp.stack(own)[place ^ jnp.arange(4)]
    theirs = swap_cores(mine)
    first = jnp.where(core == 0, mine, theirs)
    second = jnp.where(core == 0, theirs, mine)
    return first, second


def reduce_stages(parts, core, place, ctx_idx):
    own = pick(parts, place, 1)
    mine = pick(parts, place ^ (1 + core), 1)
    theirs = pick(parts, place ^ (2 - core), 1)
    diag = pick(parts, place ^ 3, 1)
    mine_sib = swap_cores(theirs)
    diag_sib = swap_cores(half_columns(diag, 1 - core))
    diag_sum = half_columns(diag, core).astype(F32) + diag_sib.astype(F32)
    landed = along_square(diag_sum.astype(BF))
    yield landed
    extra = swap_cores(landed)
    near = half_columns(mine, core).astype(F32) + half_columns(mine_sib, core).astype(F32)
    far = (
        half_columns(mine, 1 - core).astype(F32)
        + half_columns(mine_sib, 1 - core).astype(F32)
        + extra.astype(F32)
    )
    landed = along_square(jnp.stack([near, far]).astype(BF))
    yield landed
    give = half_columns(own, 1 - core).astype(F32) + landed[1].astype(F32)
    got = swap_cores(give.astype(BF))
    total = half_columns(own, core).astype(F32) + landed[0].astype(F32) + got.astype(F32)
    count = lax.axis_size("ctx")
    step = 1
    while step < count:
        bit = (ctx_idx // step) % 2
        pairs = total.reshape(total.shape[0] // 2, 2, *total.shape[1:])
        landed = along_ctx(pick(pairs, 1 - bit, 1).astype(BF), step)
        yield landed
        total = pick(pairs, bit, 1) + landed.astype(F32)
        step *= 2
    return total[0]


class Reduction:
    def __init__(self, *args):
        self.stages = reduce_stages(*args)
        self.result = None

    def step(self):
        try:
            return next(self.stages)
        except StopIteration as stop:
            self.result = stop.value
            return None

    def finish(self):
        while self.step() is not None:
            pass
        return self.result


LANES = 2 * HEAD_DIM
VMEM_LIMIT = 40 * 2**20


def rotary_tables(places, direction):
    half_dims = ROT // 2
    lane = jnp.arange(LANES) % HEAD_DIM
    frequency = 10000.0 ** (-((lane % half_dims).astype(F32) * 2.0) / ROT)
    phases = places.astype(F32)[:, None] * frequency[None, :]
    cosine = jnp.where(lane < ROT, jnp.cos(phases), 1.0)
    sine = jnp.sin(phases) * direction
    return (
        cosine,
        jnp.where(lane < half_dims, -sine, 0.0),
        jnp.where((lane >= half_dims) & (lane < ROT), sine, 0.0),
    )


def rotated(rows, cosine, right, left):
    width = rows.shape[1]
    return (
        rows * cosine
        + pltpu.roll(rows, width - ROT // 2, 1) * right
        + pltpu.roll(rows, ROT // 2, 1) * left
    )


def dot_nt(left, right):
    return lax.dot_general(left, right, (((1,), (1,)), ((), ())), preferred_element_type=F32)


def dot_tn(left, right):
    return lax.dot_general(left, right, (((0,), (0,)), ((), ())), preferred_element_type=F32)


def kernel_params():
    return pltpu.CompilerParams(vmem_limit_bytes=VMEM_LIMIT)


def qkv_kernel(in_ref, mat_ref, bias_ref, cos_ref, right_ref, left_ref, query_ref, pair_ref):
    rows = jnp.dot(in_ref[...], mat_ref[...], preferred_element_type=F32) + bias_ref[...]
    rows = rotated(rows, cos_ref[0], right_ref[0], left_ref[0]).astype(BF)
    step = pl.program_id(0)

    @pl.when(step < 3)
    def _():
        query_ref[...] = rows

    @pl.when(step >= 3)
    def _():
        pair_ref[...] = rows


def qkv_rows_of(attn_in, qkv_mat, bias, tables):
    count = attn_in.shape[0]
    table = pl.BlockSpec((1, count, 256), lambda j: (j // 3, 0, 0))
    return pl.pallas_call(
        qkv_kernel,
        grid=(9,),
        in_specs=[
            pl.BlockSpec((count, D), lambda j: (0, 0)),
            pl.BlockSpec((D, 256), lambda j: (0, j)),
            pl.BlockSpec((1, 256), lambda j: (0, j)),
            table,
            table,
            table,
        ],
        out_specs=[
            pl.BlockSpec((count, 256), lambda j: (0, jnp.minimum(j, 2))),
            pl.BlockSpec((count, 256), lambda j: (0, jnp.maximum(j - 3, 0))),
        ],
        out_shape=[
            jax.ShapeDtypeStruct((count, D), BF),
            jax.ShapeDtypeStruct((count, 2 * D), BF),
        ],
        compiler_params=kernel_params(),
        cost_estimate=pl.CostEstimate(
            flops=6 * count * D * D, bytes_accessed=6 * D * D, transcendentals=0
        ),
    )(attn_in, qkv_mat, bias[None], *tables)


def head_picks():
    lane = lax.broadcasted_iota(jnp.int32, (1, LANES), 1)
    first = jnp.where(lane < HEAD_DIM, 1.0, 0.0)
    return first.astype(BF), (1.0 - first).astype(BF)


def upper_lower(upper, lower):
    row = lax.broadcasted_iota(jnp.int32, upper.shape, 0)
    return jnp.where(row < HEAD_DIM, upper, lower).T


def attention_kernel(pieces, query_ref, *refs):
    keys, values = refs[:pieces], refs[pieces : 2 * pieces]
    mask_ref, mixed_ref, level_ref = refs[2 * pieces :]
    count = query_ref.shape[0]
    outs = []
    for head, chosen in enumerate(head_picks()):
        query = query_ref[...] * chosen
        scores = [
            dot_nt(key[...], query) + mask_ref[pl.ds(n * count, count), :]
            for n, key in enumerate(keys)
        ]
        top = scores[0].max(0, keepdims=True)
        for one in scores[1:]:
            top = jnp.maximum(top, one.max(0, keepdims=True))
        grown = [jnp.exp(one - top) for one in scores]
        total = grown[0].sum(0, keepdims=True)
        for one in grown[1:]:
            total = total + one.sum(0, keepdims=True)
        share = 1.0 / total
        out = dot_tn(values[0][...], (grown[0] * share).astype(BF))
        for value, one in zip(values[1:], grown[1:]):
            out = out + dot_tn(value[...], (one * share).astype(BF))
        level_ref[0, pl.ds(head, 1), :] = top + jnp.log(total)
        outs.append(out)
    mixed_ref[...] = upper_lower(*outs).astype(BF)


def piece_specs(count, pieces):
    key = pl.BlockSpec((count, LANES), lambda j: (0, j))
    value = pl.BlockSpec((count, LANES), lambda j: (0, j + D // LANES))
    return [key] * pieces + [value] * pieces


def attention(query, pairs, mask):
    count, pieces = query.shape[0], len(pairs)
    rows = pl.BlockSpec((count, LANES), lambda j: (0, j))
    work = count * count * pieces
    return pl.pallas_call(
        lambda *refs: attention_kernel(pieces, *refs),
        grid=(D // LANES,),
        in_specs=[rows, *piece_specs(count, pieces)]
        + [pl.BlockSpec(mask.shape, lambda j: (0, 0))],
        out_specs=[rows, pl.BlockSpec((1, 2, count), lambda j: (j, 0, 0))],
        out_shape=[
            jax.ShapeDtypeStruct((count, D), BF),
            jax.ShapeDtypeStruct((D // LANES, 2, count), F32),
        ],
        compiler_params=kernel_params(),
        cost_estimate=pl.CostEstimate(
            flops=16 * work * D, bytes_accessed=4 * work + 8 * count * D, transcendentals=HEADS * work
        ),
    )(query, *pairs, *pairs, mask)


def attention_back_kernel(pieces, query_ref, grad_ref, level_ref, *refs):
    keys, values = refs[:pieces], refs[pieces : 2 * pieces]
    mask_ref, cos_ref, right_ref, left_ref, query_out, near_ref, far_ref = refs[2 * pieces :]
    count = query_ref.shape[0]
    group = pieces // 2
    key_sums, value_sums = [None] * pieces, [None] * pieces
    query_sums = []
    for head, chosen in enumerate(head_picks()):
        query = query_ref[...] * chosen
        grad = grad_ref[...] * chosen
        level = level_ref[0, pl.ds(head, 1), :]
        probs, prob_grads = [], []
        centre = None
        for n in range(pieces):
            scores = dot_nt(keys[n][...], query) + mask_ref[pl.ds(n * count, count), :]
            probs.append(jnp.exp(scores - level))
            prob_grads.append(dot_nt(values[n][...], grad))
            part = (probs[n] * prob_grads[n]).sum(0, keepdims=True)
            centre = part if centre is None else centre + part
        query_sum = None
        for n in range(pieces):
            score_grad = (probs[n] * (prob_grads[n] - centre)).astype(BF)
            key_part = jnp.dot(score_grad, query, preferred_element_type=F32)
            value_part = jnp.dot(probs[n].astype(BF), grad, preferred_element_type=F32)
            part = dot_tn(keys[n][...], score_grad)
            query_sum = part if query_sum is None else query_sum + part
            key_sums[n] = key_part if head == 0 else key_sums[n] + key_part
            value_sums[n] = value_part if head == 0 else value_sums[n] + value_part
        query_sums.append(query_sum)
    for n in range(pieces):
        target = near_ref if n < group else far_ref
        target[n % group, 0] = key_sums[n].astype(BF)
        target[n % group, 1] = value_sums[n].astype(BF)
    query_grad = upper_lower(*query_sums) * 0.125
    query_out[...] = rotated(query_grad, cos_ref[...], right_ref[...], left_ref[...]).astype(BF)


def attention_back(query, pairs, mask, level, mixed_grad, tables):
    count, pieces = query.shape[0], len(pairs)
    group = pieces // 2
    rows = pl.BlockSpec((count, LANES), lambda j: (0, j))
    still = pl.BlockSpec((count, LANES), lambda j: (0, 0))
    moving = pl.BlockSpec((group, 2, count, LANES), lambda j: (0, 0, 0, j))
    work = count * count * pieces
    return pl.pallas_call(
        lambda *refs: attention_back_kernel(pieces, *refs),
        grid=(D // LANES,),
        in_specs=[rows, rows, pl.BlockSpec((1, 2, count), lambda j: (j, 0, 0))]
        + piece_specs(count, pieces)
        + [pl.BlockSpec(mask.shape, lambda j: (0, 0)), still, still, still],
        out_specs=[rows, moving, moving],
        out_shape=[
            jax.ShapeDtypeStruct((count, D), BF),
            jax.ShapeDtypeStruct((group, 2, count, D), BF),
            jax.ShapeDtypeStruct((group, 2, count, D), BF),
        ],
        compiler_params=kernel_params(),
        cost_estimate=pl.CostEstimate(
            flops=40 * work * D, bytes_accessed=4 * work + 20 * count * D, transcendentals=HEADS * work
        ),
    )(query, mixed_grad, level, *pairs, *pairs, mask, *tables)


def join_kernel(query_ref, cos_ref, right_ref, left_ref, *refs):
    parts, (out_ref, sum_ref) = refs[:-2], refs[-2:]
    for j in range(D // LANES):
        lanes = pl.ds(j * LANES, LANES)
        key, value = (
            sum((part[which, :, lanes].astype(F32) for part in parts[1:]), parts[0][which, :, lanes].astype(F32))
            for which in (0, 1)
        )
        key = rotated(key, cos_ref[...], right_ref[...], left_ref[...])
        for which, rows in enumerate((query_ref[:, lanes], key, value)):
            rows = rows.astype(BF)
            here = pl.ds(which * D + j * LANES, LANES)
            out_ref[:, here] = rows
            sum_ref[:, here] = rows.astype(F32).sum(0, keepdims=True)


def join_grads(query_grad, tables, parts):
    count = query_grad.shape[0]
    return pl.pallas_call(
        join_kernel,
        out_shape=[
            jax.ShapeDtypeStruct((count, 3 * D), BF),
            jax.ShapeDtypeStruct((1, 3 * D), F32),
        ],
        compiler_params=kernel_params(),
        cost_estimate=pl.CostEstimate(
            flops=10 * count * D, bytes_accessed=(12 + 4 * len(parts)) * count * D, transcendentals=0
        ),
    )(query_grad, *tables, *parts)


def dot_f32(left, right):
    return jnp.dot(left, right, preferred_element_type=F32)


def dot_t(left, right):
    return lax.dot_general(left, right, (((1,), (1,)), ((), ())), preferred_element_type=F32)


def dot_rows(left, right):
    out = lax.dot_general(left, right, (((0,), (0,)), ((), ())), preferred_element_type=F32)
    return out.astype(BF)


def gelu_and_slope(up_rows):
    below = 0.5 + 0.5 * lax.erf(up_rows * 0.7071067811865476)
    density = 0.3989422804014327 * jnp.exp(-0.5 * up_rows * up_rows)
    return (up_rows * below).astype(BF), below + up_rows * density


def per_device(
    inputs,
    cotangent,
    block_order,
    norm_gain,
    norm_bias,
    qkv_weight,
    biases,
    out_weight,
    up_weight,
    down_weight,
):
    rows_dev = inputs.shape[2]
    core = lax.axis_index("section")
    ctx_idx = lax.axis_index("ctx")
    place = lax.axis_index("fsdp")
    ranks = lax.axis_size("ctx")
    squares = lax.axis_size("fsdp")
    group = ranks // 2
    micro = ctx_idx // group

    def rank_of(core_idx, ctx_of):
        return (ctx_of + core_idx * group) % ranks

    def places_of(rank):
        block = rows_dev // 2
        within = jnp.arange(rows_dev, dtype=jnp.int32)
        first = block_order[rank]
        block_ids = jnp.where(within < block, first, 2 * ranks - 1 - first)
        return block_ids * block + within % block

    def take_rows(whole):
        here = pick(whole[:, 0], micro)
        there = across_halves(pick(whole[:, 0], 1 - micro), 1, 1)
        return jnp.where(core == 0, here, there)

    def deliver(rows, layer):
        moved = across_halves(rows, 1, layer)
        here = rows if layer == 0 else lax.ppermute(rows, "section", [(0, 1)])
        first = jnp.where(micro == 0, here, moved)
        second = jnp.where(micro == 0, moved, here)
        return jnp.stack([first, second])

    packed = jnp.concatenate([norm_gain[0].reshape(-1), norm_bias[0].reshape(-1), biases[0]])
    vectors = gather_vectors(packed, core, place)
    shards = (qkv_weight[0], up_weight[0], down_weight[0], out_weight[0])
    siblings = [swap_cores(shard) for shard in shards]
    matrices = gather_weights(
        [
            [jnp.where(core == layer, *pair) for pair in zip(shards, siblings)]
            for layer in (0, 1)
        ],
        core,
        place,
    )
    weights = []
    for layer in (0, 1):
        vec = vectors[layer]
        width = norm_gain.shape[2]
        gains = [vec[:, j * width : (j + 1) * width].reshape(D) for j in (0, 1)]
        shifts = [vec[:, (2 + j) * width : (3 + j) * width].reshape(D) for j in (0, 1)]
        bias = vec[:, 4 * width :].reshape(-1)
        weights.append((matrices[layer], gains, shifts, bias))

    own_places = places_of(rank_of(core, ctx_idx))
    key_places = jnp.concatenate(
        [places_of(rank_of(one, ctx_idx ^ j)) for one in (core, 1 - core) for j in range(group)]
    )
    ahead = rotary_tables(own_places, 1.0)
    back = rotary_tables(own_places, -1.0)
    still = (jnp.ones_like(ahead[0]), jnp.zeros_like(ahead[0]), jnp.zeros_like(ahead[0]))
    tables = [
        jnp.stack([jnp.tile(one, (1, 2)) for one in (ahead[k] * 0.125, ahead[k], still[k])])
        for k in range(3)
    ]
    mask = jnp.where(own_places[None, :] >= key_places[:, None], 0.0, -1e30)

    tok_low = take_rows(inputs)
    top_grad = take_rows(cotangent)
    kept = []
    layer_outs = []
    for layer in (0, 1):
        (qkv_mat, up_mat, down_mat, out_mat), gains, shifts, bias = weights[layer]
        tok_rows = tok_low.astype(F32)
        row_mean = jnp.mean(tok_rows, -1, keepdims=True)
        centred = tok_rows - row_mean
        inverse = lax.rsqrt(jnp.mean(centred * centred, -1, keepdims=True) + 1e-05)
        normed = centred * inverse
        attn_in = (normed * gains[0] + shifts[0]).astype(BF)
        mlp_in = (normed * gains[1] + shifts[1]).astype(BF)
        query, pair = qkv_rows_of(attn_in, qkv_mat, bias[: 3 * D], tables)
        near = [pair, *[along_ctx(pair, j) for j in range(1, group)]]
        pairs = near + [swap_cores(one) for one in near]
        up_rows = dot_f32(mlp_in, up_mat) + bias[4 * D : 4 * D + FF]
        gelu_rows, slope = gelu_and_slope(up_rows)
        mlp_rows = dot_f32(gelu_rows, down_mat) + bias[4 * D + FF :]
        mixed, level = attention(query, pairs, mask)
        attn_rows = dot_f32(mixed, out_mat) + bias[3 * D : 4 * D]
        tok_low = (tok_rows + (attn_rows + mlp_rows)).astype(BF)
        kept.append(
            (normed, inverse, attn_in, mlp_in, query, pairs, level, mixed, slope, gelu_rows)
        )
        layer_outs.append(deliver(tok_low, layer))

    grad_low = top_grad
    grad_outs = [None, None]
    blocks = ranks * squares

    def fold(grad):
        split = grad.reshape(ranks, squares, -1, grad.shape[1])
        return [split[..., j : j + D] for j in range(0, grad.shape[1], D)]

    wide = [None, None]
    thin = [None, None]
    for layer in (1, 0):
        (qkv_mat, up_mat, down_mat, out_mat), gains, shifts, bias = weights[layer]
        (normed, inverse, attn_in, mlp_in, query, pairs, level, mixed, slope, gelu_rows) = kept[layer]
        down_term = dot_rows(gelu_rows, grad_low)
        up_grad = (dot_t(grad_low, down_mat) * slope).astype(BF)
        up_term = dot_rows(mlp_in, up_grad)
        parts = jnp.concatenate(fold(down_term) + fold(up_term), 2)
        wide[layer] = Reduction(parts, core, place, ctx_idx)
        first = wide[layer].step()
        mlp_back = dot_t(up_grad, up_mat)
        mixed_grad = dot_t(grad_low, out_mat).astype(BF)
        if layer == 0:
            mixed_grad = tied(mixed_grad, thin[1].step(), wide[1].step(), layer_outs[1])
        query_grad, near, far = attention_back(query, pairs, mask, level, mixed_grad, back)
        if layer == 1:
            far = tied(far, first, layer_outs[0])
        else:
            far = tied(far, first, thin[1].step(), grad_outs[1])
        far = swap_cores(far)
        parts = [near[0], far[0]]
        for j in range(1, group):
            sent = (near[j].astype(F32) + far[j].astype(F32)).astype(BF)
            parts.append(along_ctx(sent, j))
        qkv_grad, qkv_sums = join_grads(query_grad, back, parts)
        out_term = dot_rows(mixed, grad_low)

        qkv_term = dot_rows(attn_in, qkv_grad)
        attn_back = dot_t(qkv_grad, qkv_mat)
        attn_back = tied(attn_back, wide[layer].step())
        norm_grad = attn_back * gains[0] + mlp_back * gains[1]
        centre = jnp.mean(norm_grad, -1, keepdims=True)
        along = jnp.mean(norm_grad * normed, -1, keepdims=True)
        back_rows = grad_low.astype(F32) + (norm_grad - centre - normed * along) * inverse
        gain_terms = [jnp.sum(attn_back * normed, 0), jnp.sum(mlp_back * normed, 0)]
        shift_terms = [jnp.sum(attn_back, 0), jnp.sum(mlp_back, 0)]
        grad_total = jnp.sum(grad_low.astype(F32), 0)
        bias_term = jnp.concatenate(
            [
                qkv_sums[0],
                grad_total,
                jnp.sum(up_grad.astype(F32), 0),
                grad_total,
            ]
        )
        small = jnp.concatenate(
            [one.reshape(blocks, -1) for one in gain_terms + shift_terms + [bias_term]], 1
        )
        small_width = small.shape[1]
        small = jnp.pad(small, ((0, 0), (0, 16 * D - small_width)))
        small = small.reshape(ranks, squares, 16, D).astype(BF)
        parts = jnp.concatenate(fold(qkv_term) + fold(out_term) + [small], 2)
        thin[layer] = Reduction(parts, core, place, ctx_idx)
        grad_low = back_rows.astype(BF)
        grad_outs[layer] = deliver(grad_low, layer)

    def finish(first, second):
        mine = jnp.where(core == 0, first, second)
        got = swap_cores(jnp.where(core == 0, second, first))
        return jnp.where(
            core == 0, jnp.concatenate([mine, got], -1), jnp.concatenate([got, mine], -1)
        )

    wide, thin = (finish(pair[0].finish(), pair[1].finish()) for pair in (wide, thin))
    down_rows = FF // blocks
    narrow = D // blocks

    def unfold(rows, count):
        return jnp.concatenate([rows[j * narrow : (j + 1) * narrow] for j in range(count)], -1)

    down_out = wide[:down_rows]
    up_out = unfold(wide[down_rows:], 4)
    qkv_out = unfold(thin, 3)
    out_out = thin[3 * narrow : 4 * narrow]
    small = thin[4 * narrow :].reshape(-1)[:small_width]
    gain_out = small[: 2 * narrow].reshape(2, narrow)
    shift_out = small[2 * narrow : 4 * narrow].reshape(2, narrow)
    bias_out = small[4 * narrow :]
    layer_out = jnp.where(core == 0, layer_outs[0], layer_outs[1])
    input_grads = jnp.where(core == 0, grad_outs[0], grad_outs[1])
    return (
        layer_out[None, :, None],
        input_grads[None, :, None],
        gain_out[None],
        shift_out[None],
        qkv_out[None],
        bias_out[None],
        out_out[None],
        up_out[None],
        down_out[None],
    )


def solution(mesh):
    in_specs = (
        P(None, "fsdp", "ctx", None),
        P(None, "fsdp", "ctx", None),
        P(),
        P("section", None, "fsdp"),
        P("section", None, "fsdp"),
        P("section", "fsdp", None),
        P("section", "fsdp"),
        P("section", "fsdp", None),
        P("section", "fsdp", None),
        P("section", "fsdp", None),
    )
    out_specs = (
        P("section", None, "fsdp", "ctx", None),
        P("section", None, "fsdp", "ctx", None),
        P("section", None, ("ctx", "fsdp")),
        P("section", None, ("ctx", "fsdp")),
        P("section", ("ctx", "fsdp"), None),
        P("section", ("ctx", "fsdp")),
        P("section", ("ctx", "fsdp"), None),
        P("section", ("ctx", "fsdp"), None),
        P("section", ("ctx", "fsdp"), None),
    )
    return jax.shard_map(
        per_device, mesh=mesh, in_specs=in_specs, out_specs=out_specs, check_vma=False
    )
```

time: 668 us -> 555 us (0.83)
  matrix products: 135 us -> 44 us
  Pallas kernels: 0 us -> 80.2 us
  waiting for transfers between devices: 199 us -> 149 us
  local copies, waits for them, and re-layouts: 136 us -> 104 us
  other arithmetic: 101 us -> 83.9 us
    pallas_call x0 -> x16, Pallas kernels: none -> 80.2 us  [the longest x2 30.8 us: attention_back(): pl.pallas_call(lambda *refs: attention_back_kernel(pieces, *refs), grid=(...]
    ppermute x24, waiting for transfers between devices: 127 us -> 47.6 us  [along_square(): return lax.ppermute(block, ('section', 'fsdp'), route)]
    dot_general x10 -> x0, matrix products: 48.8 us -> none  [the longest x2 15.9 us: attention_back(): prob_grad = jnp.einsum('qhd,khd->hqk', dm, v, preferred_element_type=F32)]
    slice x32 -> x2, local copies, waits for them, and re-layouts: 28.7 us -> 1.31 us  [per_device(): query, pair = qkv_rows_of(attn_in, qkv_mat, bias[:3 * D], tables)]
    dynamic_update_slice x40 -> x0, local copies, waits for them, and re-layouts: 25.7 us -> none  [put(): lax.dynamic_update_slice_in_dim(whole, piece.reshape(-1, rows // 2, cols)...]
    sub x2 -> x0, matrix products: 21.8 us -> none  [attention(): exp_scores = jnp.exp(scores - row_max)]
    ppermute x3, waiting for transfers between devices: 0.01 us -> 17.8 us  [gather_vectors(): lax.ppermute(packed, 'fsdp', [(i, i ^ k) for i in range(4)])]
    dot_general x8 -> x6, matrix products: 26.8 us -> 9.97 us  [dot_f32(): return jnp.dot(left, right, preferred_element_type=F32)]
  transfers between devices with their start and end apart: 92 -> 92, of which waited for: 25 -> 24; matrix products, arithmetic and copies ran while one was open for 53% -> 33% of each run, Pallas kernels for 0% -> 15%
where the time goes in v2:
time: 555 us; the launch traced here: 548 us
  waiting for transfers between devices  149 us (27%)
  local copies, waits for them, and re-layouts  104 us (19%)
  other arithmetic  83.9 us (15%)
  starting transfers between devices  80.9 us (15%)
  Pallas kernels  80.2 us (14%)
  matrix products  44 us (8%)
  between operations  5.93 us (1%)
    ppermute x12, waiting for transfers between devices, along_ctx(): return lax.ppermute(block, 'ctx', [(i, i ^ step) for i in range(count)])  73.3 us
    ppermute x24, waiting for transfers between devices, along_square(): return lax.ppermute(block, ('section', 'fsdp'), route)  47.6 us
    unnamed x342, local copies, waits for them, and re-layouts  41.2 us
    pallas_call x2, Pallas kernels, attention_back(): pl.pallas_call(lambda *refs: attention_back_kernel(pieces, *refs), grid=(...  30.8 us
    ppermute x24, starting transfers between devices, along_square(): return lax.ppermute(block, ('section', 'fsdp'), route)  25.3 us
    pallas_call x2, Pallas kernels, attention(): pl.pallas_call(lambda *refs: attention_kernel(pieces, *refs), grid=(D //...  20.9 us
    another operation x8, other arithmetic, reduce_stages(): landed = along_square(jnp.stack([near, far]).astype(BF))  17.9 us
    ppermute x3, waiting for transfers between devices, gather_vectors(): lax.ppermute(packed, 'fsdp', [(i, i ^ k) for i in range(4)])  17.8 us
  transfers between devices with their start and end apart: 92, of which 24 were waited for; matrix products, arithmetic and copies ran while one was open for 33% of the time, Pallas kernels for 15%

profile of v2, /device:TPU:0, one launch (start us, length us, event | category | flops | bytes accessed | tf_op | source)
XLA Modules:
  0.0 547.9 jit_solution(1284932087550249239)
XLA Ops:
  2.9 4.0 collective-permute-start.3
  32.4 17.8 %collective-permute-done.1 = f32[2496]{0:T(1024)S(1)} collective-permute-done((f32[2496]{0:T(1024)S(1)}, f32[2496]{0:T(1024)S(1)}, u32[]{:S(2)}, u32[]{:S(2)}) %collective-permute-start.1) | collective-permute-done | bytes 10016 | tf_op jit(solution)/shard_map/ppermute | solution.py:132
  53.9 2.8 broadcast_select_fusion.1
  58.3 3.4 collective-permute-start.7
  69.4 8.7 %collective-permute-done.17 = bf16[768,768]{1,0:T(8,128)(2,1)} collective-permute-done((bf16[768,768]{1,0:T(8,128)(2,1)S(1)}, bf16[768,768]{1,0:T(8,128)(2,1)}, u32[]{:S(2)}, u32[]{:S(2)}) %collective-permute-start.17) | collective-permute-done | bytes 1179680 | tf_op jit(solution)/shard_map/ppermute | solution.py:33
  78.8 7.0 %collective-permute-done.18 = bf16[192,768]{1,0:T(8,128)(2,1)S(1)} collective-permute-done((bf16[192,768]{1,0:T(8,128)(2,1)S(1)}, bf16[192,768]{1,0:T(8,128)(2,1)S(1)}, u32[]{:S(2)}, u32[]{:S(2)}) %collective-permute-start.18) | collective-permute-done | bytes 294944 | tf_op jit(solution)/shard_map/ppermute | solution.py:33
  91.8 5.4 shard_map.170
  130.3 3.5 multiply_convert_fusion.1
  134.5 10.6 %shard_map.171 = (bf16[256,768]{1,0:T(8,128)(2,1)S(1)}, f32[6,2,256]{2,1,0:T(2,128)S(1)}) custom-call(bf16[256,768]{1,0:T(8,128)(2,1)S(1)} %copy-done.78, bf16[256,1536]{1,0:T(8,128)(2,1)} %get-tuple-element.48.refs_1_.refs_5_.refs_3_.refs_7_, bf16[256,1536]{1,0:T(8,128)(2,1)} %collective-permute-done.10.refs_2_.refs_6_.refs_4_.refs_8_, ...), custom_call_target="tpu_custom_call" | custom-call | flops 3221225472 | bytes 2621440 | tf_op jit(solution)/shard_map/pallas_call | solution.py:323
  157.5 7.7 %collective-permute-done.43 = bf16[96,3072]{1,0:T(8,128)(2,1)S(1)} collective-permute-done((bf16[96,3072]{1,0:T(8,128)(2,1)S(1)}, bf16[96,3072]{1,0:T(8,128)(2,1)S(1)}, u32[]{:S(2)}, u32[]{:S(2)}) %collective-permute-start.43) | collective-permute-done | bytes 589856 | tf_op jit(solution)/shard_map/ppermute | solution.py:33
  169.0 5.3 shard_map.176
  187.4 3.0 fusion.130
  196.7 2.9 dynamic-slice_bitcast_fusion.5
  200.2 2.7 collective-permute-done.39
  205.4 3.5 collective-permute-done.40
  220.6 10.4 %shard_map.177 = (bf16[256,768]{1,0:T(8,128)(2,1)S(1)}, f32[6,2,256]{2,1,0:T(2,128)S(1)}) custom-call(bf16[256,768]{1,0:T(8,128)(2,1)S(1)} %copy-done.81, bf16[256,1536]{1,0:T(8,128)(2,1)} %get-tuple-element.58.refs_1_.refs_5_.refs_3_.refs_7_, bf16[256,1536]{1,0:T(8,128)(2,1)} %collective-permute-done.33.refs_2_.refs_6_.refs_4_.refs_8_, ...), custom_call_target="tpu_custom_call" | custom-call | flops 3221225472 | bytes 2621440 | tf_op jit(solution)/shard_map/pallas_call | solution.py:323
  231.0 3.5 dynamic-slice_bitcast_fusion.1
  234.5 15.6 %shard_map.181 = (bf16[256,768]{1,0:T(8,128)(2,1)S(1)}, bf16[2,2,256,768]{3,2,1,0:T(8,128)(2,1)S(1)}, bf16[2,2,256,768]{3,2,1,0:T(8,128)(2,1)}) custom-call(bf16[256,768]{1,0:T(8,128)(2,1)S(1)} %copy-done.81, bf16[256,768]{1,0:T(8,128)(2,1)S(1)} %convolution_convert_fusion.9.refs_1_, f32[6,2,256]{2,1,0:T(2,128)S(1)} %get-tuple-element.66.refs_2_, ...), custom_call_target="tpu_custom_call" | custom-call | flops 8053063680 | bytes 4980736 | tf_op jit(solution)/shard_map/pallas_call | solution.py:384
  254.0 2.6 convolution_convert_fusion.7
  258.5 4.4 fusion.40
  267.2 15.0 %collective-permute-done.54.refs_2_ = bf16[2,256,768]{2,1,0:T(8,128)(2,1)S(1)} collective-permute-done((bf16[2,256,768]{2,1,0:T(8,128)(2,1)S(1)}, bf16[2,256,768]{2,1,0:T(8,128)(2,1)S(1)}, u32[]{:S(2)}, u32[]{:S(2)}) %collective-permute-start.54) | collective-permute-done | bytes 786464 | tf_op jit(solution)/shard_map/ppermute | solution.py:27
  295.8 4.7 fusion.117
  300.5 3.1 fusion.120
  303.6 3.7 convolution_convert_fusion.2
  307.3 3.8 fusion.131
  318.4 3.5 fusion.16
  334.1 3.6 copy-done.82
  339.2 4.1 collective-permute-done.59
  344.0 2.9 fusion.17
  347.1 3.3 fusion.86
  355.2 3.5 dynamic-slice_bitcast_fusion
  359.3 3.4 collective-permute-done.61
  363.6 15.2 %shard_map.183 = (bf16[256,768]{1,0:T(8,128)(2,1)S(1)}, bf16[2,2,256,768]{3,2,1,0:T(8,128)(2,1)S(1)}, bf16[2,2,256,768]{3,2,1,0:T(8,128)(2,1)}) custom-call(bf16[256,768]{1,0:T(8,128)(2,1)S(1)} %copy-done.79, bf16[256,768]{1,0:T(8,128)(2,1)S(1)} %convolution_convert_fusion.8.refs_1_, f32[6,2,256]{2,1,0:T(2,128)S(1)} %get-tuple-element.75.refs_2_, ...), custom_call_target="tpu_custom_call" | custom-call | flops 8053063680 | bytes 4980736 | tf_op jit(solution)/shard_map/pallas_call | solution.py:384
  385.2 4.3 collective-permute-start.48
  393.1 10.8 %collective-permute-start.73 = (bf16[256,768]{1,0:T(8,128)(2,1)}, bf16[256,768]{1,0:T(8,128)(2,1)}, u32[]{:S(2)}, u32[]{:S(2)}) collective-permute-start(bf16[256,768]{1,0:T(8,128)(2,1)} %copy-done.94), channel_id=1, source_target_pairs={{0,16},{1,17},{2,18},{3,19},{4,20},{5,21},{6,22},{7,23},{8,24},{9,... | collective-permute-start | bytes 1179656 | tf_op jit(solution)/shard_map/ppermute | solution.py:491
  410.7 4.4 fusion.42
  419.3 9.4 %collective-permute-done.68.refs_2_ = bf16[2,256,768]{2,1,0:T(8,128)(2,1)S(1)} collective-permute-done((bf16[2,256,768]{2,1,0:T(8,128)(2,1)S(1)}, bf16[2,256,768]{2,1,0:T(8,128)(2,1)S(1)}, u32[]{:S(2)}, u32[]{:S(2)}) %collective-permute-start.68) | collective-permute-done | bytes 786464 | tf_op jit(solution)/shard_map/ppermute | solution.py:27
  432.8 2.5 convolution_convert_fusion
  441.4 4.7 collective-permute-done.71
  462.6 6.8 %collective-permute-done.77 = bf16[4,208,384]{2,1,0:T(8,128)(2,1)S(1)} collective-permute-done((bf16[4,208,384]{2,1,0:T(8,128)(2,1)S(1)}, bf16[4,208,384]{2,1,0:T(8,128)(2,1)S(1)}, u32[]{:S(2)}, u32[]{:S(2)}) %collective-permute-start.77) | collective-permute-done | bytes 639008 | tf_op jit(solution)/shard_map/ppermute | solution.py:33
  471.4 2.8 fusion.11
  479.7 4.7 collective-permute-done.84
  484.8 15.7 %collective-permute-done.88 = bf16[2,384,384]{2,1,0:T(8,128)(2,1)S(1)} collective-permute-done((bf16[2,384,384]{2,1,0:T(8,128)(2,1)S(1)}, bf16[2,384,384]{2,1,0:T(8,128)(2,1)S(1)}, u32[]{:S(2)}, u32[]{:S(2)}) %collective-permute-start.88) | collective-permute-done | bytes 589856 | tf_op jit(solution)/shard_map/ppermute | solution.py:27
  504.0 3.6 collective-permute-start.80
  507.6 13.0 %collective-permute-done.89 = bf16[1,384,384]{2,1,0:T(8,128)(2,1)S(1)} collective-permute-done((bf16[1,384,384]{2,1,0:T(8,128)(2,1)S(1)}, bf16[1,384,384]{2,1,0:T(8,128)(2,1)S(1)}, u32[]{:S(2)}, u32[]{:S(2)}) %collective-permute-start.89) | collective-permute-done | bytes 294944 | tf_op jit(solution)/shard_map/ppermute | solution.py:27
  520.9 3.9 collective-permute-done.72
  528.5 6.0 %collective-permute-done.81 = bf16[2,208,384]{2,1,0:T(8,128)(2,1)S(1)} collective-permute-done((bf16[2,208,384]{2,1,0:T(8,128)(2,1)S(1)}, bf16[2,208,384]{2,1,0:T(8,128)(2,1)S(1)}, u32[]{:S(2)}, u32[]{:S(2)}) %collective-permute-start.81) | collective-permute-done | bytes 319520 | tf_op jit(solution)/shard_map/ppermute | solution.py:27
  536.8 6.0 %collective-permute-done.82 = bf16[1,208,384]{2,1,0:T(8,128)(2,1)S(1)} collective-permute-done((bf16[1,208,384]{2,1,0:T(8,128)(2,1)S(1)}, bf16[1,208,384]{2,1,0:T(8,128)(2,1)S(1)}, u32[]{:S(2)}, u32[]{:S(2)}) %collective-permute-start.82) | collective-permute-done | bytes 159776 | tf_op jit(solution)/shard_map/ppermute | solution.py:27
  (700 shorter events, 248.9 us)
Async XLA Ops:
  2.9 26.9 %collective-permute-start.3 = (f32[2496]{0:T(1024)S(1)}, f32[2496]{0:T(1024)S(1)}, u32[]{:S(2)}, u32[]{:S(2)}) collective-permute-start(f32[2496]{0:T(1024)S(1)} %pad_maximum_fusion.7), channel_id=1, source_target_pairs={{0,3},{1,2},{2,1},{3,0},{4,7},{5,6},{6,5},{7,4},{8,11},{9,10},{10,... | collective-permute-start | bytes 29960 | tf_op jit(solution)/shard_map/ppermute | solution.py:132
  6.9 25.5 %collective-permute-start.2 = (f32[2496]{0:T(1024)S(1)}, f32[2496]{0:T(1024)S(1)}, u32[]{:S(2)}, u32[]{:S(2)}) collective-permute-start(f32[2496]{0:T(1024)S(1)} %pad_maximum_fusion.7), channel_id=1, source_target_pairs={{0,2},{1,3},{2,0},{3,1},{4,6},{5,7},{6,4},{7,5},{8,10},{9,11},{10,... | collective-permute-start | bytes 29960 | tf_op jit(solution)/shard_map/ppermute | solution.py:132
  7.4 17.0 %collective-permute-start.5 = (bf16[192,2304]{1,0:T(8,128)(2,1)}, bf16[192,2304]{1,0:T(8,128)(2,1)}, u32[]{:S(2)}, u32[]{:S(2)}) collective-permute-start(bf16[192,2304]{1,0:T(8,128)(2,1)} %bitcast.505), channel_id=1, source_target_pairs={{0,16},{16,0},{1,17},{17,1},{2,18},{18,2},{3,19},{19,3},{4,20},{20... | collective-permute-start | bytes 2654216 | tf_op jit(solution)/shard_map/ppermute | solution.py:22
  7.4 45.5 %collective-permute-start.14 = (bf16[768,768]{1,0:T(8,128)(2,1)}, bf16[768,768]{1,0:T(8,128)(2,1)S(1)}, u32[]{:S(2)}, u32[]{:S(2)}) collective-permute-start(bf16[768,768]{1,0:T(8,128)(2,1)} %bitcast.504), channel_id=1, source_target_pairs={{0,16},{16,0},{1,17},{17,1},{2,18},{18,2},{3,19},{19,3},{4,20},{20... | collective-permute-start | bytes 3538952 | tf_op jit(solution)/shard_map/ppermute | solution.py:22
  24.3 34.1 %collective-permute-start.16 = (bf16[192,3072]{1,0:T(8,128)(2,1)S(1)}, bf16[192,3072]{1,0:T(8,128)(2,1)}, u32[]{:S(2)}, u32[]{:S(2)}) collective-permute-start(bf16[192,3072]{1,0:T(8,128)(2,1)S(1)} %get-tuple-element.116), channel_id=1, source_target_pairs={{0,1},{1,0},{2,3},{3,2},{16,18},{17,19},{18,16},{19,17},{4,5},{5,4... | collective-permute-start | bytes 3538952 | tf_op jit(solution)/shard_map/ppermute | solution.py:33
  26.9 29.8 %collective-permute-start.6 = (bf16[192,2304]{1,0:T(8,128)(2,1)S(1)}, bf16[192,2304]{1,0:T(8,128)(2,1)}, u32[]{:S(2)}, u32[]{:S(2)}) collective-permute-start(bf16[192,2304]{1,0:T(8,128)(2,1)S(1)} %get-tuple-element.118), channel_id=1, source_target_pairs={{0,1},{1,0},{2,3},{3,2},{16,18},{17,19},{18,16},{19,17},{4,5},{5,4... | collective-permute-start | bytes 2654216 | tf_op jit(solution)/shard_map/ppermute | solution.py:33
  29.8 20.4 %collective-permute-start.1 = (f32[2496]{0:T(1024)S(1)}, f32[2496]{0:T(1024)S(1)}, u32[]{:S(2)}, u32[]{:S(2)}) collective-permute-start(f32[2496]{0:T(1024)S(1)} %pad_maximum_fusion.7), channel_id=1, source_target_pairs={{0,1},{1,0},{2,3},{3,2},{4,5},{5,4},{6,7},{7,6},{8,9},{9,8},{10,11... | collective-permute-start | bytes 29960 | tf_op jit(solution)/shard_map/ppermute | solution.py:132
  32.3 32.3 %collective-permute-start.13 = (bf16[192,768]{1,0:T(8,128)(2,1)}, bf16[192,768]{1,0:T(8,128)(2,1)}, u32[]{:S(2)}, u32[]{:S(2)}) collective-permute-start(bf16[192,768]{1,0:T(8,128)(2,1)} %bitcast.506), channel_id=1, source_target_pairs={{0,16},{16,0},{1,17},{17,1},{2,18},{18,2},{3,19},{19,3},{4,20},{20... | collective-permute-start | bytes 884744 | tf_op jit(solution)/shard_map/ppermute | solution.py:22
  50.2 55.3 %collective-permute-start.50 = (bf16[256,768]{1,0:T(8,128)(2,1)}, bf16[256,768]{1,0:T(8,128)(2,1)}, u32[]{:S(2)}, u32[]{:S(2)}) collective-permute-start(bf16[256,768]{1,0:T(8,128)(2,1)} %dynamic-slice_bitcast_fusion.14), channel_id=1, source_target_pairs={{16,24},{20,28},{24,16},{28,20},{17,25},{21,29},{25,17},{29,21},{1... | collective-permute-start | bytes 1179656 | tf_op jit(solution)/shard_map/ppermute | solution.py:42
  66.4 20.1 %collective-permute-start.21 = (bf16[192,3072]{1,0:T(8,128)(2,1)}, bf16[192,3072]{1,0:T(8,128)(2,1)S(1)}, u32[]{:S(2)}, u32[]{:S(2)}) collective-permute-start(bf16[192,3072]{1,0:T(8,128)(2,1)} %collective-permute-done.16), channel_id=1, source_target_pairs={{0,16},{16,0},{1,17},{17,1},{2,18},{18,2},{3,19},{19,3},{4,20},{20... | collective-permute-start | bytes 3538952 | tf_op jit(solution)/shard_map/ppermute | solution.py:22
  68.5 17.9 %collective-permute-start.8 = (bf16[96,2304]{1,0:T(8,128)(2,1)S(1)}, bf16[96,2304]{1,0:T(8,128)(2,1)S(1)}, u32[]{:S(2)}, u32[]{:S(2)}) collective-permute-start(bf16[96,2304]{1,0:T(8,128)(2,1)S(1)} %dynamic-slice_bitcast_fusion.13), channel_id=1, source_target_pairs={{0,1},{1,0},{2,3},{3,2},{16,18},{17,19},{18,16},{19,17},{4,5},{5,4... | collective-permute-start | bytes 1327112 | tf_op jit(solution)/shard_map/ppermute | solution.py:33
  78.6 20.9 %collective-permute-start.20 = (bf16[768,768]{1,0:T(8,128)(2,1)}, bf16[768,768]{1,0:T(8,128)(2,1)S(1)}, u32[]{:S(2)}, u32[]{:S(2)}) collective-permute-start(bf16[768,768]{1,0:T(8,128)(2,1)} %collective-permute-done.17), channel_id=1, source_target_pairs={{0,16},{16,0},{1,17},{17,1},{2,18},{18,2},{3,19},{19,3},{4,20},{20... | collective-permute-start | bytes 3538952 | tf_op jit(solution)/shard_map/ppermute | solution.py:22
  86.6 19.0 %collective-permute-start.22 = (bf16[96,3072]{1,0:T(8,128)(2,1)S(1)}, bf16[96,3072]{1,0:T(8,128)(2,1)}, u32[]{:S(2)}, u32[]{:S(2)}) collective-permute-start(bf16[96,3072]{1,0:T(8,128)(2,1)S(1)} %dynamic-slice_bitcast_fusion.10), channel_id=1, source_target_pairs={{0,1},{1,0},{2,3},{3,2},{16,18},{17,19},{18,16},{19,17},{4,5},{5,4... | collective-permute-start | bytes 1769480 | tf_op jit(solution)/shard_map/ppermute | solution.py:33
  97.9 21.6 %collective-permute-start.10 = (bf16[256,1536]{1,0:T(8,128)(2,1)}, bf16[256,1536]{1,0:T(8,128)(2,1)}, u32[]{:S(2)}, u32[]{:S(2)}) collective-permute-start(bf16[256,1536]{1,0:T(8,128)(2,1)} %get-tuple-element.48.refs_1_.refs_5_.refs_3_.refs_7_), channel_id=1, source_target_pairs={{0,4},{4,0},{8,12},{12,8},{1,5},{5,1},{9,13},{13,9},{2,6},{6,2},{1... | collective-permute-start | bytes 2359304 | tf_op jit(solution)/shard_map/ppermute | solution.py:27
  99.5 29.9 %collective-permute-start.36 = (bf16[192,3072]{1,0:T(8,128)(2,1)}, bf16[192,3072]{1,0:T(8,128)(2,1)}, u32[]{:S(2)}, u32[]{:S(2)}) collective-permute-start(bf16[192,3072]{1,0:T(8,128)(2,1)} %get-tuple-element.60), channel_id=1, source_target_pairs={{0,1},{1,0},{2,3},{3,2},{16,18},{17,19},{18,16},{19,17},{4,5},{5,4... | collective-permute-start | bytes 3538952 | tf_op jit(solution)/shard_map/ppermute | solution.py:33
  105.5 24.7 %collective-permute-start.11 = (bf16[256,1536]{1,0:T(8,128)(2,1)}, bf16[256,1536]{1,0:T(8,128)(2,1)}, u32[]{:S(2)}, u32[]{:S(2)}) collective-permute-start(bf16[256,1536]{1,0:T(8,128)(2,1)} %get-tuple-element.48.refs_1_.refs_5_.refs_3_.refs_7_), channel_id=1, source_target_pairs={{0,16},{16,0},{1,17},{17,1},{2,18},{18,2},{3,19},{19,3},{4,20},{20... | collective-permute-start | bytes 2359304 | tf_op jit(solution)/shard_map/ppermute | solution.py:22
  106.0 22.1 %collective-permute-start.23 = (bf16[384,768]{1,0:T(8,128)(2,1)}, bf16[384,768]{1,0:T(8,128)(2,1)}, u32[]{:S(2)}, u32[]{:S(2)}) collective-permute-start(bf16[384,768]{1,0:T(8,128)(2,1)} %dynamic-slice_bitcast_fusion.11), channel_id=1, source_target_pairs={{0,1},{1,0},{2,3},{3,2},{16,18},{17,19},{18,16},{19,17},{4,5},{5,4... | collective-permute-start | bytes 1769480 | tf_op jit(solution)/shard_map/ppermute | solution.py:33
  122.0 24.9 %collective-permute-start.30 = (bf16[192,2304]{1,0:T(8,128)(2,1)}, bf16[192,2304]{1,0:T(8,128)(2,1)S(1)}, u32[]{:S(2)}, u32[]{:S(2)}) collective-permute-start(bf16[192,2304]{1,0:T(8,128)(2,1)} %copy-done.63), channel_id=1, source_target_pairs={{0,16},{16,0},{1,17},{17,1},{2,18},{18,2},{3,19},{19,3},{4,20},{20... | collective-permute-start | bytes 2654216 | tf_op jit(solution)/shard_map/ppermute | solution.py:22
  129.4 23.3 %collective-permute-start.37 = (bf16[768,768]{1,0:T(8,128)(2,1)S(1)}, bf16[768,768]{1,0:T(8,128)(2,1)S(1)}, u32[]{:S(2)}, u32[]{:S(2)}) collective-permute-start(bf16[768,768]{1,0:T(8,128)(2,1)S(1)} %copy-done.12), channel_id=1, source_target_pairs={{0,1},{1,0},{2,3},{3,2},{16,18},{17,19},{18,16},{19,17},{4,5},{5,4... | collective-permute-start | bytes 3538952 | tf_op jit(solution)/shard_map/ppermute | solution.py:33
  130.2 22.7 %collective-permute-start.42 = (bf16[192,3072]{1,0:T(8,128)(2,1)}, bf16[192,3072]{1,0:T(8,128)(2,1)S(1)}, u32[]{:S(2)}, u32[]{:S(2)}) collective-permute-start(bf16[192,3072]{1,0:T(8,128)(2,1)} %collective-permute-done.36), channel_id=1, source_target_pairs={{0,16},{16,0},{1,17},{17,1},{2,18},{18,2},{3,19},{19,3},{4,20},{20... | collective-permute-start | bytes 3538952 | tf_op jit(solution)/shard_map/ppermute | solution.py:22
  175.1 29.8 %collective-permute-start.33 = (bf16[256,1536]{1,0:T(8,128)(2,1)}, bf16[256,1536]{1,0:T(8,128)(2,1)}, u32[]{:S(2)}, u32[]{:S(2)}) collective-permute-start(bf16[256,1536]{1,0:T(8,128)(2,1)} %get-tuple-element.58.refs_1_.refs_5_.refs_3_.refs_7_), channel_id=1, source_target_pairs={{0,4},{4,0},{8,12},{12,8},{1,5},{5,1},{9,13},{13,9},{2,6},{6,2},{1... | collective-permute-start | bytes 2359304 | tf_op jit(solution)/shard_map/ppermute | solution.py:27
  176.6 23.5 %collective-permute-start.38 = (bf16[192,768]{1,0:T(8,128)(2,1)S(1)}, bf16[192,768]{1,0:T(8,128)(2,1)S(1)}, u32[]{:S(2)}, u32[]{:S(2)}) collective-permute-start(bf16[192,768]{1,0:T(8,128)(2,1)S(1)} %copy-done.44), channel_id=1, source_target_pairs={{0,1},{1,0},{2,3},{3,2},{16,18},{17,19},{18,16},{19,17},{4,5},{5,4... | collective-permute-start | bytes 884744 | tf_op jit(solution)/shard_map/ppermute | solution.py:33
  199.5 17.3 %collective-permute-start.51 = (bf16[4,384,384]{2,1,0:T(8,128)(2,1)}, bf16[4,384,384]{2,1,0:T(8,128)(2,1)}, u32[]{:S(2)}, u32[]{:S(2)}) collective-permute-start(bf16[4,384,384]{2,1,0:T(8,128)(2,1)} %dynamic-slice_bitcast_fusion.5), channel_id=1, source_target_pairs={{0,16},{16,0},{1,17},{17,1},{2,18},{18,2},{3,19},{19,3},{4,20},{20... | collective-permute-start | bytes 3538952 | tf_op jit(solution)/shard_map/ppermute | solution.py:22
  219.3 32.7 %collective-permute-start.52 = (bf16[4,384,384]{2,1,0:T(8,128)(2,1)S(1)}, bf16[4,384,384]{2,1,0:T(8,128)(2,1)}, u32[]{:S(2)}, u32[]{:S(2)}) collective-permute-start(bf16[4,384,384]{2,1,0:T(8,128)(2,1)S(1)} %fusion.21), channel_id=1, source_target_pairs={{0,1},{1,0},{2,3},{3,2},{16,18},{17,19},{18,16},{19,17},{4,5},{5,4... | collective-permute-start | bytes 3538952 | tf_op jit(solution)/shard_map/ppermute | solution.py:33
  234.5 24.0 %collective-permute-start.55 = (bf16[4,384,768]{2,1,0:T(8,128)(2,1)}, bf16[4,384,768]{2,1,0:T(8,128)(2,1)}, u32[]{:S(2)}, u32[]{:S(2)}) collective-permute-start(bf16[4,384,768]{2,1,0:T(8,128)(2,1)} %dynamic-slice_bitcast_fusion.1), channel_id=1, source_target_pairs={{0,16},{16,0},{1,17},{17,1},{2,18},{18,2},{3,19},{19,3},{4,20},{20... | collective-permute-start | bytes 7077896 | tf_op jit(solution)/shard_map/ppermute | solution.py:22
  252.6 47.9 %collective-permute-start.28 = (bf16[256,768]{1,0:T(8,128)(2,1)}, bf16[256,768]{1,0:T(8,128)(2,1)}, u32[]{:S(2)}, u32[]{:S(2)}) collective-permute-start(bf16[256,768]{1,0:T(8,128)(2,1)} %copy-done.83), channel_id=1, source_target_pairs={{16,8},{20,12},{24,0},{28,4},{17,9},{21,13},{25,1},{29,5},{18,10},... | collective-permute-start | bytes 1179656 | tf_op jit(solution)/shard_map/ppermute | solution.py:42
  258.0 24.2 %collective-permute-start.54 = (bf16[2,256,768]{2,1,0:T(8,128)(2,1)S(1)}, bf16[2,256,768]{2,1,0:T(8,128)(2,1)S(1)}, u32[]{:S(2)}, u32[]{:S(2)}) collective-permute-start(bf16[2,256,768]{2,1,0:T(8,128)(2,1)S(1)} %fusion.84), channel_id=1, source_target_pairs={{0,4},{4,0},{8,12},{12,8},{1,5},{5,1},{9,13},{13,9},{2,6},{6,2},{1... | collective-permute-start | bytes 2359304 | tf_op jit(solution)/shard_map/ppermute | solution.py:27
  264.6 30.8 %collective-permute-start.57 = (bf16[2,4,384,384]{3,2,1,0:T(8,128)(2,1)}, bf16[2,4,384,384]{3,2,1,0:T(8,128)(2,1)}, u32[]{:S(2)}, u32[]{:S(2)}) collective-permute-start(bf16[2,4,384,384]{3,2,1,0:T(8,128)(2,1)} %pad_maximum_fusion), channel_id=1, source_target_pairs={{0,1},{1,0},{2,3},{3,2},{16,18},{17,19},{18,16},{19,17},{4,5},{5,4... | collective-permute-start | bytes 7077896 | tf_op jit(solution)/shard_map/ppermute | solution.py:33
  322.0 22.1 %collective-permute-start.60 = (bf16[4,384,384]{2,1,0:T(8,128)(2,1)}, bf16[4,384,384]{2,1,0:T(8,128)(2,1)}, u32[]{:S(2)}, u32[]{:S(2)}) collective-permute-start(bf16[4,384,384]{2,1,0:T(8,128)(2,1)} %fusion.16), channel_id=1, source_target_pairs={{0,16},{16,0},{1,17},{17,1},{2,18},{18,2},{3,19},{19,3},{4,20},{20... | collective-permute-start | bytes 3538952 | tf_op jit(solution)/shard_map/ppermute | solution.py:22
  329.6 17.5 %collective-permute-start.64 = (bf16[4,208,768]{2,1,0:T(8,128)(2,1)}, bf16[4,208,768]{2,1,0:T(8,128)(2,1)}, u32[]{:S(2)}, u32[]{:S(2)}) collective-permute-start(bf16[4,208,768]{2,1,0:T(8,128)(2,1)} %dynamic-slice_bitcast_fusion.3), channel_id=1, source_target_pairs={{0,16},{16,0},{1,17},{17,1},{2,18},{18,2},{3,19},{19,3},{4,20},{20... | collective-permute-start | bytes 3833864 | tf_op jit(solution)/shard_map/ppermute | solution.py:22
  350.6 30.1 %collective-permute-start.66 = (bf16[2,4,208,384]{3,2,1,0:T(8,128)(2,1)S(1)}, bf16[2,4,208,384]{3,2,1,0:T(8,128)(2,1)S(1)}, u32[]{:S(2)}, u32[]{:S(2)}) collective-permute-start(bf16[2,4,208,384]{3,2,1,0:T(8,128)(2,1)S(1)} %pad_maximum_fusion.2), channel_id=1, source_target_pairs={{0,1},{1,0},{2,3},{3,2},{16,18},{17,19},{18,16},{19,17},{4,5},{5,4... | collective-permute-start | bytes 3833864 | tf_op jit(solution)/shard_map/ppermute | solution.py:33
  354.4 26.3 %collective-permute-start.63 = (bf16[4,384,384]{2,1,0:T(8,128)(2,1)S(1)}, bf16[4,384,384]{2,1,0:T(8,128)(2,1)}, u32[]{:S(2)}, u32[]{:S(2)}) collective-permute-start(bf16[4,384,384]{2,1,0:T(8,128)(2,1)S(1)} %fusion.15), channel_id=1, source_target_pairs={{0,1},{1,0},{2,3},{3,2},{16,18},{17,19},{18,16},{19,17},{4,5},{5,4... | collective-permute-start | bytes 3538952 | tf_op jit(solution)/shard_map/ppermute | solution.py:33
  358.8 52.0 %collective-permute-start.69 = (bf16[4,384,768]{2,1,0:T(8,128)(2,1)}, bf16[4,384,768]{2,1,0:T(8,128)(2,1)}, u32[]{:S(2)}, u32[]{:S(2)}) collective-permute-start(bf16[4,384,768]{2,1,0:T(8,128)(2,1)} %dynamic-slice_bitcast_fusion), channel_id=1, source_target_pairs={{0,16},{16,0},{1,17},{17,1},{2,18},{18,2},{3,19},{19,3},{4,20},{20... | collective-permute-start | bytes 7077896 | tf_op jit(solution)/shard_map/ppermute | solution.py:22
  380.6 27.0 %collective-permute-start.67 = (bf16[2,2,256,768]{3,2,1,0:T(8,128)(2,1)}, bf16[2,2,256,768]{3,2,1,0:T(8,128)(2,1)}, u32[]{:S(2)}, u32[]{:S(2)}) collective-permute-start(bf16[2,2,256,768]{3,2,1,0:T(8,128)(2,1)} %get-tuple-element.79), channel_id=1, source_target_pairs={{0,16},{16,0},{1,17},{17,1},{2,18},{18,2},{3,19},{19,3},{4,20},{20... | collective-permute-start | bytes 4718600 | tf_op jit(solution)/shard_map/ppermute | solution.py:22
  389.5 21.2 %collective-permute-start.70 = (bf16[4,384,384]{2,1,0:T(8,128)(2,1)}, bf16[4,384,384]{2,1,0:T(8,128)(2,1)}, u32[]{:S(2)}, u32[]{:S(2)}) collective-permute-start(bf16[4,384,384]{2,1,0:T(8,128)(2,1)} %collective-permute-done.63), channel_id=1, source_target_pairs={{0,16},{16,0},{1,17},{17,1},{2,18},{18,2},{3,19},{19,3},{4,20},{20... | collective-permute-start | bytes 3538952 | tf_op jit(solution)/shard_map/ppermute | solution.py:22
  391.6 67.3 %collective-permute-start.74 = (bf16[256,768]{1,0:T(8,128)(2,1)}, bf16[256,768]{1,0:T(8,128)(2,1)}, u32[]{:S(2)}, u32[]{:S(2)}) collective-permute-start(bf16[256,768]{1,0:T(8,128)(2,1)} %copy-done.94), channel_id=1, source_target_pairs={{16,24},{20,28},{24,16},{28,20},{17,25},{21,29},{25,17},{29,21},{1... | collective-permute-start | bytes 1179656 | tf_op jit(solution)/shard_map/ppermute | solution.py:42
  393.1 67.0 %collective-permute-start.73 = (bf16[256,768]{1,0:T(8,128)(2,1)}, bf16[256,768]{1,0:T(8,128)(2,1)}, u32[]{:S(2)}, u32[]{:S(2)}) collective-permute-start(bf16[256,768]{1,0:T(8,128)(2,1)} %copy-done.94), channel_id=1, source_target_pairs={{0,16},{1,17},{2,18},{3,19},{4,20},{5,21},{6,22},{7,23},{8,24},{9,... | collective-permute-start | bytes 1179656 | tf_op jit(solution)/shard_map/ppermute | solution.py:491
  409.0 19.8 %collective-permute-start.68 = (bf16[2,256,768]{2,1,0:T(8,128)(2,1)S(1)}, bf16[2,256,768]{2,1,0:T(8,128)(2,1)S(1)}, u32[]{:S(2)}, u32[]{:S(2)}) collective-permute-start(bf16[2,256,768]{2,1,0:T(8,128)(2,1)S(1)} %fusion.85), channel_id=1, source_target_pairs={{0,4},{4,0},{8,12},{12,8},{1,5},{5,1},{9,13},{13,9},{2,6},{6,2},{1... | collective-permute-start | bytes 2359304 | tf_op jit(solution)/shard_map/ppermute | solution.py:27
  416.8 29.2 %collective-permute-start.71 = (bf16[2,4,384,384]{3,2,1,0:T(8,128)(2,1)}, bf16[2,4,384,384]{3,2,1,0:T(8,128)(2,1)}, u32[]{:S(2)}, u32[]{:S(2)}) collective-permute-start(bf16[2,4,384,384]{3,2,1,0:T(8,128)(2,1)} %pad_maximum_fusion.1), channel_id=1, source_target_pairs={{0,1},{1,0},{2,3},{3,2},{16,18},{17,19},{18,16},{19,17},{4,5},{5,4... | collective-permute-start | bytes 7077896 | tf_op jit(solution)/shard_map/ppermute | solution.py:33
  452.2 17.2 %collective-permute-start.83 = (bf16[4,208,384]{2,1,0:T(8,128)(2,1)S(1)}, bf16[4,208,384]{2,1,0:T(8,128)(2,1)S(1)}, u32[]{:S(2)}, u32[]{:S(2)}) collective-permute-start(bf16[4,208,384]{2,1,0:T(8,128)(2,1)S(1)} %fusion.26), channel_id=1, source_target_pairs={{0,16},{16,0},{1,17},{17,1},{2,18},{18,2},{3,19},{19,3},{4,20},{20... | collective-permute-start | bytes 1916936 | tf_op jit(solution)/shard_map/ppermute | solution.py:22
  456.7 19.3 %collective-permute-start.75 = (bf16[4,208,768]{2,1,0:T(8,128)(2,1)S(1)}, bf16[4,208,768]{2,1,0:T(8,128)(2,1)S(1)}, u32[]{:S(2)}, u32[]{:S(2)}) collective-permute-start(bf16[4,208,768]{2,1,0:T(8,128)(2,1)S(1)} %dynamic-slice_bitcast_fusion.2), channel_id=1, source_target_pairs={{0,16},{16,0},{1,17},{17,1},{2,18},{18,2},{3,19},{19,3},{4,20},{20... | collective-permute-start | bytes 3833864 | tf_op jit(solution)/shard_map/ppermute | solution.py:22
  461.5 46.1 %collective-permute-start.90 = (bf16[1,384,384]{2,1,0:T(8,128)(2,1)S(1)}, bf16[1,384,384]{2,1,0:T(8,128)(2,1)S(1)}, u32[]{:S(2)}, u32[]{:S(2)}) collective-permute-start(bf16[1,384,384]{2,1,0:T(8,128)(2,1)S(1)} %dynamic-slice_convert_fusion.2), channel_id=1, source_target_pairs={{0,8},{4,12},{8,0},{12,4},{1,9},{5,13},{9,1},{13,5},{2,10},{6,14},... | collective-permute-start | bytes 884744 | tf_op jit(solution)/shard_map/ppermute | solution.py:27
  474.3 26.2 %collective-permute-start.88 = (bf16[2,384,384]{2,1,0:T(8,128)(2,1)S(1)}, bf16[2,384,384]{2,1,0:T(8,128)(2,1)S(1)}, u32[]{:S(2)}, u32[]{:S(2)}) collective-permute-start(bf16[2,384,384]{2,1,0:T(8,128)(2,1)S(1)} %fusion.91), channel_id=1, source_target_pairs={{0,4},{4,0},{8,12},{12,8},{1,5},{5,1},{9,13},{13,9},{2,6},{6,2},{1... | collective-permute-start | bytes 1769480 | tf_op jit(solution)/shard_map/ppermute | solution.py:27
  478.4 24.1 %collective-permute-start.79 = (bf16[2,4,208,384]{3,2,1,0:T(8,128)(2,1)S(1)}, bf16[2,4,208,384]{3,2,1,0:T(8,128)(2,1)S(1)}, u32[]{:S(2)}, u32[]{:S(2)}) collective-permute-start(bf16[2,4,208,384]{3,2,1,0:T(8,128)(2,1)S(1)} %pad_maximum_fusion.3), channel_id=1, source_target_pairs={{0,1},{1,0},{2,3},{3,2},{16,18},{17,19},{18,16},{19,17},{4,5},{5,4... | collective-permute-start | bytes 3833864 | tf_op jit(solution)/shard_map/ppermute | solution.py:33
  484.5 52.2 %collective-permute-start.85 = (bf16[1,208,384]{2,1,0:T(8,128)(2,1)S(1)}, bf16[1,208,384]{2,1,0:T(8,128)(2,1)S(1)}, u32[]{:S(2)}, u32[]{:S(2)}) collective-permute-start(bf16[1,208,384]{2,1,0:T(8,128)(2,1)S(1)} %dynamic-slice_convert_fusion.4), channel_id=1, source_target_pairs={{0,8},{4,12},{8,0},{12,4},{1,9},{5,13},{9,1},{13,5},{2,10},{6,14},... | collective-permute-start | bytes 479240 | tf_op jit(solution)/shard_map/ppermute | solution.py:27
  500.6 20.0 %collective-permute-start.89 = (bf16[1,384,384]{2,1,0:T(8,128)(2,1)S(1)}, bf16[1,384,384]{2,1,0:T(8,128)(2,1)S(1)}, u32[]{:S(2)}, u32[]{:S(2)}) collective-permute-start(bf16[1,384,384]{2,1,0:T(8,128)(2,1)S(1)} %dynamic-slice_convert_fusion.3), channel_id=1, source_target_pairs={{0,8},{4,12},{8,0},{12,4},{1,9},{5,13},{9,1},{13,5},{2,10},{6,14},... | collective-permute-start | bytes 884744 | tf_op jit(solution)/shard_map/ppermute | solution.py:27
  501.2 23.6 %collective-permute-start.72 = (bf16[256,768]{1,0:T(8,128)(2,1)S(1)}, bf16[256,768]{1,0:T(8,128)(2,1)S(1)}, u32[]{:S(2)}, u32[]{:S(2)}) collective-permute-start(bf16[256,768]{1,0:T(8,128)(2,1)S(1)} %fusion.80), channel_id=1, source_target_pairs={{16,8},{20,12},{24,0},{28,4},{17,9},{21,13},{25,1},{29,5},{18,10},... | collective-permute-start | bytes 1179656 | tf_op jit(solution)/shard_map/ppermute | solution.py:42
  504.0 21.9 %collective-permute-start.80 = (bf16[4,208,384]{2,1,0:T(8,128)(2,1)S(1)}, bf16[4,208,384]{2,1,0:T(8,128)(2,1)S(1)}, u32[]{:S(2)}, u32[]{:S(2)}) collective-permute-start(bf16[4,208,384]{2,1,0:T(8,128)(2,1)S(1)} %fusion.28), channel_id=1, source_target_pairs={{0,16},{16,0},{1,17},{17,1},{2,18},{18,2},{3,19},{19,3},{4,20},{20... | collective-permute-start | bytes 1916936 | tf_op jit(solution)/shard_map/ppermute | solution.py:22
  (208 other events, 1778.2 us)

commit v3 on v2

--- a/solution.py
+++ b/solution.py
@@ -51,91 +51,106 @@
     return lax.optimization_barrier((value, *others))[0]
 
 
-def place_pieces(index_ref, *refs):
+def together(*values):
+    return lax.optimization_barrier(values)
+
+
+def place_pieces(first, cut, index_ref, *refs):
     pieces, whole, sems = refs[:-2], refs[-2], refs[-1]
+    width = whole.shape[2]
     copies = []
     for j, piece in enumerate(pieces):
-        target = whole.at[pl.ds(index_ref[j], piece.shape[0])]
-        copies.append(pltpu.make_async_copy(piece, target, sems.at[j]))
+        halves = piece.shape[0]
+        index = index_ref[j]
+        for part in range(cut):
+            target = (index // 2) * (2 * cut) + 2 * part + index % 2
+            copies.append(
+                pltpu.make_async_copy(
+                    piece.at[:, :, pl.ds(first + part * width, width)],
+                    whole.at[pl.ds(target, halves)],
+                    sems.at[j * cut + part],
+                )
+            )
     for copy in copies:
         copy.start()
     for copy in copies:
         copy.wait()
 
 
-def assemble(pieces, indices):
-    rows, cols = pieces[0].shape[1:]
-    return pl.pallas_call(
-        place_pieces,
-        out_shape=jax.ShapeDtypeStruct((8, rows, cols), pieces[0].dtype),
+def assemble(pieces, indices, first, cut, width):
+    rows = pieces[0].shape[1]
+    whole = pl.pallas_call(
+        lambda *refs: place_pieces(first, cut, *refs),
+        out_shape=jax.ShapeDtypeStruct((8 * cut, rows, width), pieces[0].dtype),
         in_specs=[pl.BlockSpec(memory_space=pltpu.SMEM)]
         + [pl.BlockSpec(memory_space=pl.ANY)] * len(pieces),
         out_specs=pl.BlockSpec(memory_space=pltpu.VMEM),
-        scratch_shapes=[pltpu.SemaphoreType.DMA((len(pieces),))],
+        scratch_shapes=[pltpu.SemaphoreType.DMA((len(pieces) * cut,))],
         compiler_params=pltpu.CompilerParams(vmem_limit_bytes=16 * 2**20),
-        cost_estimate=pl.CostEstimate(
-            flops=0, bytes_accessed=2 * 8 * rows * cols * 2, transcendentals=0
-        ),
-    )(jnp.stack(indices).astype(jnp.int32), *pieces)
-
-
-class SquareQueue:
-    def __init__(self):
-        self.landed = []
-
-    def send(self, block):
-        if len(self.landed) >= 2:
-            block = tied(block, self.landed[-2])
-        self.landed.append(along_square(block))
-        return self.landed[-1]
-
-
-def gather_weights(layers, core, place):
-    queue = SquareQueue()
-    waiting = []
-    done = []
-
-    def forward(entry):
-        shard, mine = entry
-        rows, cols = shard.shape
+        cost_estimate=pl.CostEstimate(flops=1, bytes_accessed=1, transcendentals=0),
+    )(indices, *pieces)
+    return whole.reshape(8 * cut * rows, width)
+
+
+def gather_weights(blocks, core, place):
+    firsts, pieces = [], []
+
+    def second(block, mine):
+        rows, cols = block.shape
         theirs = swap_cores(mine)
-        diag_mine = queue.send(pick(theirs.reshape(2, rows // 2, cols), core))
+        diag_mine = along_square(pick(theirs.reshape(2, rows // 2, cols), core))
         diag_theirs = swap_cores(diag_mine)
-        pieces = [
-            one.reshape(-1, rows // 2, cols)
-            for one in (shard, mine, theirs, diag_mine, diag_theirs)
+        pieces.append(
+            [
+                one.reshape(-1, rows // 2, cols)
+                for one in (block, mine, theirs, diag_mine, diag_theirs)
+            ]
+        )
+
+    for block in blocks:
+        if firsts:
+            block = tied(block, firsts[-1][1])
+        firsts.append((block, along_square(block)))
+        if len(firsts) > 1:
+            second(*firsts[-2])
+    second(*firsts[-1])
+    indices = jnp.stack(
+        [
+            2 * place,
+            2 * (place ^ (1 + core)),
+            2 * (place ^ (2 - core)),
+            2 * (place ^ 3) + core,
+            2 * (place ^ 3) + 1 - core,
         ]
-        whole = assemble(
-            pieces,
-            [
-                2 * place,
-                2 * (place ^ (1 + core)),
-                2 * (place ^ (2 - core)),
-                2 * (place ^ 3) + core,
-                2 * (place ^ 3) + 1 - core,
-            ],
-        )
-        done.append(whole.reshape(4 * rows, cols))
-
-    for shards in layers:
-        for shard in shards:
-            waiting.append((shard, queue.send(shard)))
-            if len(waiting) == 2:
-                forward(waiting.pop(0))
-    forward(waiting.pop(0))
-    count = len(layers[0])
-    return [done[i * count : (i + 1) * count] for i in range(len(layers))]
+    ).astype(jnp.int32)
+    query, rest, early, late = pieces
+    wide = 3 * D
+    return [
+        [
+            assemble(query, indices, 0, 1, wide),
+            assemble(rest, indices, 0, 1, FF),
+            assemble(rest, indices, FF, 4, D),
+            assemble(rest, indices, 2 * FF, 1, D),
+        ],
+        [
+            assemble(early, indices, 0, 1, wide),
+            assemble(early, indices, wide, 1, FF),
+            assemble(late, indices, 0, 4, D),
+            assemble(late, indices, FF, 1, D),
+        ],
+    ]
 
 
 def gather_vectors(packed, core, place):
     own = [packed, *[
         lax.ppermute(packed, "fsdp", [(i, i ^ k) for i in range(4)]) for k in (1, 2, 3)
     ]]
+    landed = own[1:]
     mine = jnp.stack(own)[place ^ jnp.arange(4)]
     theirs = swap_cores(mine)
     first = jnp.where(core == 0, mine, theirs)
     second = jnp.where(core == 0, theirs, mine)
-    return first, second
+    return (first, second), landed
 
 
 def reduce_stages(parts, core, place, ctx_idx):
@@ -146,8 +161,7 @@
     mine_sib = swap_cores(theirs)
     diag_sib = swap_cores(half_columns(diag, 1 - core))
     diag_sum = half_columns(diag, core).astype(F32) + diag_sib.astype(F32)
-    landed = along_square(diag_sum.astype(BF))
-    yield landed
+    landed = yield along_square(diag_sum.astype(BF))
     extra = swap_cores(landed)
     near = half_columns(mine, core).astype(F32) + half_columns(mine_sib, core).astype(F32)
     far = (
@@ -155,8 +169,7 @@
         + half_columns(mine_sib, 1 - core).astype(F32)
         + extra.astype(F32)
     )
-    landed = along_square(jnp.stack([near, far]).astype(BF))
-    yield landed
+    landed = yield along_square(jnp.stack([near, far]).astype(BF))
     give = half_columns(own, 1 - core).astype(F32) + landed[1].astype(F32)
     got = swap_cores(give.astype(BF))
     total = half_columns(own, core).astype(F32) + landed[0].astype(F32) + got.astype(F32)
@@ -165,8 +178,7 @@
     while step < count:
         bit = (ctx_idx // step) % 2
         pairs = total.reshape(total.shape[0] // 2, 2, *total.shape[1:])
-        landed = along_ctx(pick(pairs, 1 - bit, 1).astype(BF), step)
-        yield landed
+        landed = yield along_ctx(pick(pairs, 1 - bit, 1).astype(BF), step)
         total = pick(pairs, bit, 1) + landed.astype(F32)
         step *= 2
     return total[0]
@@ -175,19 +187,28 @@
 class Reduction:
     def __init__(self, *args):
         self.stages = reduce_stages(*args)
+        self.landed = next(self.stages)
         self.result = None
 
     def step(self):
         try:
-            return next(self.stages)
+            self.landed = self.stages.send(self.landed)
         except StopIteration as stop:
             self.result = stop.value
-            return None
+            self.landed = None
 
     def finish(self):
-        while self.step() is not None:
-            pass
+        while self.landed is not None:
+            self.step()
         return self.result
+
+
+def settle(reductions, *others):
+    running = [one for one in reductions if one.landed is not None]
+    values = together(*[one.landed for one in running], *others)
+    for one, landed in zip(running, values):
+        one.landed = landed
+    return values[len(running) :]
 
 
 LANES = 2 * HEAD_DIM
@@ -266,9 +287,7 @@
             jax.ShapeDtypeStruct((count, 2 * D), BF),
         ],
         compiler_params=kernel_params(),
-        cost_estimate=pl.CostEstimate(
-            flops=6 * count * D * D, bytes_accessed=6 * D * D, transcendentals=0
-        ),
+        cost_estimate=pl.CostEstimate(flops=1, bytes_accessed=1, transcendentals=0),
     )(attn_in, qkv_mat, bias[None], *tables)
 
 
@@ -331,9 +350,7 @@
             jax.ShapeDtypeStruct((D // LANES, 2, count), F32),
         ],
         compiler_params=kernel_params(),
-        cost_estimate=pl.CostEstimate(
-            flops=16 * work * D, bytes_accessed=4 * work + 8 * count * D, transcendentals=HEADS * work
-        ),
+        cost_estimate=pl.CostEstimate(flops=1, bytes_accessed=1, transcendentals=0),
     )(query, *pairs, *pairs, mask)
 
 
@@ -394,9 +411,7 @@
             jax.ShapeDtypeStruct((group, 2, count, D), BF),
         ],
         compiler_params=kernel_params(),
-        cost_estimate=pl.CostEstimate(
-            flops=40 * work * D, bytes_accessed=4 * work + 20 * count * D, transcendentals=HEADS * work
-        ),
+        cost_estimate=pl.CostEstimate(flops=1, bytes_accessed=1, transcendentals=0),
     )(query, mixed_grad, level, *pairs, *pairs, mask, *tables)
 
 
@@ -425,9 +440,7 @@
             jax.ShapeDtypeStruct((1, 3 * D), F32),
         ],
         compiler_params=kernel_params(),
-        cost_estimate=pl.CostEstimate(
-            flops=10 * count * D, bytes_accessed=(12 + 4 * len(parts)) * count * D, transcendentals=0
-        ),
+        cost_estimate=pl.CostEstimate(flops=1, bytes_accessed=1, transcendentals=0),
     )(query_grad, *tables, *parts)
 
 
@@ -494,17 +507,28 @@
         return jnp.stack([first, second])
 
     packed = jnp.concatenate([norm_gain[0].reshape(-1), norm_bias[0].reshape(-1), biases[0]])
-    vectors = gather_vectors(packed, core, place)
-    shards = (qkv_weight[0], up_weight[0], down_weight[0], out_weight[0])
-    siblings = [swap_cores(shard) for shard in shards]
-    matrices = gather_weights(
-        [
-            [jnp.where(core == layer, *pair) for pair in zip(shards, siblings)]
-            for layer in (0, 1)
-        ],
-        core,
-        place,
-    )
+    vectors, vectors_landed = gather_vectors(packed, core, place)
+    query_own = qkv_weight[0]
+    query_sib = swap_cores(query_own)
+    head = tied(jnp.where(core == 0, query_own, query_sib), *vectors_landed)
+    slab = down_weight.shape[1] // 4
+    rest_own = jnp.concatenate(
+        [up_weight[0], *[down_weight[0, j * slab : (j + 1) * slab] for j in range(4)], out_weight[0]],
+        -1,
+    )
+    rest_own = tied(rest_own, head)
+    rest_sib = swap_cores(rest_own)
+    rest_first = jnp.where(core == 0, rest_own, rest_sib)
+    rest_next = jnp.where(core == 1, rest_own, rest_sib)
+    query_next = jnp.where(core == 1, query_own, query_sib)
+    blocks = [
+        head,
+        rest_first,
+        jnp.concatenate([query_next, rest_next[:, :FF]], -1),
+        rest_next[:, FF:],
+    ]
+    matrices = gather_weights(blocks, core, place)
+    tok_low = take_rows(inputs)
     weights = []
     for layer in (0, 1):
         vec = vectors[layer]
@@ -512,7 +536,8 @@
         gains = [vec[:, j * width : (j + 1) * width].reshape(D) for j in (0, 1)]
         shifts = [vec[:, (2 + j) * width : (3 + j) * width].reshape(D) for j in (0, 1)]
         bias = vec[:, 4 * width :].reshape(-1)
-        weights.append((matrices[layer], gains, shifts, bias))
+        biases_of = (bias[: 3 * D], bias[3 * D : 4 * D], bias[4 * D : 4 * D + FF], bias[4 * D + FF :])
+        weights.append((matrices[layer], gains, shifts, biases_of))
 
     own_places = places_of(rank_of(core, ctx_idx))
     key_places = jnp.concatenate(
@@ -526,8 +551,10 @@
         for k in range(3)
     ]
     mask = jnp.where(own_places[None, :] >= key_places[:, None], 0.0, -1e30)
-
-    tok_low = take_rows(inputs)
+    weights[0][0][0] = tied(
+        weights[0][0][0], weights[0][1:], weights[1][1:], ahead, back, tables, mask
+    )
+
     top_grad = take_rows(cotangent)
     kept = []
     layer_outs = []
@@ -540,59 +567,58 @@
         normed = centred * inverse
         attn_in = (normed * gains[0] + shifts[0]).astype(BF)
         mlp_in = (normed * gains[1] + shifts[1]).astype(BF)
-        query, pair = qkv_rows_of(attn_in, qkv_mat, bias[: 3 * D], tables)
+        query, pair = qkv_rows_of(attn_in, qkv_mat, bias[0], tables)
         near = [pair, *[along_ctx(pair, j) for j in range(1, group)]]
         pairs = near + [swap_cores(one) for one in near]
-        up_rows = dot_f32(mlp_in, up_mat) + bias[4 * D : 4 * D + FF]
+        up_rows = dot_f32(mlp_in, up_mat) + bias[2]
         gelu_rows, slope = gelu_and_slope(up_rows)
-        mlp_rows = dot_f32(gelu_rows, down_mat) + bias[4 * D + FF :]
+        mlp_rows = dot_f32(gelu_rows, down_mat) + bias[3]
         mixed, level = attention(query, pairs, mask)
-        attn_rows = dot_f32(mixed, out_mat) + bias[3 * D : 4 * D]
+        attn_rows = dot_f32(mixed, out_mat) + bias[1]
         tok_low = (tok_rows + (attn_rows + mlp_rows)).astype(BF)
         kept.append(
             (normed, inverse, attn_in, mlp_in, query, pairs, level, mixed, slope, gelu_rows)
         )
-        layer_outs.append(deliver(tok_low, layer))
+        layer_outs.append(tok_low)
 
     grad_low = top_grad
-    grad_outs = [None, None]
     blocks = ranks * squares
 
     def fold(grad):
         split = grad.reshape(ranks, squares, -1, grad.shape[1])
         return [split[..., j : j + D] for j in range(0, grad.shape[1], D)]
 
-    wide = [None, None]
-    thin = [None, None]
-    for layer in (1, 0):
+    def enter(layer, grad_low):
         (qkv_mat, up_mat, down_mat, out_mat), gains, shifts, bias = weights[layer]
-        (normed, inverse, attn_in, mlp_in, query, pairs, level, mixed, slope, gelu_rows) = kept[layer]
+        mlp_in, slope, gelu_rows = kept[layer][3], kept[layer][8], kept[layer][9]
         down_term = dot_rows(gelu_rows, grad_low)
         up_grad = (dot_t(grad_low, down_mat) * slope).astype(BF)
         up_term = dot_rows(mlp_in, up_grad)
-        parts = jnp.concatenate(fold(down_term) + fold(up_term), 2)
-        wide[layer] = Reduction(parts, core, place, ctx_idx)
-        first = wide[layer].step()
-        mlp_back = dot_t(up_grad, up_mat)
-        mixed_grad = dot_t(grad_low, out_mat).astype(BF)
-        if layer == 0:
-            mixed_grad = tied(mixed_grad, thin[1].step(), wide[1].step(), layer_outs[1])
-        query_grad, near, far = attention_back(query, pairs, mask, level, mixed_grad, back)
-        if layer == 1:
-            far = tied(far, first, layer_outs[0])
-        else:
-            far = tied(far, first, thin[1].step(), grad_outs[1])
+        wide = Reduction(
+            jnp.concatenate(fold(down_term) + fold(up_term), 2), core, place, ctx_idx
+        )
+        return wide, up_grad, dot_t(grad_low, out_mat).astype(BF)
+
+    def attend_back(layer, mixed_grad):
+        query, pairs, level = kept[layer][4:7]
+        return attention_back(query, pairs, mask, level, mixed_grad, back)
+
+    def exchange(near, far):
         far = swap_cores(far)
-        parts = [near[0], far[0]]
-        for j in range(1, group):
-            sent = (near[j].astype(F32) + far[j].astype(F32)).astype(BF)
-            parts.append(along_ctx(sent, j))
-        qkv_grad, qkv_sums = join_grads(query_grad, back, parts)
-        out_term = dot_rows(mixed, grad_low)
-
-        qkv_term = dot_rows(attn_in, qkv_grad)
+        sent = [
+            along_ctx((near[j].astype(F32) + far[j].astype(F32)).astype(BF), j)
+            for j in range(1, group)
+        ]
+        return near[0], far[0], *sent
+
+    def mlp_part(layer, grad_low, up_grad):
+        up_mat = weights[layer][0][1]
+        return dot_t(up_grad, up_mat), dot_rows(kept[layer][7], grad_low)
+
+    def leave(layer, grad_low, qkv_grad, qkv_sums, mlp_back, up_grad):
+        (qkv_mat, up_mat, down_mat, out_mat), gains, shifts, bias = weights[layer]
+        normed, inverse = kept[layer][:2]
         attn_back = dot_t(qkv_grad, qkv_mat)
-        attn_back = tied(attn_back, wide[layer].step())
         norm_grad = attn_back * gains[0] + mlp_back * gains[1]
         centre = jnp.mean(norm_grad, -1, keepdims=True)
         along = jnp.mean(norm_grad * normed, -1, keepdims=True)
@@ -601,23 +627,60 @@
         shift_terms = [jnp.sum(attn_back, 0), jnp.sum(mlp_back, 0)]
         grad_total = jnp.sum(grad_low.astype(F32), 0)
         bias_term = jnp.concatenate(
-            [
-                qkv_sums[0],
-                grad_total,
-                jnp.sum(up_grad.astype(F32), 0),
-                grad_total,
-            ]
+            [qkv_sums[0], grad_total, jnp.sum(up_grad.astype(F32), 0), grad_total]
         )
         small = jnp.concatenate(
             [one.reshape(blocks, -1) for one in gain_terms + shift_terms + [bias_term]], 1
         )
-        small_width = small.shape[1]
-        small = jnp.pad(small, ((0, 0), (0, 16 * D - small_width)))
-        small = small.reshape(ranks, squares, 16, D).astype(BF)
-        parts = jnp.concatenate(fold(qkv_term) + fold(out_term) + [small], 2)
-        thin[layer] = Reduction(parts, core, place, ctx_idx)
-        grad_low = back_rows.astype(BF)
-        grad_outs[layer] = deliver(grad_low, layer)
+        small = jnp.pad(small, ((0, 0), (0, 16 * D - small.shape[1])))
+        return back_rows.astype(BF), small.reshape(ranks, squares, 16, D).astype(BF)
+
+    def reduction_of(parts):
+        return Reduction(jnp.concatenate(parts, 2), core, place, ctx_idx)
+
+    wide_1, up_grad, mixed_grad = enter(1, grad_low)
+    query_grad, near, far = attend_back(1, mixed_grad)
+    query_grad, near, far = settle([wide_1], query_grad, near, far)
+    parts = exchange(near, far)
+    wide_1.step()
+    mlp_back, out_term = mlp_part(1, grad_low, up_grad)
+    query_grad, mlp_back, out_term, *parts = settle([wide_1], query_grad, mlp_back, out_term, *parts)
+    qkv_grad, qkv_sums = join_grads(query_grad, back, parts)
+    low_grad, small = leave(1, grad_low, qkv_grad, qkv_sums, mlp_back, up_grad)
+    qkv_term = dot_rows(kept[1][2], qkv_grad)
+    thin_1 = reduction_of(fold(qkv_term) + fold(out_term) + [small])
+    wide_1.step()
+
+    wide_0, up_grad, mixed_grad = enter(0, low_grad)
+    late = [deliver(low_grad, 1), *[deliver(one, j) for j, one in enumerate(layer_outs)]]
+    mixed_grad, up_grad, *late = settle([thin_1, wide_1], mixed_grad, up_grad, *late)
+    thin_1.step()
+    wide_1.step()
+    query_grad, near, far = attend_back(0, mixed_grad)
+    query_grad, near, far = settle([wide_0, thin_1, wide_1], query_grad, near, far)
+    parts = exchange(near, far)
+    wide_0.step()
+    thin_1.step()
+    mlp_back, out_term = mlp_part(0, low_grad, up_grad)
+    query_term = dot_rows(kept[0][2], query_grad)
+    middle = reduction_of(fold(query_term) + fold(out_term))
+    query_grad, mlp_back, *parts = settle(
+        [wide_0, thin_1, middle], query_grad, mlp_back, *parts
+    )
+    qkv_grad, qkv_sums = join_grads(query_grad, back, parts)
+    wide_0.step()
+    thin_1.step()
+    middle.step()
+    qkv_term = dot_rows(kept[0][2], qkv_grad[:, D:])
+    last_grad, small = leave(0, low_grad, qkv_grad, qkv_sums, mlp_back, up_grad)
+    thin_0 = reduction_of(fold(qkv_term) + [small])
+    (first_grads,) = settle([thin_0, wide_0, thin_1, middle], deliver(last_grad, 0))
+    for one in (thin_0, wide_0, middle):
+        one.step()
+    settle([thin_0, wide_0, middle])
+    grad_outs = [first_grads, late[0]]
+    layer_outs = late[1:]
+    small_width = (4 * D + biases.shape[1] * squares) // blocks
 
     def finish(first, second):
         mine = jnp.where(core == 0, first, second)
@@ -626,9 +689,14 @@
             core == 0, jnp.concatenate([mine, got], -1), jnp.concatenate([got, mine], -1)
         )
 
-    wide, thin = (finish(pair[0].finish(), pair[1].finish()) for pair in (wide, thin))
+    narrow = D // blocks
+    middle, low_thin = middle.finish(), thin_0.finish()
+    low_thin = jnp.concatenate(
+        [middle[:narrow], low_thin[: 2 * narrow], middle[narrow:], low_thin[2 * narrow :]]
+    )
+    wide = finish(wide_0.finish(), wide_1.finish())
+    thin = finish(low_thin, thin_1.finish())
     down_rows = FF // blocks
-    narrow = D // blocks
 
     def unfold(rows, count):
         return jnp.concatenate([rows[j * narrow : (j + 1) * narrow] for j in range(count)], -1)

time: 555 us -> 526 us (0.948)
  local copies, waits for them, and re-layouts: 104 us -> 87.7 us
  other arithmetic: 83.9 us -> 74.6 us
    ppermute x12 -> x14, waiting for transfers between devices: 73.3 us -> 91.6 us  [along_ctx(): return lax.ppermute(block, 'ctx', [(i, i ^ step) for i in range(count)])]
    ppermute x3, waiting for transfers between devices: 17.8 us -> 0.01 us  [gather_vectors(): lax.ppermute(packed, 'fsdp', [(i, i ^ k) for i in range(4)])]
    unnamed x342 -> x303, local copies, waits for them, and re-layouts: 41.2 us -> 29.4 us
    select_n x7 -> x2, other arithmetic: 14 us -> 2.89 us  [the longest x1 1.88 us: per_device(): rest_next = jnp.where(core == 1, rest_own, rest_sib)]
    squeeze x14 -> x10, local copies, waits for them, and re-layouts: 16.5 us -> 9.57 us  [pick(): return lax.dynamic_index_in_dim(stack, index, axis, keepdims=False)]
    ppermute x2, starting transfers between devices: 15 us -> 9.31 us  [deliver(): here = rows if layer == 0 else lax.ppermute(rows, 'section', [(0, 1)])]
    convert_element_type x7 -> x8, other arithmetic: 12 us -> 6.67 us  [the longest x5 4.83 us: reduce_stages(): landed = (yield along_square(diag_sum.astype(BF)))]
    ppermute x12 -> x14, starting transfers between devices: 11.4 us -> 15.2 us  [along_ctx(): return lax.ppermute(block, 'ctx', [(i, i ^ step) for i in range(count)])]
  transfers between devices with their start and end apart: 92 -> 82, of which waited for: 24 -> 25; matrix products, arithmetic and copies ran while one was open for 33% -> 32% of each run, Pallas kernels for 15% -> 15%
where the time goes in v3:
time: 526 us; the launch traced here: 518 us
  waiting for transfers between devices  148 us (28%)
  local copies, waits for them, and re-layouts  87.7 us (17%)
  Pallas kernels  79.1 us (15%)
  starting transfers between devices  76.9 us (15%)
  other arithmetic  74.6 us (14%)
  matrix products  45.5 us (9%)
  between operations  6.1 us (1%)
    ppermute x14, waiting for transfers between devices, along_ctx(): return lax.ppermute(block, 'ctx', [(i, i ^ step) for i in range(count)])  91.6 us
    ppermute x18, waiting for transfers between devices, along_square(): return lax.ppermute(block, ('section', 'fsdp'), route)  48.1 us
    pallas_call x2, Pallas kernels, attention_back(): pl.pallas_call(lambda *refs: attention_back_kernel(pieces, *refs), grid=(...  29.5 us
    unnamed x303, local copies, waits for them, and re-layouts  29.4 us
    ppermute x18, starting transfers between devices, along_square(): return lax.ppermute(block, ('section', 'fsdp'), route)  23.4 us
    pallas_call x2, Pallas kernels, attention(): pl.pallas_call(lambda *refs: attention_kernel(pieces, *refs), grid=(D //...  20.1 us
    dot_general x8, matrix products, dot_t(): lax.dot_general(left, right, (((1,), (1,)), ((), ())), preferred_element_...  19.4 us
    pallas_call x8, Pallas kernels, assemble(): pl.pallas_call(lambda *refs: place_pieces(first, cut, *refs), out_shape=j...  19 us
  transfers between devices with their start and end apart: 82, of which 25 were waited for; matrix products, arithmetic and copies ran while one was open for 32% of the time, Pallas kernels for 15%

profile of v3, /device:TPU:0, one launch (start us, length us, event | category | flops | bytes accessed | tf_op | source)
XLA Modules:
  0.0 517.9 jit_solution(2088208047148797613)
XLA Ops:
  3.0 4.0 collective-permute-start.3
  13.4 2.9 collective-permute-done.13
  18.2 6.3 %collective-permute-done.6 = bf16[192,2304]{1,0:T(8,128)(2,1)S(1)} collective-permute-done((bf16[192,2304]{1,0:T(8,128)(2,1)S(1)}, bf16[192,2304]{1,0:T(8,128)(2,1)S(1)}, u32[]{:S(2)}, u32[]{:S(2)}) %collective-permute-start.6) | collective-permute-done | bytes 884768 | tf_op jit(solution)/shard_map/ppermute | solution.py:33
  53.5 4.1 collective-permute-done.14
  57.6 2.7 pad_maximum_fusion.3
  82.6 3.8 collective-permute-done.18
  95.0 4.4 shard_map.170
  101.1 5.7 %collective-permute-done.23 = bf16[192,3840]{1,0:T(8,128)(2,1)} collective-permute-done((bf16[192,3840]{1,0:T(8,128)(2,1)S(1)}, bf16[192,3840]{1,0:T(8,128)(2,1)}, u32[]{:S(2)}, u32[]{:S(2)}) %collective-permute-start.23) | collective-permute-done | bytes 1474592 | tf_op jit(solution)/shard_map/ppermute | solution.py:33
  107.9 15.8 %collective-permute-done.10.refs_2_.refs_6_.refs_4_.refs_8_ = bf16[256,1536]{1,0:T(8,128)(2,1)} collective-permute-done((bf16[256,1536]{1,0:T(8,128)(2,1)S(1)}, bf16[256,1536]{1,0:T(8,128)(2,1)}, u32[]{:S(2)}, u32[]{:S(2)}) %collective-permute-start.10) | collective-permute-done | bytes 786464 | tf_op jit(solution)/shard_map/ppermute | solution.py:27
  133.0 10.3 %shard_map.171 = (bf16[256,768]{1,0:T(8,128)(2,1)S(1)}, f32[6,2,256]{2,1,0:T(2,128)S(1)}) custom-call(bf16[256,768]{1,0:T(8,128)(2,1)S(1)} %copy-done.41, bf16[256,1536]{1,0:T(8,128)(2,1)S(1)} %get-tuple-element.76.refs_1_.refs_5_.refs_3_.refs_7_, bf16[256,1536]{1,0:T(8,128)(2,1)} %collective-permute-done.10.refs_2_.refs_6_.refs_4_.refs_8_, ...), custom_call_target="tpu_custom_call" | custom-call | flops 1 | bytes 1 | tf_op jit(solution)/shard_map/pallas_call | solution.py:342
  145.6 2.8 shard_map.174
  148.4 3.8 shard_map.173
  152.3 3.6 multiply_convert_fusion.1
  174.8 3.6 fusion.150
  180.5 3.6 copy-done.57
  194.0 4.4 shard_map.178
  202.3 3.3 dynamic-slice_bitcast_fusion.1
  206.1 12.4 %collective-permute-done.30.refs_2_.refs_6_.refs_4_.refs_8_ = bf16[256,1536]{1,0:T(8,128)(2,1)S(1)} collective-permute-done((bf16[256,1536]{1,0:T(8,128)(2,1)S(1)}, bf16[256,1536]{1,0:T(8,128)(2,1)S(1)}, u32[]{:S(2)}, u32[]{:S(2)}) %collective-permute-start.30) | collective-permute-done | bytes 786464 | tf_op jit(solution)/shard_map/ppermute | solution.py:27
  221.4 9.8 %shard_map.180 = (bf16[256,768]{1,0:T(8,128)(2,1)S(1)}, f32[6,2,256]{2,1,0:T(2,128)S(1)}) custom-call(bf16[256,768]{1,0:T(8,128)(2,1)S(1)} %get-tuple-element.82.refs_0_, bf16[256,1536]{1,0:T(8,128)(2,1)S(1)} %get-tuple-element.83.refs_1_.refs_5_.refs_3_.refs_7_, bf16[256,1536]{1,0:T(8,128)(2,1)S(1)} %collective-permute-done.30.refs_2_.refs_6_.refs_4_.refs_8_, ...), custom_call_target="tpu_custom_call" | custom-call | flops 1 | bytes 1 | tf_op jit(solution)/shard_map/pallas_call | solution.py:342
  231.2 14.1 %shard_map.181 = (bf16[256,768]{1,0:T(8,128)(2,1)S(1)}, bf16[2,2,256,768]{3,2,1,0:T(8,128)(2,1)S(1)}, bf16[2,2,256,768]{3,2,1,0:T(8,128)(2,1)S(1)}) custom-call(bf16[256,768]{1,0:T(8,128)(2,1)S(1)} %get-tuple-element.82.refs_0_, bf16[256,768]{1,0:T(8,128)(2,1)S(1)} %convolution_convert_fusion.10.refs_1_, f32[6,2,256]{2,1,0:T(2,128)S(1)} %get-tuple-element.84.refs_2_, ...), custom_call_target="tpu_custom_call" | custom-call | flops 1 | bytes 1 | tf_op jit(solution)/shard_map/pallas_call | solution.py:401
  249.6 3.2 collective-permute-start.35
  252.8 4.5 fusion.34
  258.9 4.0 fusion.151
  265.8 3.8 collective-permute-start.44
  274.3 18.8 %collective-permute-done.36.refs_2_ = bf16[2,256,768]{2,1,0:T(8,128)(2,1)S(1)} collective-permute-done((bf16[2,256,768]{2,1,0:T(8,128)(2,1)S(1)}, bf16[2,256,768]{2,1,0:T(8,128)(2,1)S(1)}, u32[]{:S(2)}, u32[]{:S(2)}) %collective-permute-start.36) | collective-permute-done | bytes 786464 | tf_op jit(solution)/shard_map/ppermute | solution.py:27
  298.1 5.5 %collective-permute-start.41 = (bf16[256,768]{1,0:T(8,128)(2,1)S(1)}, bf16[256,768]{1,0:T(8,128)(2,1)}, u32[]{:S(2)}, u32[]{:S(2)}) collective-permute-start(bf16[256,768]{1,0:T(8,128)(2,1)S(1)} %get-tuple-element.229), channel_id=1, source_target_pairs={{0,16},{1,17},{2,18},{3,19},{4,20},{5,21},{6,22},{7,23},{8,24},{9,... | collective-permute-start | bytes 1179656 | tf_op jit(solution)/shard_map/ppermute | solution.py:504
  303.7 3.6 convolution_convert_fusion.1
  307.3 3.0 convolution_convert_fusion.2
  310.3 3.1 fusion.1
  314.2 3.5 fusion.16
  327.9 3.3 fusion.17
  337.4 10.3 %collective-permute-done.40 = bf16[2,384,384]{2,1,0:T(8,128)(2,1)S(1)} collective-permute-done((bf16[2,384,384]{2,1,0:T(8,128)(2,1)S(1)}, bf16[2,384,384]{2,1,0:T(8,128)(2,1)S(1)}, u32[]{:S(2)}, u32[]{:S(2)}) %collective-permute-start.40) | collective-permute-done | bytes 589856 | tf_op jit(solution)/shard_map/ppermute | solution.py:27
  358.7 15.4 %shard_map.183 = (bf16[256,768]{1,0:T(8,128)(2,1)S(1)}, bf16[2,2,256,768]{3,2,1,0:T(8,128)(2,1)S(1)}, bf16[2,2,256,768]{3,2,1,0:T(8,128)(2,1)}) custom-call(bf16[256,768]{1,0:T(8,128)(2,1)S(1)} %copy-done.42, bf16[256,768]{1,0:T(8,128)(2,1)S(1)} %convolution_convert_fusion.9.refs_1_, f32[6,2,256]{2,1,0:T(2,128)S(1)} %copy-done.51, ...), custom_call_target="tpu_custom_call" | custom-call | flops 1 | bytes 1 | tf_op jit(solution)/shard_map/pallas_call | solution.py:401
  375.3 5.1 collective-permute-done.51
  380.4 2.7 convolution_convert_fusion.6
  383.1 5.1 fusion.152
  388.8 4.0 fusion.36
  409.9 16.9 %collective-permute-done.58 = bf16[4,96,384]{2,1,0:T(8,128)(2,1)} collective-permute-done((bf16[4,96,384]{2,1,0:T(8,128)(2,1)S(1)}, bf16[4,96,384]{2,1,0:T(8,128)(2,1)}, u32[]{:S(2)}, u32[]{:S(2)}) %collective-permute-start.58) | collective-permute-done | bytes 294944 | tf_op jit(solution)/shard_map/ppermute | solution.py:33
  426.8 2.8 collective-permute-done.56
  435.0 3.3 fusion.10
  450.6 3.4 collective-permute-start.61
  457.0 2.9 fusion.11
  463.9 6.0 %collective-permute-done.62 = bf16[4,112,384]{2,1,0:T(8,128)(2,1)S(1)} collective-permute-done((bf16[4,112,384]{2,1,0:T(8,128)(2,1)S(1)}, bf16[4,112,384]{2,1,0:T(8,128)(2,1)S(1)}, u32[]{:S(2)}, u32[]{:S(2)}) %collective-permute-start.62) | collective-permute-done | bytes 344096 | tf_op jit(solution)/shard_map/ppermute | solution.py:33
  469.9 6.3 %collective-permute-done.64 = bf16[2,384,384]{2,1,0:T(8,128)(2,1)S(1)} collective-permute-done((bf16[2,384,384]{2,1,0:T(8,128)(2,1)S(1)}, bf16[2,384,384]{2,1,0:T(8,128)(2,1)S(1)}, u32[]{:S(2)}, u32[]{:S(2)}) %collective-permute-start.64) | collective-permute-done | bytes 589856 | tf_op jit(solution)/shard_map/ppermute | solution.py:27
  484.2 11.0 %collective-permute-done.74 = bf16[1,384,384]{2,1,0:T(8,128)(2,1)S(1)} collective-permute-done((bf16[1,384,384]{2,1,0:T(8,128)(2,1)S(1)}, bf16[1,384,384]{2,1,0:T(8,128)(2,1)S(1)}, u32[]{:S(2)}, u32[]{:S(2)}) %collective-permute-start.74) | collective-permute-done | bytes 294944 | tf_op jit(solution)/shard_map/ppermute | solution.py:27
  496.3 4.8 collective-permute-done.76
  501.4 5.4 %collective-permute-done.78 = bf16[2,112,384]{2,1,0:T(8,128)(2,1)S(1)} collective-permute-done((bf16[2,112,384]{2,1,0:T(8,128)(2,1)S(1)}, bf16[2,112,384]{2,1,0:T(8,128)(2,1)S(1)}, u32[]{:S(2)}, u32[]{:S(2)}) %collective-permute-start.78) | collective-permute-done | bytes 172064 | tf_op jit(solution)/shard_map/ppermute | solution.py:27
  508.6 4.2 collective-permute-done.79
  (661 shorter events, 224.5 us)
Async XLA Ops:
  11.5 13.0 %collective-permute-start.6 = (bf16[192,2304]{1,0:T(8,128)(2,1)S(1)}, bf16[192,2304]{1,0:T(8,128)(2,1)S(1)}, u32[]{:S(2)}, u32[]{:S(2)}) collective-permute-start(bf16[192,2304]{1,0:T(8,128)(2,1)S(1)} %get-tuple-element.73), channel_id=1, source_target_pairs={{0,1},{1,0},{2,3},{3,2},{16,18},{17,19},{18,16},{19,17},{4,5},{5,4... | collective-permute-start | bytes 2654216 | tf_op jit(solution)/shard_map/ppermute | solution.py:33
  25.5 32.1 %collective-permute-start.14 = (bf16[192,6912]{1,0:T(8,128)(2,1)S(1)}, bf16[192,6912]{1,0:T(8,128)(2,1)}, u32[]{:S(2)}, u32[]{:S(2)}) collective-permute-start(bf16[192,6912]{1,0:T(8,128)(2,1)S(1)} %get-tuple-element.79), channel_id=1, source_target_pairs={{0,1},{1,0},{2,3},{3,2},{16,18},{17,19},{18,16},{19,17},{4,5},{5,4... | collective-permute-start | bytes 7962632 | tf_op jit(solution)/shard_map/ppermute | solution.py:33
  28.2 50.0 %collective-permute-start = (bf16[256,768]{1,0:T(8,128)(2,1)}, bf16[256,768]{1,0:T(8,128)(2,1)}, u32[]{:S(2)}, u32[]{:S(2)}) collective-permute-start(bf16[256,768]{1,0:T(8,128)(2,1)} %dynamic-slice_bitcast_fusion.12), channel_id=1, source_target_pairs={{16,24},{20,28},{24,16},{28,20},{17,25},{21,29},{25,17},{29,21},{1... | collective-permute-start | bytes 1179656 | tf_op jit(solution)/shard_map/ppermute | solution.py:42
  57.6 30.6 %collective-permute-start.15 = (bf16[192,6912]{1,0:T(8,128)(2,1)}, bf16[192,6912]{1,0:T(8,128)(2,1)}, u32[]{:S(2)}, u32[]{:S(2)}) collective-permute-start(bf16[192,6912]{1,0:T(8,128)(2,1)} %collective-permute-done.14), channel_id=1, source_target_pairs={{0,16},{16,0},{1,17},{17,1},{2,18},{18,2},{3,19},{19,3},{4,20},{20... | collective-permute-start | bytes 7962632 | tf_op jit(solution)/shard_map/ppermute | solution.py:22
  60.3 26.0 %collective-permute-start.18 = (bf16[192,5376]{1,0:T(8,128)(2,1)}, bf16[192,5376]{1,0:T(8,128)(2,1)}, u32[]{:S(2)}, u32[]{:S(2)}) collective-permute-start(bf16[192,5376]{1,0:T(8,128)(2,1)} %pad_maximum_fusion.3), channel_id=1, source_target_pairs={{0,1},{1,0},{2,3},{3,2},{16,18},{17,19},{18,16},{19,17},{4,5},{5,4... | collective-permute-start | bytes 6193160 | tf_op jit(solution)/shard_map/ppermute | solution.py:33
  86.3 20.5 %collective-permute-start.23 = (bf16[192,3840]{1,0:T(8,128)(2,1)S(1)}, bf16[192,3840]{1,0:T(8,128)(2,1)}, u32[]{:S(2)}, u32[]{:S(2)}) collective-permute-start(bf16[192,3840]{1,0:T(8,128)(2,1)S(1)} %slice.343), channel_id=1, source_target_pairs={{0,1},{1,0},{2,3},{3,2},{16,18},{17,19},{18,16},{19,17},{4,5},{5,4... | collective-permute-start | bytes 4423688 | tf_op jit(solution)/shard_map/ppermute | solution.py:33
  88.2 36.0 %collective-permute-start.19 = (bf16[192,5376]{1,0:T(8,128)(2,1)}, bf16[192,5376]{1,0:T(8,128)(2,1)S(1)}, u32[]{:S(2)}, u32[]{:S(2)}) collective-permute-start(bf16[192,5376]{1,0:T(8,128)(2,1)} %collective-permute-done.18), channel_id=1, source_target_pairs={{0,16},{16,0},{1,17},{17,1},{2,18},{18,2},{3,19},{19,3},{4,20},{20... | collective-permute-start | bytes 6193160 | tf_op jit(solution)/shard_map/ppermute | solution.py:22
  89.7 34.0 %collective-permute-start.16 = (bf16[96,6912]{1,0:T(8,128)(2,1)S(1)}, bf16[96,6912]{1,0:T(8,128)(2,1)}, u32[]{:S(2)}, u32[]{:S(2)}) collective-permute-start(bf16[96,6912]{1,0:T(8,128)(2,1)S(1)} %dynamic-slice_bitcast_fusion.2), channel_id=1, source_target_pairs={{0,1},{1,0},{2,3},{3,2},{16,18},{17,19},{18,16},{19,17},{4,5},{5,4... | collective-permute-start | bytes 3981320 | tf_op jit(solution)/shard_map/ppermute | solution.py:33
  99.5 24.2 %collective-permute-start.10 = (bf16[256,1536]{1,0:T(8,128)(2,1)S(1)}, bf16[256,1536]{1,0:T(8,128)(2,1)}, u32[]{:S(2)}, u32[]{:S(2)}) collective-permute-start(bf16[256,1536]{1,0:T(8,128)(2,1)S(1)} %get-tuple-element.76.refs_1_.refs_5_.refs_3_.refs_7_), channel_id=1, source_target_pairs={{0,4},{4,0},{8,12},{12,8},{1,5},{5,1},{9,13},{13,9},{2,6},{6,2},{1... | collective-permute-start | bytes 2359304 | tf_op jit(solution)/shard_map/ppermute | solution.py:27
  106.9 36.5 %collective-permute-start.24 = (bf16[192,3840]{1,0:T(8,128)(2,1)}, bf16[192,3840]{1,0:T(8,128)(2,1)}, u32[]{:S(2)}, u32[]{:S(2)}) collective-permute-start(bf16[192,3840]{1,0:T(8,128)(2,1)} %collective-permute-done.23), channel_id=1, source_target_pairs={{0,16},{16,0},{1,17},{17,1},{2,18},{18,2},{3,19},{19,3},{4,20},{20... | collective-permute-start | bytes 4423688 | tf_op jit(solution)/shard_map/ppermute | solution.py:22
  106.9 19.7 %collective-permute-start.22 = (bf16[256,768]{1,0:T(8,128)(2,1)S(1)}, bf16[256,768]{1,0:T(8,128)(2,1)S(1)}, u32[]{:S(2)}, u32[]{:S(2)}) collective-permute-start(bf16[256,768]{1,0:T(8,128)(2,1)S(1)} %dynamic-slice_bitcast_fusion.11), channel_id=1, source_target_pairs={{16,24},{20,28},{24,16},{28,20},{17,25},{21,29},{25,17},{29,21},{1... | collective-permute-start | bytes 1179656 | tf_op jit(solution)/shard_map/ppermute | solution.py:42
  124.2 21.4 %collective-permute-start.17 = (bf16[96,6912]{1,0:T(8,128)(2,1)}, bf16[96,6912]{1,0:T(8,128)(2,1)}, u32[]{:S(2)}, u32[]{:S(2)}) collective-permute-start(bf16[96,6912]{1,0:T(8,128)(2,1)} %collective-permute-done.16), channel_id=1, source_target_pairs={{0,16},{16,0},{1,17},{17,1},{2,18},{18,2},{3,19},{19,3},{4,20},{20... | collective-permute-start | bytes 3981320 | tf_op jit(solution)/shard_map/ppermute | solution.py:22
  127.4 18.2 %collective-permute-start.20 = (bf16[96,5376]{1,0:T(8,128)(2,1)}, bf16[96,5376]{1,0:T(8,128)(2,1)}, u32[]{:S(2)}, u32[]{:S(2)}) collective-permute-start(bf16[96,5376]{1,0:T(8,128)(2,1)} %dynamic-slice_bitcast_fusion.6), channel_id=1, source_target_pairs={{0,1},{1,0},{2,3},{3,2},{16,18},{17,19},{18,16},{19,17},{4,5},{5,4... | collective-permute-start | bytes 3096584 | tf_op jit(solution)/shard_map/ppermute | solution.py:33
  144.7 17.6 %collective-permute-start.25 = (bf16[96,3840]{1,0:T(8,128)(2,1)S(1)}, bf16[96,3840]{1,0:T(8,128)(2,1)S(1)}, u32[]{:S(2)}, u32[]{:S(2)}) collective-permute-start(bf16[96,3840]{1,0:T(8,128)(2,1)S(1)} %dynamic-slice_bitcast_fusion.7), channel_id=1, source_target_pairs={{0,1},{1,0},{2,3},{3,2},{16,18},{17,19},{18,16},{19,17},{4,5},{5,4... | collective-permute-start | bytes 2211848 | tf_op jit(solution)/shard_map/ppermute | solution.py:33
  145.6 17.3 %collective-permute-start.21 = (bf16[96,5376]{1,0:T(8,128)(2,1)}, bf16[96,5376]{1,0:T(8,128)(2,1)S(1)}, u32[]{:S(2)}, u32[]{:S(2)}) collective-permute-start(bf16[96,5376]{1,0:T(8,128)(2,1)} %collective-permute-done.20), channel_id=1, source_target_pairs={{0,16},{16,0},{1,17},{17,1},{2,18},{18,2},{3,19},{19,3},{4,20},{20... | collective-permute-start | bytes 3096584 | tf_op jit(solution)/shard_map/ppermute | solution.py:22
  198.4 20.0 %collective-permute-start.30 = (bf16[256,1536]{1,0:T(8,128)(2,1)S(1)}, bf16[256,1536]{1,0:T(8,128)(2,1)S(1)}, u32[]{:S(2)}, u32[]{:S(2)}) collective-permute-start(bf16[256,1536]{1,0:T(8,128)(2,1)S(1)} %get-tuple-element.83.refs_1_.refs_5_.refs_3_.refs_7_), channel_id=1, source_target_pairs={{0,4},{4,0},{8,12},{12,8},{1,5},{5,1},{9,13},{13,9},{2,6},{6,2},{1... | collective-permute-start | bytes 2359304 | tf_op jit(solution)/shard_map/ppermute | solution.py:27
  201.0 46.6 %collective-permute-start.29 = (bf16[4,384,384]{2,1,0:T(8,128)(2,1)S(1)}, bf16[4,384,384]{2,1,0:T(8,128)(2,1)}, u32[]{:S(2)}, u32[]{:S(2)}) collective-permute-start(bf16[4,384,384]{2,1,0:T(8,128)(2,1)S(1)} %fusion.18), channel_id=1, source_target_pairs={{0,1},{1,0},{2,3},{3,2},{16,18},{17,19},{18,16},{19,17},{4,5},{5,4... | collective-permute-start | bytes 3538952 | tf_op jit(solution)/shard_map/ppermute | solution.py:33
  205.6 47.3 %collective-permute-start.27 = (bf16[4,384,768]{2,1,0:T(8,128)(2,1)}, bf16[4,384,768]{2,1,0:T(8,128)(2,1)}, u32[]{:S(2)}, u32[]{:S(2)}) collective-permute-start(bf16[4,384,768]{2,1,0:T(8,128)(2,1)} %dynamic-slice_bitcast_fusion.1), channel_id=1, source_target_pairs={{0,16},{16,0},{1,17},{17,1},{2,18},{18,2},{3,19},{19,3},{4,20},{20... | collective-permute-start | bytes 7077896 | tf_op jit(solution)/shard_map/ppermute | solution.py:22
  205.7 15.0 %collective-permute-start.31 = (bf16[256,1536]{1,0:T(8,128)(2,1)S(1)}, bf16[256,1536]{1,0:T(8,128)(2,1)S(1)}, u32[]{:S(2)}, u32[]{:S(2)}) collective-permute-start(bf16[256,1536]{1,0:T(8,128)(2,1)S(1)} %get-tuple-element.83.refs_1_.refs_5_.refs_3_.refs_7_), channel_id=1, source_target_pairs={{0,16},{16,0},{1,17},{17,1},{2,18},{18,2},{3,19},{19,3},{4,20},{20... | collective-permute-start | bytes 2359304 | tf_op jit(solution)/shard_map/ppermute | solution.py:22
  248.2 47.3 %collective-permute-start.43 = (bf16[256,768]{1,0:T(8,128)(2,1)}, bf16[256,768]{1,0:T(8,128)(2,1)S(1)}, u32[]{:S(2)}, u32[]{:S(2)}) collective-permute-start(bf16[256,768]{1,0:T(8,128)(2,1)} %copy-done.64), channel_id=1, source_target_pairs={{16,8},{20,12},{24,0},{28,4},{17,9},{21,13},{25,1},{29,5},{18,10},... | collective-permute-start | bytes 1179656 | tf_op jit(solution)/shard_map/ppermute | solution.py:42
  249.6 21.5 %collective-permute-start.35 = (bf16[2,2,256,768]{3,2,1,0:T(8,128)(2,1)}, bf16[2,2,256,768]{3,2,1,0:T(8,128)(2,1)S(1)}, u32[]{:S(2)}, u32[]{:S(2)}) collective-permute-start(bf16[2,2,256,768]{3,2,1,0:T(8,128)(2,1)} %copy-done.52), channel_id=1, source_target_pairs={{0,16},{16,0},{1,17},{17,1},{2,18},{18,2},{3,19},{19,3},{4,20},{20... | collective-permute-start | bytes 4718600 | tf_op jit(solution)/shard_map/ppermute | solution.py:22
  257.7 35.5 %collective-permute-start.34 = (bf16[2,4,384,384]{3,2,1,0:T(8,128)(2,1)S(1)}, bf16[2,4,384,384]{3,2,1,0:T(8,128)(2,1)}, u32[]{:S(2)}, u32[]{:S(2)}) collective-permute-start(bf16[2,4,384,384]{3,2,1,0:T(8,128)(2,1)S(1)} %pad_maximum_fusion.1), channel_id=1, source_target_pairs={{0,1},{1,0},{2,3},{3,2},{16,18},{17,19},{18,16},{19,17},{4,5},{5,4... | collective-permute-start | bytes 7077896 | tf_op jit(solution)/shard_map/ppermute | solution.py:33
  271.3 21.8 %collective-permute-start.36 = (bf16[2,256,768]{2,1,0:T(8,128)(2,1)S(1)}, bf16[2,256,768]{2,1,0:T(8,128)(2,1)S(1)}, u32[]{:S(2)}, u32[]{:S(2)}) collective-permute-start(bf16[2,256,768]{2,1,0:T(8,128)(2,1)S(1)} %fusion.78), channel_id=1, source_target_pairs={{0,4},{4,0},{8,12},{12,8},{1,5},{5,1},{9,13},{13,9},{2,6},{6,2},{1... | collective-permute-start | bytes 2359304 | tf_op jit(solution)/shard_map/ppermute | solution.py:27
  296.6 34.7 %collective-permute-start.42 = (bf16[256,768]{1,0:T(8,128)(2,1)S(1)}, bf16[256,768]{1,0:T(8,128)(2,1)}, u32[]{:S(2)}, u32[]{:S(2)}) collective-permute-start(bf16[256,768]{1,0:T(8,128)(2,1)S(1)} %get-tuple-element.229), channel_id=1, source_target_pairs={{16,24},{20,28},{24,16},{28,20},{17,25},{21,29},{25,17},{29,21},{1... | collective-permute-start | bytes 1179656 | tf_op jit(solution)/shard_map/ppermute | solution.py:42
  298.1 37.2 %collective-permute-start.41 = (bf16[256,768]{1,0:T(8,128)(2,1)S(1)}, bf16[256,768]{1,0:T(8,128)(2,1)}, u32[]{:S(2)}, u32[]{:S(2)}) collective-permute-start(bf16[256,768]{1,0:T(8,128)(2,1)S(1)} %get-tuple-element.229), channel_id=1, source_target_pairs={{0,16},{1,17},{2,18},{3,19},{4,20},{5,21},{6,22},{7,23},{8,24},{9,... | collective-permute-start | bytes 1179656 | tf_op jit(solution)/shard_map/ppermute | solution.py:504
  324.9 23.6 %collective-permute-start.47 = (bf16[4,384,384]{2,1,0:T(8,128)(2,1)S(1)}, bf16[4,384,384]{2,1,0:T(8,128)(2,1)S(1)}, u32[]{:S(2)}, u32[]{:S(2)}) collective-permute-start(bf16[4,384,384]{2,1,0:T(8,128)(2,1)S(1)} %dynamic-slice_bitcast_fusion.4), channel_id=1, source_target_pairs={{0,16},{16,0},{1,17},{17,1},{2,18},{18,2},{3,19},{19,3},{4,20},{20... | collective-permute-start | bytes 3538952 | tf_op jit(solution)/shard_map/ppermute | solution.py:22
  325.8 25.6 %collective-permute-start.49 = (bf16[4,208,768]{2,1,0:T(8,128)(2,1)S(1)}, bf16[4,208,768]{2,1,0:T(8,128)(2,1)S(1)}, u32[]{:S(2)}, u32[]{:S(2)}) collective-permute-start(bf16[4,208,768]{2,1,0:T(8,128)(2,1)S(1)} %dynamic-slice_bitcast_fusion.3), channel_id=1, source_target_pairs={{0,16},{16,0},{1,17},{17,1},{2,18},{18,2},{3,19},{19,3},{4,20},{20... | collective-permute-start | bytes 3833864 | tf_op jit(solution)/shard_map/ppermute | solution.py:22
  331.3 16.4 %collective-permute-start.40 = (bf16[2,384,384]{2,1,0:T(8,128)(2,1)S(1)}, bf16[2,384,384]{2,1,0:T(8,128)(2,1)S(1)}, u32[]{:S(2)}, u32[]{:S(2)}) collective-permute-start(bf16[2,384,384]{2,1,0:T(8,128)(2,1)S(1)} %fusion.89), channel_id=1, source_target_pairs={{0,4},{4,0},{8,12},{12,8},{1,5},{5,1},{9,13},{13,9},{2,6},{6,2},{1... | collective-permute-start | bytes 1769480 | tf_op jit(solution)/shard_map/ppermute | solution.py:27
  350.2 25.1 %collective-permute-start.48 = (bf16[4,384,384]{2,1,0:T(8,128)(2,1)}, bf16[4,384,384]{2,1,0:T(8,128)(2,1)}, u32[]{:S(2)}, u32[]{:S(2)}) collective-permute-start(bf16[4,384,384]{2,1,0:T(8,128)(2,1)} %fusion.12), channel_id=1, source_target_pairs={{0,1},{1,0},{2,3},{3,2},{16,18},{17,19},{18,16},{19,17},{4,5},{5,4... | collective-permute-start | bytes 3538952 | tf_op jit(solution)/shard_map/ppermute | solution.py:33
  353.6 26.8 %collective-permute-start.51 = (bf16[2,4,208,384]{3,2,1,0:T(8,128)(2,1)}, bf16[2,4,208,384]{3,2,1,0:T(8,128)(2,1)}, u32[]{:S(2)}, u32[]{:S(2)}) collective-permute-start(bf16[2,4,208,384]{3,2,1,0:T(8,128)(2,1)} %pad_maximum_fusion.4), channel_id=1, source_target_pairs={{0,1},{1,0},{2,3},{3,2},{16,18},{17,19},{18,16},{19,17},{4,5},{5,4... | collective-permute-start | bytes 3833864 | tf_op jit(solution)/shard_map/ppermute | solution.py:33
  356.0 32.8 %collective-permute-start.46 = (bf16[4,384,768]{2,1,0:T(8,128)(2,1)}, bf16[4,384,768]{2,1,0:T(8,128)(2,1)}, u32[]{:S(2)}, u32[]{:S(2)}) collective-permute-start(bf16[4,384,768]{2,1,0:T(8,128)(2,1)} %dynamic-slice_bitcast_fusion), channel_id=1, source_target_pairs={{0,16},{16,0},{1,17},{17,1},{2,18},{18,2},{3,19},{19,3},{4,20},{20... | collective-permute-start | bytes 7077896 | tf_op jit(solution)/shard_map/ppermute | solution.py:22
  357.7 17.6 %collective-permute-start.52 = (bf16[1,384,384]{2,1,0:T(8,128)(2,1)S(1)}, bf16[1,384,384]{2,1,0:T(8,128)(2,1)S(1)}, u32[]{:S(2)}, u32[]{:S(2)}) collective-permute-start(bf16[1,384,384]{2,1,0:T(8,128)(2,1)S(1)} %dynamic-slice_convert_fusion.3), channel_id=1, source_target_pairs={{0,8},{4,12},{8,0},{12,4},{1,9},{5,13},{9,1},{13,5},{2,10},{6,14},... | collective-permute-start | bytes 884744 | tf_op jit(solution)/shard_map/ppermute | solution.py:27
  388.2 14.2 %collective-permute-start.59 = (bf16[2,2,256,768]{3,2,1,0:T(8,128)(2,1)}, bf16[2,2,256,768]{3,2,1,0:T(8,128)(2,1)}, u32[]{:S(2)}, u32[]{:S(2)}) collective-permute-start(bf16[2,2,256,768]{3,2,1,0:T(8,128)(2,1)} %get-tuple-element.116), channel_id=1, source_target_pairs={{0,16},{16,0},{1,17},{17,1},{2,18},{18,2},{3,19},{19,3},{4,20},{20... | collective-permute-start | bytes 4718600 | tf_op jit(solution)/shard_map/ppermute | solution.py:22
  394.5 35.2 %collective-permute-start.54 = (bf16[2,4,384,384]{3,2,1,0:T(8,128)(2,1)}, bf16[2,4,384,384]{3,2,1,0:T(8,128)(2,1)}, u32[]{:S(2)}, u32[]{:S(2)}) collective-permute-start(bf16[2,4,384,384]{3,2,1,0:T(8,128)(2,1)} %pad_maximum_fusion.2), channel_id=1, source_target_pairs={{0,1},{1,0},{2,3},{3,2},{16,18},{17,19},{18,16},{19,17},{4,5},{5,4... | collective-permute-start | bytes 7077896 | tf_op jit(solution)/shard_map/ppermute | solution.py:33
  401.6 25.2 %collective-permute-start.58 = (bf16[4,96,384]{2,1,0:T(8,128)(2,1)S(1)}, bf16[4,96,384]{2,1,0:T(8,128)(2,1)}, u32[]{:S(2)}, u32[]{:S(2)}) collective-permute-start(bf16[4,96,384]{2,1,0:T(8,128)(2,1)S(1)} %fusion.98), channel_id=1, source_target_pairs={{0,1},{1,0},{2,3},{3,2},{16,18},{17,19},{18,16},{19,17},{4,5},{5,4... | collective-permute-start | bytes 884744 | tf_op jit(solution)/shard_map/ppermute | solution.py:33
  403.8 25.9 %collective-permute-start.60 = (bf16[2,256,768]{2,1,0:T(8,128)(2,1)S(1)}, bf16[2,256,768]{2,1,0:T(8,128)(2,1)S(1)}, u32[]{:S(2)}, u32[]{:S(2)}) collective-permute-start(bf16[2,256,768]{2,1,0:T(8,128)(2,1)S(1)} %fusion.79), channel_id=1, source_target_pairs={{0,4},{4,0},{8,12},{12,8},{1,5},{5,1},{9,13},{13,9},{2,6},{6,2},{1... | collective-permute-start | bytes 2359304 | tf_op jit(solution)/shard_map/ppermute | solution.py:27
  407.4 22.2 %collective-permute-start.56 = (bf16[2,208,384]{2,1,0:T(8,128)(2,1)S(1)}, bf16[2,208,384]{2,1,0:T(8,128)(2,1)S(1)}, u32[]{:S(2)}, u32[]{:S(2)}) collective-permute-start(bf16[2,208,384]{2,1,0:T(8,128)(2,1)S(1)} %fusion.101), channel_id=1, source_target_pairs={{0,4},{4,0},{8,12},{12,8},{1,5},{5,1},{9,13},{13,9},{2,6},{6,2},{1... | collective-permute-start | bytes 958472 | tf_op jit(solution)/shard_map/ppermute | solution.py:27
  408.6 42.0 %collective-permute-start.66 = (bf16[4,96,768]{2,1,0:T(8,128)(2,1)}, bf16[4,96,768]{2,1,0:T(8,128)(2,1)}, u32[]{:S(2)}, u32[]{:S(2)}) collective-permute-start(bf16[4,96,768]{2,1,0:T(8,128)(2,1)} %fusion.92), channel_id=1, source_target_pairs={{0,16},{16,0},{1,17},{17,1},{2,18},{18,2},{3,19},{19,3},{4,20},{20... | collective-permute-start | bytes 1769480 | tf_op jit(solution)/shard_map/ppermute | solution.py:22
  434.7 29.2 %collective-permute-start.65 = (bf16[1,208,384]{2,1,0:T(8,128)(2,1)}, bf16[1,208,384]{2,1,0:T(8,128)(2,1)S(1)}, u32[]{:S(2)}, u32[]{:S(2)}) collective-permute-start(bf16[1,208,384]{2,1,0:T(8,128)(2,1)} %dynamic-slice_convert_fusion.4), channel_id=1, source_target_pairs={{0,8},{4,12},{8,0},{12,4},{1,9},{5,13},{9,1},{13,5},{2,10},{6,14},... | collective-permute-start | bytes 479240 | tf_op jit(solution)/shard_map/ppermute | solution.py:27
  435.0 19.1 %collective-permute-start.67 = (bf16[4,96,384]{2,1,0:T(8,128)(2,1)}, bf16[4,96,384]{2,1,0:T(8,128)(2,1)}, u32[]{:S(2)}, u32[]{:S(2)}) collective-permute-start(bf16[4,96,384]{2,1,0:T(8,128)(2,1)} %collective-permute-done.58), channel_id=1, source_target_pairs={{0,16},{16,0},{1,17},{17,1},{2,18},{18,2},{3,19},{19,3},{4,20},{20... | collective-permute-start | bytes 884744 | tf_op jit(solution)/shard_map/ppermute | solution.py:22
  438.4 17.4 %collective-permute-start.63 = (bf16[4,384,384]{2,1,0:T(8,128)(2,1)}, bf16[4,384,384]{2,1,0:T(8,128)(2,1)}, u32[]{:S(2)}, u32[]{:S(2)}) collective-permute-start(bf16[4,384,384]{2,1,0:T(8,128)(2,1)} %fusion.10), channel_id=1, source_target_pairs={{0,16},{16,0},{1,17},{17,1},{2,18},{18,2},{3,19},{19,3},{4,20},{20... | collective-permute-start | bytes 3538952 | tf_op jit(solution)/shard_map/ppermute | solution.py:22
  448.5 14.2 %collective-permute-start.69 = (bf16[256,768]{1,0:T(8,128)(2,1)S(1)}, bf16[256,768]{1,0:T(8,128)(2,1)S(1)}, u32[]{:S(2)}, u32[]{:S(2)}) collective-permute-start(bf16[256,768]{1,0:T(8,128)(2,1)S(1)} %fusion.76), channel_id=1, source_target_pairs={{16,8},{20,12},{24,0},{28,4},{17,9},{21,13},{25,1},{29,5},{18,10},... | collective-permute-start | bytes 1179656 | tf_op jit(solution)/shard_map/ppermute | solution.py:42
  454.1 23.0 %collective-permute-start.71 = (bf16[4,112,768]{2,1,0:T(8,128)(2,1)S(1)}, bf16[4,112,768]{2,1,0:T(8,128)(2,1)S(1)}, u32[]{:S(2)}, u32[]{:S(2)}) collective-permute-start(bf16[4,112,768]{2,1,0:T(8,128)(2,1)S(1)} %dynamic-slice_bitcast_fusion.8), channel_id=1, source_target_pairs={{0,16},{16,0},{1,17},{17,1},{2,18},{18,2},{3,19},{19,3},{4,20},{20... | collective-permute-start | bytes 2064392 | tf_op jit(solution)/shard_map/ppermute | solution.py:22
  455.8 14.1 %collective-permute-start.68 = (bf16[2,4,96,384]{3,2,1,0:T(8,128)(2,1)S(1)}, bf16[2,4,96,384]{3,2,1,0:T(8,128)(2,1)S(1)}, u32[]{:S(2)}, u32[]{:S(2)}) collective-permute-start(bf16[2,4,96,384]{3,2,1,0:T(8,128)(2,1)S(1)} %pad_maximum_fusion.10), channel_id=1, source_target_pairs={{0,1},{1,0},{2,3},{3,2},{16,18},{17,19},{18,16},{19,17},{4,5},{5,4... | collective-permute-start | bytes 1769480 | tf_op jit(solution)/shard_map/ppermute | solution.py:33
  460.0 16.2 %collective-permute-start.64 = (bf16[2,384,384]{2,1,0:T(8,128)(2,1)S(1)}, bf16[2,384,384]{2,1,0:T(8,128)(2,1)S(1)}, u32[]{:S(2)}, u32[]{:S(2)}) collective-permute-start(bf16[2,384,384]{2,1,0:T(8,128)(2,1)S(1)} %fusion.90), channel_id=1, source_target_pairs={{0,4},{4,0},{8,12},{12,8},{1,5},{5,1},{9,13},{13,9},{2,6},{6,2},{1... | collective-permute-start | bytes 1769480 | tf_op jit(solution)/shard_map/ppermute | solution.py:27
  478.4 16.7 %collective-permute-start.73 = (bf16[2,4,112,384]{3,2,1,0:T(8,128)(2,1)S(1)}, bf16[2,4,112,384]{3,2,1,0:T(8,128)(2,1)S(1)}, u32[]{:S(2)}, u32[]{:S(2)}) collective-permute-start(bf16[2,4,112,384]{3,2,1,0:T(8,128)(2,1)S(1)} %pad_maximum_fusion.9), channel_id=1, source_target_pairs={{0,1},{1,0},{2,3},{3,2},{16,18},{17,19},{18,16},{19,17},{4,5},{5,4... | collective-permute-start | bytes 2064392 | tf_op jit(solution)/shard_map/ppermute | solution.py:33
  479.3 15.8 %collective-permute-start.74 = (bf16[1,384,384]{2,1,0:T(8,128)(2,1)S(1)}, bf16[1,384,384]{2,1,0:T(8,128)(2,1)S(1)}, u32[]{:S(2)}, u32[]{:S(2)}) collective-permute-start(bf16[1,384,384]{2,1,0:T(8,128)(2,1)S(1)} %dynamic-slice_convert_fusion.2), channel_id=1, source_target_pairs={{0,8},{4,12},{8,0},{12,4},{1,9},{5,13},{9,1},{13,5},{2,10},{6,14},... | collective-permute-start | bytes 884744 | tf_op jit(solution)/shard_map/ppermute | solution.py:27
  480.7 14.5 %collective-permute-start.75 = (bf16[2,96,384]{2,1,0:T(8,128)(2,1)S(1)}, bf16[2,96,384]{2,1,0:T(8,128)(2,1)S(1)}, u32[]{:S(2)}, u32[]{:S(2)}) collective-permute-start(bf16[2,96,384]{2,1,0:T(8,128)(2,1)S(1)} %fusion.117), channel_id=1, source_target_pairs={{0,4},{4,0},{8,12},{12,8},{1,5},{5,1},{9,13},{13,9},{2,6},{6,2},{1... | collective-permute-start | bytes 442376 | tf_op jit(solution)/shard_map/ppermute | solution.py:27
  (178 other events, 1506.5 us)

commit v4 on v3

--- a/solution.py
+++ b/solution.py
@@ -87,7 +87,7 @@
         out_specs=pl.BlockSpec(memory_space=pltpu.VMEM),
         scratch_shapes=[pltpu.SemaphoreType.DMA((len(pieces) * cut,))],
         compiler_params=pltpu.CompilerParams(vmem_limit_bytes=16 * 2**20),
-        cost_estimate=pl.CostEstimate(flops=1, bytes_accessed=1, transcendentals=0),
+        cost_estimate=pl.CostEstimate(flops=0, bytes_accessed=4 * 8 * cut * rows * width, transcendentals=0),
     )(indices, *pieces)
     return whole.reshape(8 * cut * rows, width)
 
@@ -215,9 +215,9 @@
 VMEM_LIMIT = 40 * 2**20
 
 
-def rotary_tables(places, direction):
+def rotary_tables(places, direction, width):
     half_dims = ROT // 2
-    lane = jnp.arange(LANES) % HEAD_DIM
+    lane = jnp.arange(width) % HEAD_DIM
     frequency = 10000.0 ** (-((lane % half_dims).astype(F32) * 2.0) / ROT)
     phases = places.astype(F32)[:, None] * frequency[None, :]
     cosine = jnp.where(lane < ROT, jnp.cos(phases), 1.0)
@@ -287,7 +287,7 @@
             jax.ShapeDtypeStruct((count, 2 * D), BF),
         ],
         compiler_params=kernel_params(),
-        cost_estimate=pl.CostEstimate(flops=1, bytes_accessed=1, transcendentals=0),
+        cost_estimate=pl.CostEstimate(flops=6 * count * D * D, bytes_accessed=6 * D * D, transcendentals=0),
     )(attn_in, qkv_mat, bias[None], *tables)
 
 
@@ -350,34 +350,34 @@
             jax.ShapeDtypeStruct((D // LANES, 2, count), F32),
         ],
         compiler_params=kernel_params(),
-        cost_estimate=pl.CostEstimate(flops=1, bytes_accessed=1, transcendentals=0),
+        cost_estimate=pl.CostEstimate(flops=16 * count * count * len(pairs) * D, bytes_accessed=8 * count * D, transcendentals=0),
     )(query, *pairs, *pairs, mask)
 
 
-def attention_back_kernel(pieces, query_ref, grad_ref, level_ref, *refs):
+def attention_back_kernel(chosen_rows, last, query_ref, grad_ref, mixed_ref, level_ref, *refs):
+    pieces = len(chosen_rows)
     keys, values = refs[:pieces], refs[pieces : 2 * pieces]
-    mask_ref, cos_ref, right_ref, left_ref, query_out, near_ref, far_ref = refs[2 * pieces :]
+    mask_ref, *tables, before_ref, query_out, near_ref, far_ref = refs[2 * pieces :]
     count = query_ref.shape[0]
     group = pieces // 2
     key_sums, value_sums = [None] * pieces, [None] * pieces
     query_sums = []
+    products = (grad_ref[...].astype(F32) * mixed_ref[...].astype(F32)).T
+    centres = [
+        products[half : half + HEAD_DIM].sum(0, keepdims=True) for half in (0, HEAD_DIM)
+    ]
     for head, chosen in enumerate(head_picks()):
         query = query_ref[...] * chosen
         grad = grad_ref[...] * chosen
         level = level_ref[0, pl.ds(head, 1), :]
-        probs, prob_grads = [], []
-        centre = None
-        for n in range(pieces):
-            scores = dot_nt(keys[n][...], query) + mask_ref[pl.ds(n * count, count), :]
-            probs.append(jnp.exp(scores - level))
-            prob_grads.append(dot_nt(values[n][...], grad))
-            part = (probs[n] * prob_grads[n]).sum(0, keepdims=True)
-            centre = part if centre is None else centre + part
+        centre = centres[head]
         query_sum = None
-        for n in range(pieces):
-            score_grad = (probs[n] * (prob_grads[n] - centre)).astype(BF)
+        for n, place in enumerate(chosen_rows):
+            scores = dot_nt(keys[n][...], query) + mask_ref[pl.ds(place * count, count), :]
+            probs = jnp.exp(scores - level)
+            score_grad = (probs * (dot_nt(values[n][...], grad) - centre)).astype(BF)
             key_part = jnp.dot(score_grad, query, preferred_element_type=F32)
-            value_part = jnp.dot(probs[n].astype(BF), grad, preferred_element_type=F32)
+            value_part = jnp.dot(probs.astype(BF), grad, preferred_element_type=F32)
             part = dot_tn(keys[n][...], score_grad)
             query_sum = part if query_sum is None else query_sum + part
             key_sums[n] = key_part if head == 0 else key_sums[n] + key_part
@@ -387,32 +387,46 @@
         target = near_ref if n < group else far_ref
         target[n % group, 0] = key_sums[n].astype(BF)
         target[n % group, 1] = value_sums[n].astype(BF)
-    query_grad = upper_lower(*query_sums) * 0.125
-    query_out[...] = rotated(query_grad, cos_ref[...], right_ref[...], left_ref[...]).astype(BF)
-
-
-def attention_back(query, pairs, mask, level, mixed_grad, tables):
-    count, pieces = query.shape[0], len(pairs)
+    query_grad = upper_lower(*query_sums)
+    if last:
+        query_grad = (query_grad + before_ref[...]) * 0.125
+        query_grad = rotated(query_grad, *[table[...] for table in tables])
+    query_out[...] = query_grad.astype(query_out.dtype)
+
+
+def attention_back(query, pairs, chosen_rows, mask, level, mixed, mixed_grad, tables, before):
+    count, pieces = query.shape[0], len(chosen_rows)
     group = pieces // 2
+    last = before is not None
+    pairs = [pairs[n] for n in chosen_rows]
     rows = pl.BlockSpec((count, LANES), lambda j: (0, j))
     still = pl.BlockSpec((count, LANES), lambda j: (0, 0))
     moving = pl.BlockSpec((group, 2, count, LANES), lambda j: (0, 0, 0, j))
-    work = count * count * pieces
     return pl.pallas_call(
-        lambda *refs: attention_back_kernel(pieces, *refs),
+        lambda *refs: attention_back_kernel(chosen_rows, last, *refs),
         grid=(D // LANES,),
-        in_specs=[rows, rows, pl.BlockSpec((1, 2, count), lambda j: (j, 0, 0))]
+        in_specs=[rows, rows, rows, pl.BlockSpec((1, 2, count), lambda j: (j, 0, 0))]
         + piece_specs(count, pieces)
-        + [pl.BlockSpec(mask.shape, lambda j: (0, 0)), still, still, still],
+        + [pl.BlockSpec(mask.shape, lambda j: (0, 0)), still, still, still, rows if last else still],
         out_specs=[rows, moving, moving],
         out_shape=[
-            jax.ShapeDtypeStruct((count, D), BF),
+            jax.ShapeDtypeStruct((count, D), BF if last else F32),
             jax.ShapeDtypeStruct((group, 2, count, D), BF),
             jax.ShapeDtypeStruct((group, 2, count, D), BF),
         ],
         compiler_params=kernel_params(),
         cost_estimate=pl.CostEstimate(flops=1, bytes_accessed=1, transcendentals=0),
-    )(query, mixed_grad, level, *pairs, *pairs, mask, *tables)
+    )(
+        query,
+        mixed_grad,
+        mixed,
+        level,
+        *pairs,
+        *pairs,
+        mask,
+        *tables,
+        before if last else tables[0],
+    )
 
 
 def join_kernel(query_ref, cos_ref, right_ref, left_ref, *refs):
@@ -440,7 +454,7 @@
             jax.ShapeDtypeStruct((1, 3 * D), F32),
         ],
         compiler_params=kernel_params(),
-        cost_estimate=pl.CostEstimate(flops=1, bytes_accessed=1, transcendentals=0),
+        cost_estimate=pl.CostEstimate(flops=1, bytes_accessed=16 * count * D, transcendentals=0),
     )(query_grad, *tables, *parts)
 
 
@@ -501,7 +515,7 @@
 
     def deliver(rows, layer):
         moved = across_halves(rows, 1, layer)
-        here = rows if layer == 0 else lax.ppermute(rows, "section", [(0, 1)])
+        here = rows if layer == 0 else swap_cores(rows)
         first = jnp.where(micro == 0, here, moved)
         second = jnp.where(micro == 0, moved, here)
         return jnp.stack([first, second])
@@ -543,13 +557,10 @@
     key_places = jnp.concatenate(
         [places_of(rank_of(one, ctx_idx ^ j)) for one in (core, 1 - core) for j in range(group)]
     )
-    ahead = rotary_tables(own_places, 1.0)
-    back = rotary_tables(own_places, -1.0)
+    ahead = rotary_tables(own_places, 1.0, 2 * LANES)
+    back = rotary_tables(own_places, -1.0, LANES)
     still = (jnp.ones_like(ahead[0]), jnp.zeros_like(ahead[0]), jnp.zeros_like(ahead[0]))
-    tables = [
-        jnp.stack([jnp.tile(one, (1, 2)) for one in (ahead[k] * 0.125, ahead[k], still[k])])
-        for k in range(3)
-    ]
+    tables = [jnp.stack([ahead[k] * 0.125, ahead[k], still[k]]) for k in range(3)]
     mask = jnp.where(own_places[None, :] >= key_places[:, None], 0.0, -1e30)
     weights[0][0][0] = tied(
         weights[0][0][0], weights[0][1:], weights[1][1:], ahead, back, tables, mask
@@ -599,17 +610,20 @@
         )
         return wide, up_grad, dot_t(grad_low, out_mat).astype(BF)
 
-    def attend_back(layer, mixed_grad):
-        query, pairs, level = kept[layer][4:7]
-        return attention_back(query, pairs, mask, level, mixed_grad, back)
+    remote = [n for n in range(2 * group) if n % group]
+
+    def attend_back(layer, mixed_grad, chosen_rows, before=None):
+        query, pairs, level, mixed = kept[layer][4:8]
+        return attention_back(
+            query, pairs, chosen_rows, mask, level, mixed, mixed_grad, back, before
+        )
 
     def exchange(near, far):
         far = swap_cores(far)
-        sent = [
-            along_ctx((near[j].astype(F32) + far[j].astype(F32)).astype(BF), j)
-            for j in range(1, group)
+        return [
+            along_ctx((near[j].astype(F32) + far[j].astype(F32)).astype(BF), j + 1)
+            for j in range(group - 1)
         ]
-        return near[0], far[0], *sent
 
     def mlp_part(layer, grad_low, up_grad):
         up_mat = weights[layer][0][1]
@@ -639,12 +653,17 @@
         return Reduction(jnp.concatenate(parts, 2), core, place, ctx_idx)
 
     wide_1, up_grad, mixed_grad = enter(1, grad_low)
-    query_grad, near, far = attend_back(1, mixed_grad)
-    query_grad, near, far = settle([wide_1], query_grad, near, far)
+    before, near, far = attend_back(1, mixed_grad, remote)
+    before, near, far, mixed_grad = settle([wide_1], before, near, far, mixed_grad)
     parts = exchange(near, far)
     wide_1.step()
     mlp_back, out_term = mlp_part(1, grad_low, up_grad)
-    query_grad, mlp_back, out_term, *parts = settle([wide_1], query_grad, mlp_back, out_term, *parts)
+    before, mlp_back, out_term = together(before, mlp_back, out_term)
+    query_grad, near, far = attend_back(1, mixed_grad, [0, group], before)
+    query_grad, near, far, mlp_back, out_term, *parts = settle(
+        [wide_1], query_grad, near, far, mlp_back, out_term, *parts
+    )
+    parts = [near[0], swap_cores(far)[0], *parts]
     qkv_grad, qkv_sums = join_grads(query_grad, back, parts)
     low_grad, small = leave(1, grad_low, qkv_grad, qkv_sums, mlp_back, up_grad)
     qkv_term = dot_rows(kept[1][2], qkv_grad)
@@ -656,17 +675,23 @@
     mixed_grad, up_grad, *late = settle([thin_1, wide_1], mixed_grad, up_grad, *late)
     thin_1.step()
     wide_1.step()
-    query_grad, near, far = attend_back(0, mixed_grad)
-    query_grad, near, far = settle([wide_0, thin_1, wide_1], query_grad, near, far)
+    before, near, far = attend_back(0, mixed_grad, remote)
+    before, near, far, mixed_grad = settle(
+        [wide_0, thin_1, wide_1], before, near, far, mixed_grad
+    )
     parts = exchange(near, far)
     wide_0.step()
     thin_1.step()
     mlp_back, out_term = mlp_part(0, low_grad, up_grad)
+    before, mlp_back, out_term = together(before, mlp_back, out_term)
+    query_grad, near, far = attend_back(0, mixed_grad, [0, group], before)
+    far = swap_cores(far)
     query_term = dot_rows(kept[0][2], query_grad)
     middle = reduction_of(fold(query_term) + fold(out_term))
-    query_grad, mlp_back, *parts = settle(
-        [wide_0, thin_1, middle], query_grad, mlp_back, *parts
-    )
+    query_grad, near, far, mlp_back, *parts = settle(
+        [wide_0, thin_1, middle], query_grad, near, far, mlp_back, *parts
+    )
+    parts = [near[0], far[0], *parts]
     qkv_grad, qkv_sums = join_grads(query_grad, back, parts)
     wide_0.step()
     thin_1.step()

time: 526 us -> 522 us (level)
  local copies, waits for them, and re-layouts: 87.7 us -> 56.1 us
  waiting for transfers between devices: 148 us -> 179 us
  starting transfers between devices: 76.9 us -> 62.8 us
  Pallas kernels: 79.1 us -> 90.1 us
    ppermute x18, waiting for transfers between devices: 48.1 us -> 69 us  [along_square(): return lax.ppermute(block, ('section', 'fsdp'), route)]
    ppermute x2 -> x0, starting transfers between devices: 9.31 us -> none  [deliver(): here = rows if layer == 0 else lax.ppermute(rows, 'section', [(0, 1)])]
    pallas_call x2 -> x4, Pallas kernels: 29.5 us -> 37.2 us  [attention_back(): pl.pallas_call(lambda *refs: attention_back_kernel(chosen_rows, last, *re...]
    another operation x14 -> x0, local copies, waits for them, and re-layouts: 7.33 us -> none  [the longest x12 7.19 us: per_device(): jnp.tile(one, (1, 2))]
    reshape x10, local copies, waits for them, and re-layouts: 6.64 us -> 0.89 us  [leave(): one.reshape(blocks, -1)]
    ppermute x14, waiting for transfers between devices: 91.6 us -> 97.4 us  [along_ctx(): return lax.ppermute(block, 'ctx', [(i, i ^ step) for i in range(count)])]
    unnamed x303 -> x261, local copies, waits for them, and re-layouts: 29.4 us -> 28.2 us
    ppermute x39 -> x43, starting transfers between devices: 16.7 us -> 17.8 us  [swap_cores(): return lax.ppermute(block, 'section', [(0, 1), (1, 0)])]
  transfers between devices with their start and end apart: 82 -> 84, of which waited for: 25 -> 25; matrix products, arithmetic and copies ran while one was open for 32% -> 25% of each run, Pallas kernels for 15% -> 17%
where the time goes in v4:
time: 522 us; the launch traced here: 515 us
  waiting for transfers between devices  179 us (34%)
  Pallas kernels  90.1 us (17%)
  other arithmetic  76.1 us (15%)
  starting transfers between devices  62.8 us (12%)
  local copies, waits for them, and re-layouts  56.1 us (11%)
  matrix products  44.7 us (9%)
  between operations  5.88 us (1%)
    ppermute x14, waiting for transfers between devices, along_ctx(): return lax.ppermute(block, 'ctx', [(i, i ^ step) for i in range(count)])  97.4 us
    ppermute x18, waiting for transfers between devices, along_square(): return lax.ppermute(block, ('section', 'fsdp'), route)  69 us
    pallas_call x4, Pallas kernels, attention_back(): pl.pallas_call(lambda *refs: attention_back_kernel(chosen_rows, last, *re...  37.2 us
    unnamed x261, local copies, waits for them, and re-layouts  28.2 us
    pallas_call x2, Pallas kernels, attention(): pl.pallas_call(lambda *refs: attention_kernel(pieces, *refs), grid=(D //...  20.9 us
    ppermute x18, starting transfers between devices, along_square(): return lax.ppermute(block, ('section', 'fsdp'), route)  20.5 us
    pallas_call x8, Pallas kernels, assemble(): pl.pallas_call(lambda *refs: place_pieces(first, cut, *refs), out_shape=j...  19.6 us
    ppermute x43, starting transfers between devices, swap_cores(): return lax.ppermute(block, 'section', [(0, 1), (1, 0)])  17.8 us
  transfers between devices with their start and end apart: 84, of which 25 were waited for; matrix products, arithmetic and copies ran while one was open for 25% of the time, Pallas kernels for 17%

profile of v4, /device:TPU:0, one launch (start us, length us, event | category | flops | bytes accessed | tf_op | source)
XLA Modules:
  0.0 514.7 jit_solution(16809758963395106334)
XLA Ops:
  2.9 4.0 collective-permute-start.3
  10.3 2.7 broadcast_select_fusion.2
  18.5 4.4 broadcast_select_fusion
  22.9 6.9 %collective-permute-done.6 = bf16[192,2304]{1,0:T(8,128)(2,1)S(1)} collective-permute-done((bf16[192,2304]{1,0:T(8,128)(2,1)}, bf16[192,2304]{1,0:T(8,128)(2,1)S(1)}, u32[]{:S(2)}, u32[]{:S(2)}) %collective-permute-start.6) | collective-permute-done | bytes 884768 | tf_op jit(solution)/shard_map/ppermute | solution.py:33
  48.2 14.8 %collective-permute-done.14 = bf16[192,6912]{1,0:T(8,128)(2,1)} collective-permute-done((bf16[192,6912]{1,0:T(8,128)(2,1)S(1)}, bf16[192,6912]{1,0:T(8,128)(2,1)}, u32[]{:S(2)}, u32[]{:S(2)}) %collective-permute-start.14) | collective-permute-done | bytes 2654240 | tf_op jit(solution)/shard_map/ppermute | solution.py:33
  70.5 25.5 %collective-permute-done.8 = bf16[96,2304]{1,0:T(8,128)(2,1)S(1)} collective-permute-done((bf16[96,2304]{1,0:T(8,128)(2,1)S(1)}, bf16[96,2304]{1,0:T(8,128)(2,1)S(1)}, u32[]{:S(2)}, u32[]{:S(2)}) %collective-permute-start.8) | collective-permute-done | bytes 442400 | tf_op jit(solution)/shard_map/ppermute | solution.py:33
  105.1 5.4 %shard_map.170 = (bf16[256,768]{1,0:T(8,128)(2,1)S(1)}, bf16[256,1536]{1,0:T(8,128)(2,1)}) custom-call(bf16[256,768]{1,0:T(8,128)(2,1)S(1)} %fusion.67.in_ref, bf16[768,2304]{1,0:T(8,128)(2,1)S(1)} %bitcast.439, f32[1,2304]{1,0:T(1,128)S(1)} %broadcast_in_dim.140.bias_ref, f32[3,256,256]{2,1,0:T(8,128)S(1)} %copy-done.15, f32[3,256,256]{2,1,0:T(8,128)S(1)} %copy-done.19, ...), custom_call_target="tpu_custom_call" | custom-call | flops 905969664 | bytes 3538944 | tf_op jit(solution)/shard_map/pallas_call | solution.py:270
  112.0 5.1 collective-permute-done.23
  118.1 16.3 %collective-permute-done.10.refs_2_.refs_6_.refs_4_ = bf16[256,1536]{1,0:T(8,128)(2,1)} collective-permute-done((bf16[256,1536]{1,0:T(8,128)(2,1)}, bf16[256,1536]{1,0:T(8,128)(2,1)}, u32[]{:S(2)}, u32[]{:S(2)}) %collective-permute-start.10) | collective-permute-done | bytes 786464 | tf_op jit(solution)/shard_map/ppermute | solution.py:27
  142.0 10.3 %shard_map.171 = (bf16[256,768]{1,0:T(8,128)(2,1)S(1)}, f32[6,2,256]{2,1,0:T(2,128)S(1)}) custom-call(bf16[256,768]{1,0:T(8,128)(2,1)S(1)} %copy-done.38, bf16[256,1536]{1,0:T(8,128)(2,1)} %get-tuple-element.90.refs_1_.refs_5_.refs_4_.refs_6_, bf16[256,1536]{1,0:T(8,128)(2,1)} %collective-permute-done.10.refs_2_.refs_6_.refs_4_, ...), custom_call_target="tpu_custom_call" | custom-call | flops 3221225472 | bytes 1572864 | tf_op jit(solution)/shard_map/pallas_call | solution.py:342
  154.9 2.8 shard_map.174
  157.8 3.8 shard_map.173
  161.6 3.6 multiply_convert_fusion.1
  180.8 2.9 fusion.157
  195.6 5.3 %shard_map.178 = (bf16[256,768]{1,0:T(8,128)(2,1)S(1)}, bf16[256,1536]{1,0:T(8,128)(2,1)}) custom-call(bf16[256,768]{1,0:T(8,128)(2,1)S(1)} %fusion.55.in_ref, bf16[768,2304]{1,0:T(8,128)(2,1)S(1)} %bitcast.441, f32[1,2304]{1,0:T(1,128)S(1)} %broadcast_in_dim.141.bias_ref, f32[3,256,256]{2,1,0:T(8,128)S(1)} %copy-done.16, f32[3,256,256]{2,1,0:T(8,128)S(1)} %copy-done.20, ...), custom_call_target="tpu_custom_call" | custom-call | flops 905969664 | bytes 3538944 | tf_op jit(solution)/shard_map/pallas_call | solution.py:270
  204.9 3.2 dynamic-slice_bitcast_fusion.1
  208.7 13.3 %collective-permute-done.30.refs_2_.refs_6_.refs_4_ = bf16[256,1536]{1,0:T(8,128)(2,1)} collective-permute-done((bf16[256,1536]{1,0:T(8,128)(2,1)}, bf16[256,1536]{1,0:T(8,128)(2,1)}, u32[]{:S(2)}, u32[]{:S(2)}) %collective-permute-start.30) | collective-permute-done | bytes 786464 | tf_op jit(solution)/shard_map/ppermute | solution.py:27
  225.2 10.6 %shard_map.180 = (bf16[256,768]{1,0:T(8,128)(2,1)S(1)}, f32[6,2,256]{2,1,0:T(2,128)S(1)}) custom-call(bf16[256,768]{1,0:T(8,128)(2,1)S(1)} %copy-done.41, bf16[256,1536]{1,0:T(8,128)(2,1)} %get-tuple-element.97.refs_1_.refs_5_.refs_4_.refs_6_, bf16[256,1536]{1,0:T(8,128)(2,1)} %collective-permute-done.30.refs_2_.refs_6_.refs_4_, ...), custom_call_target="tpu_custom_call" | custom-call | flops 3221225472 | bytes 1572864 | tf_op jit(solution)/shard_map/pallas_call | solution.py:342
  235.8 8.5 %shard_map.181 = (f32[256,768]{1,0:T(8,128)S(1)}, bf16[1,2,256,768]{3,2,1,0:T(8,128)(2,1)S(1)}, bf16[1,2,256,768]{3,2,1,0:T(8,128)(2,1)S(1)}) custom-call(bf16[256,768]{1,0:T(8,128)(2,1)S(1)} %copy-done.41, bf16[256,768]{1,0:T(8,128)(2,1)S(1)} %convolution_convert_fusion.10.refs_1_, bf16[256,768]{1,0:T(8,128)(2,1)S(1)} %get-tuple-element.98.refs_2_, ...), custom_call_target="tpu_custom_call" | custom-call | flops 1 | bytes 1 | tf_op jit(solution)/shard_map/pallas_call | solution.py:405
  246.7 2.8 collective-permute-done.33
  249.5 4.5 fusion.34
  255.1 4.1 convolution_add_fusion.4
  263.5 2.9 collective-permute-start.45
  270.2 9.8 %shard_map.182 = (bf16[256,768]{1,0:T(8,128)(2,1)S(1)}, bf16[1,2,256,768]{3,2,1,0:T(8,128)(2,1)S(1)}, bf16[1,2,256,768]{3,2,1,0:T(8,128)(2,1)}) custom-call(bf16[256,768]{1,0:T(8,128)(2,1)S(1)} %copy-done.42, bf16[256,768]{1,0:T(8,128)(2,1)S(1)} %convolution_convert_fusion.10.refs_1_, bf16[256,768]{1,0:T(8,128)(2,1)S(1)} %get-tuple-element.98.refs_2_, ...), custom_call_target="tpu_custom_call" | custom-call | flops 1 | bytes 1 | tf_op jit(solution)/shard_map/pallas_call | solution.py:405
  288.6 3.1 fusion.16
  296.5 2.8 collective-permute-done.44
  301.6 3.6 convolution_convert_fusion.1
  305.2 3.0 convolution_convert_fusion.2
  308.2 3.1 fusion.1
  312.1 3.1 convolution_convert_fusion
  323.3 3.5 fusion.17
  332.5 9.9 %collective-permute-done.41 = bf16[2,384,384]{2,1,0:T(8,128)(2,1)S(1)} collective-permute-done((bf16[2,384,384]{2,1,0:T(8,128)(2,1)S(1)}, bf16[2,384,384]{2,1,0:T(8,128)(2,1)S(1)}, u32[]{:S(2)}, u32[]{:S(2)}) %collective-permute-start.41) | collective-permute-done | bytes 589856 | tf_op jit(solution)/shard_map/ppermute | solution.py:27
  353.2 9.5 %shard_map.184 = (f32[256,768]{1,0:T(8,128)S(1)}, bf16[1,2,256,768]{3,2,1,0:T(8,128)(2,1)S(1)}, bf16[1,2,256,768]{3,2,1,0:T(8,128)(2,1)}) custom-call(bf16[256,768]{1,0:T(8,128)(2,1)S(1)} %copy-done.39, bf16[256,768]{1,0:T(8,128)(2,1)S(1)} %convolution_convert_fusion.9.refs_1_, bf16[256,768]{1,0:T(8,128)(2,1)S(1)} %get-tuple-element.91.refs_2_, ...), custom_call_target="tpu_custom_call" | custom-call | flops 1 | bytes 1 | tf_op jit(solution)/shard_map/pallas_call | solution.py:405
  362.8 5.6 %collective-permute-done.53 = bf16[1,384,384]{2,1,0:T(8,128)(2,1)S(1)} collective-permute-done((bf16[1,384,384]{2,1,0:T(8,128)(2,1)S(1)}, bf16[1,384,384]{2,1,0:T(8,128)(2,1)S(1)}, u32[]{:S(2)}, u32[]{:S(2)}) %collective-permute-start.53) | collective-permute-done | bytes 294944 | tf_op jit(solution)/shard_map/ppermute | solution.py:27
  368.4 6.1 %collective-permute-done.52 = bf16[2,4,208,384]{3,2,1,0:T(8,128)(2,1)} collective-permute-done((bf16[2,4,208,384]{3,2,1,0:T(8,128)(2,1)}, bf16[2,4,208,384]{3,2,1,0:T(8,128)(2,1)}, u32[]{:S(2)}, u32[]{:S(2)}) %collective-permute-start.52) | collective-permute-done | bytes 1277984 | tf_op jit(solution)/shard_map/ppermute | solution.py:33
  375.0 2.5 collective-permute-done.54
  377.5 4.1 fusion.36
  386.7 9.3 %shard_map.185 = (bf16[256,768]{1,0:T(8,128)(2,1)S(1)}, bf16[1,2,256,768]{3,2,1,0:T(8,128)(2,1)S(1)}, bf16[1,2,256,768]{3,2,1,0:T(8,128)(2,1)S(1)}) custom-call(bf16[256,768]{1,0:T(8,128)(2,1)S(1)} %copy-done.39, bf16[256,768]{1,0:T(8,128)(2,1)S(1)} %convolution_convert_fusion.9.refs_1_, bf16[256,768]{1,0:T(8,128)(2,1)S(1)} %get-tuple-element.91.refs_2_, ...), custom_call_target="tpu_custom_call" | custom-call | flops 1 | bytes 1 | tf_op jit(solution)/shard_map/pallas_call | solution.py:405
  411.3 4.3 collective-permute-done.59
  415.6 16.0 %collective-permute-done.57 = bf16[2,208,384]{2,1,0:T(8,128)(2,1)S(1)} collective-permute-done((bf16[2,208,384]{2,1,0:T(8,128)(2,1)S(1)}, bf16[2,208,384]{2,1,0:T(8,128)(2,1)S(1)}, u32[]{:S(2)}, u32[]{:S(2)}) %collective-permute-start.57) | collective-permute-done | bytes 319520 | tf_op jit(solution)/shard_map/ppermute | solution.py:27
  438.1 3.3 fusion.10
  451.9 2.9 fusion.11
  458.2 6.3 %collective-permute-done.64 = bf16[4,112,384]{2,1,0:T(8,128)(2,1)S(1)} collective-permute-done((bf16[4,112,384]{2,1,0:T(8,128)(2,1)S(1)}, bf16[4,112,384]{2,1,0:T(8,128)(2,1)S(1)}, u32[]{:S(2)}, u32[]{:S(2)}) %collective-permute-start.64) | collective-permute-done | bytes 344096 | tf_op jit(solution)/shard_map/ppermute | solution.py:33
  464.5 6.5 %collective-permute-done.66 = bf16[2,384,384]{2,1,0:T(8,128)(2,1)S(1)} collective-permute-done((bf16[2,384,384]{2,1,0:T(8,128)(2,1)S(1)}, bf16[2,384,384]{2,1,0:T(8,128)(2,1)S(1)}, u32[]{:S(2)}, u32[]{:S(2)}) %collective-permute-start.66) | collective-permute-done | bytes 589856 | tf_op jit(solution)/shard_map/ppermute | solution.py:27
  478.8 11.2 %collective-permute-done.76 = bf16[1,384,384]{2,1,0:T(8,128)(2,1)S(1)} collective-permute-done((bf16[1,384,384]{2,1,0:T(8,128)(2,1)S(1)}, bf16[1,384,384]{2,1,0:T(8,128)(2,1)S(1)}, u32[]{:S(2)}, u32[]{:S(2)}) %collective-permute-start.76) | collective-permute-done | bytes 294944 | tf_op jit(solution)/shard_map/ppermute | solution.py:27
  491.1 5.4 %collective-permute-done.78 = bf16[1,96,384]{2,1,0:T(8,128)(2,1)S(1)} collective-permute-done((bf16[1,96,384]{2,1,0:T(8,128)(2,1)S(1)}, bf16[1,96,384]{2,1,0:T(8,128)(2,1)S(1)}, u32[]{:S(2)}, u32[]{:S(2)}) %collective-permute-start.78) | collective-permute-done | bytes 73760 | tf_op jit(solution)/shard_map/ppermute | solution.py:27
  496.9 6.3 %collective-permute-done.80 = bf16[2,112,384]{2,1,0:T(8,128)(2,1)S(1)} collective-permute-done((bf16[2,112,384]{2,1,0:T(8,128)(2,1)S(1)}, bf16[2,112,384]{2,1,0:T(8,128)(2,1)S(1)}, u32[]{:S(2)}, u32[]{:S(2)}) %collective-permute-start.80) | collective-permute-done | bytes 172064 | tf_op jit(solution)/shard_map/ppermute | solution.py:27
  504.3 5.3 %collective-permute-done.81 = bf16[1,112,384]{2,1,0:T(8,128)(2,1)S(1)} collective-permute-done((bf16[1,112,384]{2,1,0:T(8,128)(2,1)S(1)}, bf16[1,112,384]{2,1,0:T(8,128)(2,1)S(1)}, u32[]{:S(2)}, u32[]{:S(2)}) %collective-permute-start.81) | collective-permute-done | bytes 86048 | tf_op jit(solution)/shard_map/ppermute | solution.py:27
  (615 shorter events, 198.7 us)
Async XLA Ops:
  15.2 53.8 %collective-permute-start = (bf16[256,768]{1,0:T(8,128)(2,1)}, bf16[256,768]{1,0:T(8,128)(2,1)}, u32[]{:S(2)}, u32[]{:S(2)}) collective-permute-start(bf16[256,768]{1,0:T(8,128)(2,1)} %dynamic-slice_bitcast_fusion.12), channel_id=1, source_target_pairs={{16,24},{20,28},{24,16},{28,20},{17,25},{21,29},{25,17},{29,21},{1... | collective-permute-start | bytes 1179656 | tf_op jit(solution)/shard_map/ppermute | solution.py:42
  30.8 32.1 %collective-permute-start.14 = (bf16[192,6912]{1,0:T(8,128)(2,1)S(1)}, bf16[192,6912]{1,0:T(8,128)(2,1)}, u32[]{:S(2)}, u32[]{:S(2)}) collective-permute-start(bf16[192,6912]{1,0:T(8,128)(2,1)S(1)} %get-tuple-element.93), channel_id=1, source_target_pairs={{0,1},{1,0},{2,3},{3,2},{16,18},{17,19},{18,16},{19,17},{4,5},{5,4... | collective-permute-start | bytes 7962632 | tf_op jit(solution)/shard_map/ppermute | solution.py:33
  45.1 21.8 %collective-permute-start.4 = (f32[4,2496]{1,0:T(4,128)S(1)}, f32[4,2496]{1,0:T(4,128)S(1)}, u32[]{:S(2)}, u32[]{:S(2)}) collective-permute-start(f32[4,2496]{1,0:T(4,128)S(1)} %gather_fusion), channel_id=1, source_target_pairs={{0,16},{16,0},{1,17},{17,1},{2,18},{18,2},{3,19},{19,3},{4,20},{20... | collective-permute-start | bytes 119816 | tf_op jit(solution)/shard_map/ppermute | solution.py:22
  46.7 20.7 %collective-permute-start.7 = (bf16[192,2304]{1,0:T(8,128)(2,1)}, bf16[192,2304]{1,0:T(8,128)(2,1)}, u32[]{:S(2)}, u32[]{:S(2)}) collective-permute-start(bf16[192,2304]{1,0:T(8,128)(2,1)} %copy-done.43), channel_id=1, source_target_pairs={{0,16},{16,0},{1,17},{17,1},{2,18},{18,2},{3,19},{19,3},{4,20},{20... | collective-permute-start | bytes 2654216 | tf_op jit(solution)/shard_map/ppermute | solution.py:22
  62.9 36.5 %collective-permute-start.15 = (bf16[192,6912]{1,0:T(8,128)(2,1)}, bf16[192,6912]{1,0:T(8,128)(2,1)}, u32[]{:S(2)}, u32[]{:S(2)}) collective-permute-start(bf16[192,6912]{1,0:T(8,128)(2,1)} %collective-permute-done.14), channel_id=1, source_target_pairs={{0,16},{16,0},{1,17},{17,1},{2,18},{18,2},{3,19},{19,3},{4,20},{20... | collective-permute-start | bytes 7962632 | tf_op jit(solution)/shard_map/ppermute | solution.py:22
  65.4 32.2 %collective-permute-start.18 = (bf16[192,5376]{1,0:T(8,128)(2,1)}, bf16[192,5376]{1,0:T(8,128)(2,1)}, u32[]{:S(2)}, u32[]{:S(2)}) collective-permute-start(bf16[192,5376]{1,0:T(8,128)(2,1)} %pad_maximum_fusion.3), channel_id=1, source_target_pairs={{0,1},{1,0},{2,3},{3,2},{16,18},{17,19},{18,16},{19,17},{4,5},{5,4... | collective-permute-start | bytes 6193160 | tf_op jit(solution)/shard_map/ppermute | solution.py:33
  68.5 27.6 %collective-permute-start.8 = (bf16[96,2304]{1,0:T(8,128)(2,1)S(1)}, bf16[96,2304]{1,0:T(8,128)(2,1)S(1)}, u32[]{:S(2)}, u32[]{:S(2)}) collective-permute-start(bf16[96,2304]{1,0:T(8,128)(2,1)S(1)} %dynamic-slice_bitcast_fusion.10), channel_id=1, source_target_pairs={{0,1},{1,0},{2,3},{3,2},{16,18},{17,19},{18,16},{19,17},{4,5},{5,4... | collective-permute-start | bytes 1327112 | tf_op jit(solution)/shard_map/ppermute | solution.py:33
  97.6 19.5 %collective-permute-start.23 = (bf16[192,3840]{1,0:T(8,128)(2,1)S(1)}, bf16[192,3840]{1,0:T(8,128)(2,1)}, u32[]{:S(2)}, u32[]{:S(2)}) collective-permute-start(bf16[192,3840]{1,0:T(8,128)(2,1)S(1)} %slice.311), channel_id=1, source_target_pairs={{0,1},{1,0},{2,3},{3,2},{16,18},{17,19},{18,16},{19,17},{4,5},{5,4... | collective-permute-start | bytes 4423688 | tf_op jit(solution)/shard_map/ppermute | solution.py:33
  99.1 35.8 %collective-permute-start.19 = (bf16[192,5376]{1,0:T(8,128)(2,1)}, bf16[192,5376]{1,0:T(8,128)(2,1)S(1)}, u32[]{:S(2)}, u32[]{:S(2)}) collective-permute-start(bf16[192,5376]{1,0:T(8,128)(2,1)} %collective-permute-done.18), channel_id=1, source_target_pairs={{0,16},{16,0},{1,17},{17,1},{2,18},{18,2},{3,19},{19,3},{4,20},{20... | collective-permute-start | bytes 6193160 | tf_op jit(solution)/shard_map/ppermute | solution.py:22
  100.8 33.6 %collective-permute-start.16 = (bf16[96,6912]{1,0:T(8,128)(2,1)S(1)}, bf16[96,6912]{1,0:T(8,128)(2,1)}, u32[]{:S(2)}, u32[]{:S(2)}) collective-permute-start(bf16[96,6912]{1,0:T(8,128)(2,1)S(1)} %dynamic-slice_bitcast_fusion.2), channel_id=1, source_target_pairs={{0,1},{1,0},{2,3},{3,2},{16,18},{17,19},{18,16},{19,17},{4,5},{5,4... | collective-permute-start | bytes 3981320 | tf_op jit(solution)/shard_map/ppermute | solution.py:33
  110.5 24.0 %collective-permute-start.10 = (bf16[256,1536]{1,0:T(8,128)(2,1)}, bf16[256,1536]{1,0:T(8,128)(2,1)}, u32[]{:S(2)}, u32[]{:S(2)}) collective-permute-start(bf16[256,1536]{1,0:T(8,128)(2,1)} %get-tuple-element.90.refs_1_.refs_5_.refs_4_.refs_6_), channel_id=1, source_target_pairs={{0,4},{4,0},{8,12},{12,8},{1,5},{5,1},{9,13},{13,9},{2,6},{6,2},{1... | collective-permute-start | bytes 2359304 | tf_op jit(solution)/shard_map/ppermute | solution.py:27
  117.1 35.3 %collective-permute-start.24 = (bf16[192,3840]{1,0:T(8,128)(2,1)}, bf16[192,3840]{1,0:T(8,128)(2,1)}, u32[]{:S(2)}, u32[]{:S(2)}) collective-permute-start(bf16[192,3840]{1,0:T(8,128)(2,1)} %collective-permute-done.23), channel_id=1, source_target_pairs={{0,16},{16,0},{1,17},{17,1},{2,18},{18,2},{3,19},{19,3},{4,20},{20... | collective-permute-start | bytes 4423688 | tf_op jit(solution)/shard_map/ppermute | solution.py:22
  117.1 20.4 %collective-permute-start.22 = (bf16[256,768]{1,0:T(8,128)(2,1)S(1)}, bf16[256,768]{1,0:T(8,128)(2,1)S(1)}, u32[]{:S(2)}, u32[]{:S(2)}) collective-permute-start(bf16[256,768]{1,0:T(8,128)(2,1)S(1)} %dynamic-slice_bitcast_fusion.11), channel_id=1, source_target_pairs={{16,24},{20,28},{24,16},{28,20},{17,25},{21,29},{25,17},{29,21},{1... | collective-permute-start | bytes 1179656 | tf_op jit(solution)/shard_map/ppermute | solution.py:42
  134.9 20.0 %collective-permute-start.17 = (bf16[96,6912]{1,0:T(8,128)(2,1)}, bf16[96,6912]{1,0:T(8,128)(2,1)}, u32[]{:S(2)}, u32[]{:S(2)}) collective-permute-start(bf16[96,6912]{1,0:T(8,128)(2,1)} %collective-permute-done.16), channel_id=1, source_target_pairs={{0,16},{16,0},{1,17},{17,1},{2,18},{18,2},{3,19},{19,3},{4,20},{20... | collective-permute-start | bytes 3981320 | tf_op jit(solution)/shard_map/ppermute | solution.py:22
  137.5 17.4 %collective-permute-start.20 = (bf16[96,5376]{1,0:T(8,128)(2,1)}, bf16[96,5376]{1,0:T(8,128)(2,1)}, u32[]{:S(2)}, u32[]{:S(2)}) collective-permute-start(bf16[96,5376]{1,0:T(8,128)(2,1)} %dynamic-slice_bitcast_fusion.6), channel_id=1, source_target_pairs={{0,1},{1,0},{2,3},{3,2},{16,18},{17,19},{18,16},{19,17},{4,5},{5,4... | collective-permute-start | bytes 3096584 | tf_op jit(solution)/shard_map/ppermute | solution.py:33
  153.5 16.8 %collective-permute-start.25 = (bf16[96,3840]{1,0:T(8,128)(2,1)S(1)}, bf16[96,3840]{1,0:T(8,128)(2,1)S(1)}, u32[]{:S(2)}, u32[]{:S(2)}) collective-permute-start(bf16[96,3840]{1,0:T(8,128)(2,1)S(1)} %dynamic-slice_bitcast_fusion.7), channel_id=1, source_target_pairs={{0,1},{1,0},{2,3},{3,2},{16,18},{17,19},{18,16},{19,17},{4,5},{5,4... | collective-permute-start | bytes 2211848 | tf_op jit(solution)/shard_map/ppermute | solution.py:33
  154.9 16.0 %collective-permute-start.21 = (bf16[96,5376]{1,0:T(8,128)(2,1)}, bf16[96,5376]{1,0:T(8,128)(2,1)S(1)}, u32[]{:S(2)}, u32[]{:S(2)}) collective-permute-start(bf16[96,5376]{1,0:T(8,128)(2,1)} %collective-permute-done.20), channel_id=1, source_target_pairs={{0,16},{16,0},{1,17},{17,1},{2,18},{18,2},{3,19},{19,3},{4,20},{20... | collective-permute-start | bytes 3096584 | tf_op jit(solution)/shard_map/ppermute | solution.py:22
  201.7 20.2 %collective-permute-start.30 = (bf16[256,1536]{1,0:T(8,128)(2,1)}, bf16[256,1536]{1,0:T(8,128)(2,1)}, u32[]{:S(2)}, u32[]{:S(2)}) collective-permute-start(bf16[256,1536]{1,0:T(8,128)(2,1)} %get-tuple-element.97.refs_1_.refs_5_.refs_4_.refs_6_), channel_id=1, source_target_pairs={{0,4},{4,0},{8,12},{12,8},{1,5},{5,1},{9,13},{13,9},{2,6},{6,2},{1... | collective-permute-start | bytes 2359304 | tf_op jit(solution)/shard_map/ppermute | solution.py:27
  204.2 42.0 %collective-permute-start.29 = (bf16[4,384,384]{2,1,0:T(8,128)(2,1)S(1)}, bf16[4,384,384]{2,1,0:T(8,128)(2,1)}, u32[]{:S(2)}, u32[]{:S(2)}) collective-permute-start(bf16[4,384,384]{2,1,0:T(8,128)(2,1)S(1)} %fusion.18), channel_id=1, source_target_pairs={{0,1},{1,0},{2,3},{3,2},{16,18},{17,19},{18,16},{19,17},{4,5},{5,4... | collective-permute-start | bytes 3538952 | tf_op jit(solution)/shard_map/ppermute | solution.py:33
  208.2 38.5 %collective-permute-start.27 = (bf16[4,384,768]{2,1,0:T(8,128)(2,1)}, bf16[4,384,768]{2,1,0:T(8,128)(2,1)}, u32[]{:S(2)}, u32[]{:S(2)}) collective-permute-start(bf16[4,384,768]{2,1,0:T(8,128)(2,1)} %dynamic-slice_bitcast_fusion.1), channel_id=1, source_target_pairs={{0,16},{16,0},{1,17},{17,1},{2,18},{18,2},{3,19},{19,3},{4,20},{20... | collective-permute-start | bytes 7077896 | tf_op jit(solution)/shard_map/ppermute | solution.py:22
  208.2 17.0 %collective-permute-start.31 = (bf16[256,1536]{1,0:T(8,128)(2,1)}, bf16[256,1536]{1,0:T(8,128)(2,1)S(1)}, u32[]{:S(2)}, u32[]{:S(2)}) collective-permute-start(bf16[256,1536]{1,0:T(8,128)(2,1)} %get-tuple-element.97.refs_1_.refs_5_.refs_4_.refs_6_), channel_id=1, source_target_pairs={{0,16},{16,0},{1,17},{17,1},{2,18},{18,2},{3,19},{19,3},{4,20},{20... | collective-permute-start | bytes 2359304 | tf_op jit(solution)/shard_map/ppermute | solution.py:22
  254.3 29.2 %collective-permute-start.34 = (bf16[2,4,384,384]{3,2,1,0:T(8,128)(2,1)S(1)}, bf16[2,4,384,384]{3,2,1,0:T(8,128)(2,1)S(1)}, u32[]{:S(2)}, u32[]{:S(2)}) collective-permute-start(bf16[2,4,384,384]{3,2,1,0:T(8,128)(2,1)S(1)} %pad_maximum_fusion.1), channel_id=1, source_target_pairs={{0,1},{1,0},{2,3},{3,2},{16,18},{17,19},{18,16},{19,17},{4,5},{5,4... | collective-permute-start | bytes 7077896 | tf_op jit(solution)/shard_map/ppermute | solution.py:33
  259.4 24.1 %collective-permute-start.36 = (bf16[2,256,768]{2,1,0:T(8,128)(2,1)S(1)}, bf16[2,256,768]{2,1,0:T(8,128)(2,1)S(1)}, u32[]{:S(2)}, u32[]{:S(2)}) collective-permute-start(bf16[2,256,768]{2,1,0:T(8,128)(2,1)S(1)} %fusion.78), channel_id=1, source_target_pairs={{0,4},{4,0},{8,12},{12,8},{1,5},{5,1},{9,13},{13,9},{2,6},{6,2},{1... | collective-permute-start | bytes 2359304 | tf_op jit(solution)/shard_map/ppermute | solution.py:27
  261.8 24.6 %collective-permute-start.46 = (bf16[256,768]{1,0:T(8,128)(2,1)}, bf16[256,768]{1,0:T(8,128)(2,1)}, u32[]{:S(2)}, u32[]{:S(2)}) collective-permute-start(bf16[256,768]{1,0:T(8,128)(2,1)} %fusion.33), channel_id=1, source_target_pairs={{16,24},{20,28},{24,16},{28,20},{17,25},{21,29},{25,17},{29,21},{1... | collective-permute-start | bytes 1179656 | tf_op jit(solution)/shard_map/ppermute | solution.py:42
  263.5 22.9 %collective-permute-start.45 = (bf16[256,768]{1,0:T(8,128)(2,1)}, bf16[256,768]{1,0:T(8,128)(2,1)}, u32[]{:S(2)}, u32[]{:S(2)}) collective-permute-start(bf16[256,768]{1,0:T(8,128)(2,1)} %fusion.33), channel_id=1, source_target_pairs={{0,16},{16,0},{1,17},{17,1},{2,18},{18,2},{3,19},{19,3},{4,20},{20... | collective-permute-start | bytes 1179656 | tf_op jit(solution)/shard_map/ppermute | solution.py:22
  285.0 14.3 %collective-permute-start.44 = (bf16[256,768]{1,0:T(8,128)(2,1)}, bf16[256,768]{1,0:T(8,128)(2,1)S(1)}, u32[]{:S(2)}, u32[]{:S(2)}) collective-permute-start(bf16[256,768]{1,0:T(8,128)(2,1)} %copy-done.70), channel_id=1, source_target_pairs={{16,8},{20,12},{24,0},{28,4},{17,9},{21,13},{25,1},{29,5},{18,10},... | collective-permute-start | bytes 1179656 | tf_op jit(solution)/shard_map/ppermute | solution.py:42
  291.7 29.1 %collective-permute-start.40 = (bf16[4,384,384]{2,1,0:T(8,128)(2,1)}, bf16[4,384,384]{2,1,0:T(8,128)(2,1)}, u32[]{:S(2)}, u32[]{:S(2)}) collective-permute-start(bf16[4,384,384]{2,1,0:T(8,128)(2,1)} %fusion.16), channel_id=1, source_target_pairs={{0,16},{16,0},{1,17},{17,1},{2,18},{18,2},{3,19},{19,3},{4,20},{20... | collective-permute-start | bytes 3538952 | tf_op jit(solution)/shard_map/ppermute | solution.py:22
  299.8 28.0 %collective-permute-start.43 = (bf16[256,768]{1,0:T(8,128)(2,1)S(1)}, bf16[256,768]{1,0:T(8,128)(2,1)}, u32[]{:S(2)}, u32[]{:S(2)}) collective-permute-start(bf16[256,768]{1,0:T(8,128)(2,1)S(1)} %get-tuple-element.257), channel_id=1, source_target_pairs={{16,24},{20,28},{24,16},{28,20},{17,25},{21,29},{25,17},{29,21},{1... | collective-permute-start | bytes 1179656 | tf_op jit(solution)/shard_map/ppermute | solution.py:42
  301.4 29.0 %collective-permute-start.42 = (bf16[256,768]{1,0:T(8,128)(2,1)S(1)}, bf16[256,768]{1,0:T(8,128)(2,1)}, u32[]{:S(2)}, u32[]{:S(2)}) collective-permute-start(bf16[256,768]{1,0:T(8,128)(2,1)S(1)} %get-tuple-element.257), channel_id=1, source_target_pairs={{0,16},{16,0},{1,17},{17,1},{2,18},{18,2},{3,19},{19,3},{4,20},{20... | collective-permute-start | bytes 1179656 | tf_op jit(solution)/shard_map/ppermute | solution.py:22
  320.5 21.9 %collective-permute-start.48 = (bf16[4,384,384]{2,1,0:T(8,128)(2,1)S(1)}, bf16[4,384,384]{2,1,0:T(8,128)(2,1)S(1)}, u32[]{:S(2)}, u32[]{:S(2)}) collective-permute-start(bf16[4,384,384]{2,1,0:T(8,128)(2,1)S(1)} %dynamic-slice_bitcast_fusion.4), channel_id=1, source_target_pairs={{0,16},{16,0},{1,17},{17,1},{2,18},{18,2},{3,19},{19,3},{4,20},{20... | collective-permute-start | bytes 3538952 | tf_op jit(solution)/shard_map/ppermute | solution.py:22
  320.8 24.5 %collective-permute-start.50 = (bf16[4,208,768]{2,1,0:T(8,128)(2,1)S(1)}, bf16[4,208,768]{2,1,0:T(8,128)(2,1)S(1)}, u32[]{:S(2)}, u32[]{:S(2)}) collective-permute-start(bf16[4,208,768]{2,1,0:T(8,128)(2,1)S(1)} %dynamic-slice_bitcast_fusion.3), channel_id=1, source_target_pairs={{0,16},{16,0},{1,17},{17,1},{2,18},{18,2},{3,19},{19,3},{4,20},{20... | collective-permute-start | bytes 3833864 | tf_op jit(solution)/shard_map/ppermute | solution.py:22
  326.9 15.5 %collective-permute-start.41 = (bf16[2,384,384]{2,1,0:T(8,128)(2,1)S(1)}, bf16[2,384,384]{2,1,0:T(8,128)(2,1)S(1)}, u32[]{:S(2)}, u32[]{:S(2)}) collective-permute-start(bf16[2,384,384]{2,1,0:T(8,128)(2,1)S(1)} %fusion.89), channel_id=1, source_target_pairs={{0,4},{4,0},{8,12},{12,8},{1,5},{5,1},{9,13},{13,9},{2,6},{6,2},{1... | collective-permute-start | bytes 1769480 | tf_op jit(solution)/shard_map/ppermute | solution.py:27
  327.9 14.5 %collective-permute-start.39 = (bf16[4,208,384]{2,1,0:T(8,128)(2,1)S(1)}, bf16[4,208,384]{2,1,0:T(8,128)(2,1)S(1)}, u32[]{:S(2)}, u32[]{:S(2)}) collective-permute-start(bf16[4,208,384]{2,1,0:T(8,128)(2,1)S(1)} %fusion.31), channel_id=1, source_target_pairs={{0,1},{1,0},{2,3},{3,2},{16,18},{17,19},{18,16},{19,17},{4,5},{5,4... | collective-permute-start | bytes 1916936 | tf_op jit(solution)/shard_map/ppermute | solution.py:33
  344.2 24.1 %collective-permute-start.49 = (bf16[4,384,384]{2,1,0:T(8,128)(2,1)}, bf16[4,384,384]{2,1,0:T(8,128)(2,1)}, u32[]{:S(2)}, u32[]{:S(2)}) collective-permute-start(bf16[4,384,384]{2,1,0:T(8,128)(2,1)} %fusion.12), channel_id=1, source_target_pairs={{0,1},{1,0},{2,3},{3,2},{16,18},{17,19},{18,16},{19,17},{4,5},{5,4... | collective-permute-start | bytes 3538952 | tf_op jit(solution)/shard_map/ppermute | solution.py:33
  347.5 26.9 %collective-permute-start.52 = (bf16[2,4,208,384]{3,2,1,0:T(8,128)(2,1)}, bf16[2,4,208,384]{3,2,1,0:T(8,128)(2,1)}, u32[]{:S(2)}, u32[]{:S(2)}) collective-permute-start(bf16[2,4,208,384]{3,2,1,0:T(8,128)(2,1)} %pad_maximum_fusion.4), channel_id=1, source_target_pairs={{0,1},{1,0},{2,3},{3,2},{16,18},{17,19},{18,16},{19,17},{4,5},{5,4... | collective-permute-start | bytes 3833864 | tf_op jit(solution)/shard_map/ppermute | solution.py:33
  350.1 24.9 %collective-permute-start.47 = (bf16[4,384,768]{2,1,0:T(8,128)(2,1)}, bf16[4,384,768]{2,1,0:T(8,128)(2,1)}, u32[]{:S(2)}, u32[]{:S(2)}) collective-permute-start(bf16[4,384,768]{2,1,0:T(8,128)(2,1)} %dynamic-slice_bitcast_fusion), channel_id=1, source_target_pairs={{0,16},{16,0},{1,17},{17,1},{2,18},{18,2},{3,19},{19,3},{4,20},{20... | collective-permute-start | bytes 7077896 | tf_op jit(solution)/shard_map/ppermute | solution.py:22
  351.8 16.6 %collective-permute-start.53 = (bf16[1,384,384]{2,1,0:T(8,128)(2,1)S(1)}, bf16[1,384,384]{2,1,0:T(8,128)(2,1)S(1)}, u32[]{:S(2)}, u32[]{:S(2)}) collective-permute-start(bf16[1,384,384]{2,1,0:T(8,128)(2,1)S(1)} %dynamic-slice_convert_fusion.3), channel_id=1, source_target_pairs={{0,8},{4,12},{8,0},{12,4},{1,9},{5,13},{9,1},{13,5},{2,10},{6,14},... | collective-permute-start | bytes 884744 | tf_op jit(solution)/shard_map/ppermute | solution.py:27
  383.2 48.3 %collective-permute-start.55 = (bf16[2,4,384,384]{3,2,1,0:T(8,128)(2,1)}, bf16[2,4,384,384]{3,2,1,0:T(8,128)(2,1)}, u32[]{:S(2)}, u32[]{:S(2)}) collective-permute-start(bf16[2,4,384,384]{3,2,1,0:T(8,128)(2,1)} %pad_maximum_fusion.2), channel_id=1, source_target_pairs={{0,1},{1,0},{2,3},{3,2},{16,18},{17,19},{18,16},{19,17},{4,5},{5,4... | collective-permute-start | bytes 7077896 | tf_op jit(solution)/shard_map/ppermute | solution.py:33
  386.7 17.1 %collective-permute-start.61 = (bf16[1,2,256,768]{3,2,1,0:T(8,128)(2,1)}, bf16[1,2,256,768]{3,2,1,0:T(8,128)(2,1)}, u32[]{:S(2)}, u32[]{:S(2)}) collective-permute-start(bf16[1,2,256,768]{3,2,1,0:T(8,128)(2,1)} %get-tuple-element.144), channel_id=1, source_target_pairs={{0,16},{16,0},{1,17},{17,1},{2,18},{18,2},{3,19},{19,3},{4,20},{20... | collective-permute-start | bytes 2359304 | tf_op jit(solution)/shard_map/ppermute | solution.py:22
  405.3 26.2 %collective-permute-start.62 = (bf16[2,256,768]{2,1,0:T(8,128)(2,1)S(1)}, bf16[2,256,768]{2,1,0:T(8,128)(2,1)S(1)}, u32[]{:S(2)}, u32[]{:S(2)}) collective-permute-start(bf16[2,256,768]{2,1,0:T(8,128)(2,1)S(1)} %fusion.79), channel_id=1, source_target_pairs={{0,4},{4,0},{8,12},{12,8},{1,5},{5,1},{9,13},{13,9},{2,6},{6,2},{1... | collective-permute-start | bytes 2359304 | tf_op jit(solution)/shard_map/ppermute | solution.py:27
  407.8 23.7 %collective-permute-start.57 = (bf16[2,208,384]{2,1,0:T(8,128)(2,1)S(1)}, bf16[2,208,384]{2,1,0:T(8,128)(2,1)S(1)}, u32[]{:S(2)}, u32[]{:S(2)}) collective-permute-start(bf16[2,208,384]{2,1,0:T(8,128)(2,1)S(1)} %fusion.103), channel_id=1, source_target_pairs={{0,4},{4,0},{8,12},{12,8},{1,5},{5,1},{9,13},{13,9},{2,6},{6,2},{1... | collective-permute-start | bytes 958472 | tf_op jit(solution)/shard_map/ppermute | solution.py:27
  415.5 31.3 %collective-permute-start.68 = (bf16[4,96,768]{2,1,0:T(8,128)(2,1)}, bf16[4,96,768]{2,1,0:T(8,128)(2,1)}, u32[]{:S(2)}, u32[]{:S(2)}) collective-permute-start(bf16[4,96,768]{2,1,0:T(8,128)(2,1)} %fusion.92), channel_id=1, source_target_pairs={{0,16},{16,0},{1,17},{17,1},{2,18},{18,2},{3,19},{19,3},{4,20},{20... | collective-permute-start | bytes 1769480 | tf_op jit(solution)/shard_map/ppermute | solution.py:22
  436.6 21.6 %collective-permute-start.67 = (bf16[1,208,384]{2,1,0:T(8,128)(2,1)S(1)}, bf16[1,208,384]{2,1,0:T(8,128)(2,1)S(1)}, u32[]{:S(2)}, u32[]{:S(2)}) collective-permute-start(bf16[1,208,384]{2,1,0:T(8,128)(2,1)S(1)} %dynamic-slice_convert_fusion.4), channel_id=1, source_target_pairs={{0,8},{4,12},{8,0},{12,4},{1,9},{5,13},{9,1},{13,5},{2,10},{6,14},... | collective-permute-start | bytes 479240 | tf_op jit(solution)/shard_map/ppermute | solution.py:27
  443.1 14.2 %collective-permute-start.71 = (bf16[256,768]{1,0:T(8,128)(2,1)S(1)}, bf16[256,768]{1,0:T(8,128)(2,1)S(1)}, u32[]{:S(2)}, u32[]{:S(2)}) collective-permute-start(bf16[256,768]{1,0:T(8,128)(2,1)S(1)} %fusion.76), channel_id=1, source_target_pairs={{16,8},{20,12},{24,0},{28,4},{17,9},{21,13},{25,1},{29,5},{18,10},... | collective-permute-start | bytes 1179656 | tf_op jit(solution)/shard_map/ppermute | solution.py:42
  449.2 22.7 %collective-permute-start.73 = (bf16[4,112,768]{2,1,0:T(8,128)(2,1)S(1)}, bf16[4,112,768]{2,1,0:T(8,128)(2,1)S(1)}, u32[]{:S(2)}, u32[]{:S(2)}) collective-permute-start(bf16[4,112,768]{2,1,0:T(8,128)(2,1)S(1)} %dynamic-slice_bitcast_fusion.8), channel_id=1, source_target_pairs={{0,16},{16,0},{1,17},{17,1},{2,18},{18,2},{3,19},{19,3},{4,20},{20... | collective-permute-start | bytes 2064392 | tf_op jit(solution)/shard_map/ppermute | solution.py:22
  454.9 16.1 %collective-permute-start.66 = (bf16[2,384,384]{2,1,0:T(8,128)(2,1)S(1)}, bf16[2,384,384]{2,1,0:T(8,128)(2,1)S(1)}, u32[]{:S(2)}, u32[]{:S(2)}) collective-permute-start(bf16[2,384,384]{2,1,0:T(8,128)(2,1)S(1)} %fusion.90), channel_id=1, source_target_pairs={{0,4},{4,0},{8,12},{12,8},{1,5},{5,1},{9,13},{13,9},{2,6},{6,2},{1... | collective-permute-start | bytes 1769480 | tf_op jit(solution)/shard_map/ppermute | solution.py:27
  473.2 16.8 %collective-permute-start.75 = (bf16[2,4,112,384]{3,2,1,0:T(8,128)(2,1)S(1)}, bf16[2,4,112,384]{3,2,1,0:T(8,128)(2,1)S(1)}, u32[]{:S(2)}, u32[]{:S(2)}) collective-permute-start(bf16[2,4,112,384]{3,2,1,0:T(8,128)(2,1)S(1)} %pad_maximum_fusion.12), channel_id=1, source_target_pairs={{0,1},{1,0},{2,3},{3,2},{16,18},{17,19},{18,16},{19,17},{4,5},{5,4... | collective-permute-start | bytes 2064392 | tf_op jit(solution)/shard_map/ppermute | solution.py:33
  474.3 15.6 %collective-permute-start.76 = (bf16[1,384,384]{2,1,0:T(8,128)(2,1)S(1)}, bf16[1,384,384]{2,1,0:T(8,128)(2,1)S(1)}, u32[]{:S(2)}, u32[]{:S(2)}) collective-permute-start(bf16[1,384,384]{2,1,0:T(8,128)(2,1)S(1)} %dynamic-slice_convert_fusion.2), channel_id=1, source_target_pairs={{0,8},{4,12},{8,0},{12,4},{1,9},{5,13},{9,1},{13,5},{2,10},{6,14},... | collective-permute-start | bytes 884744 | tf_op jit(solution)/shard_map/ppermute | solution.py:27
  (160 other events, 1222.8 us)
